TPU v7x, 256 devices: a whole 4x4x8 slice. The times are simulated.
256 devices in a mesh: section: 16 (over y_hi, z), rep: 16 (over x, y_lo, core).
Axes of the slice: x: 4, y: 4 (y_hi: 2, y_lo: 2; y = y_hi * 2 + y_lo), z: 8, core: 2. Of those that a mesh axis runs over, the one named last changes fastest.
Arguments:
- features: bfloat16 [32768, 256], P(('section', 'rep')), may hold values from -6 to 6
- tiles: bfloat16 [256, 64, 128, 128], P(('section', 'rep')), may hold values from 0 to 0.019042969
- columns: int32 [256, 64], P(('section', 'rep')), may hold values from 0 to 255
- weight: bfloat16 [256, 256], replicated, may hold values from -0.375 to 0.375
Outputs:
- hidden: bfloat16 [32768, 256], P(('section', 'rep'))
All inputs are finite; a program needn't handle non-finite values.
Results may differ from a plain program's by a relative error of at most 0.0049.
Values may be sent and summed in bfloat16 or wider, within the bound.
No kernel may reach another device: no remote copies, remote signals or barrier semaphores. Data moves between devices by JAX's collectives and lax.ppermute only.
A program may use at most 64 MiB of HBM per device.

v0:
```python
import jax
import jax.numpy as jnp
from jax import lax
from jax.sharding import PartitionSpec as P


def on_device(features, tiles, columns, weight):
    width = features.shape[1]
    side = tiles.shape[2]
    group = lax.all_gather(features, "rep", axis=0, tiled=True)
    gathered = lax.all_gather(group, "section", axis=0, tiled=True)
    blocks = gathered.reshape(-1, side, width)
    picked = blocks[columns]
    summed = jnp.einsum("okij,okjf->oif", tiles, picked, preferred_element_type=jnp.float32)
    aggregated = summed.astype(jnp.bfloat16).reshape(-1, width)
    product = jnp.dot(aggregated, weight, preferred_element_type=jnp.float32)
    return jnp.maximum(product, 0.0).astype(jnp.bfloat16)


def solution(mesh):
    return jax.shard_map(
        on_device,
        mesh=mesh,
        in_specs=(
            P(("section", "rep"), None),
            P(("section", "rep"), None, None, None),
            P(("section", "rep"), None),
            P(),
        ),
        out_specs=P(("section", "rep"), None),
        check_vma=False,
    )
```

profile of v0, /device:TPU:1, one launch (start us, length us, event | category | flops | bytes accessed | tf_op | source)
XLA Modules:
  0.0 295.1 jit_solution(13435849618271010857)
XLA Ops:
  6.5 0.0 copy-start
  6.5 0.0 all-gather.3.cloned.1.call-start
  6.5 0.7 all-gather.3.cloned.1.call-update
  7.3 0.0 all-gather.5.cloned.1.call-start
  7.3 41.1 %all-gather.3.cloned.1.call-done = bf16[2048,256]{1,0:T(8,128)(2,1)} async-done(((bf16[128,256]{1,0:T(8,128)(2,1)}), bf16[2048,256]{1,0:T(8,128)(2,1)}) %all-gather.3.cloned.1.call-update) | async-done | bytes 1048592 | tf_op jit(solution)/shard_map/all_gather | solution.py:10
  48.4 0.0 all-gather.5.cloned.1.call-update
  48.4 0.7 fusion.11
  49.1 226.3 %all-gather.5.cloned.1.call-done = bf16[32768,256]{1,0:T(8,128)(2,1)} async-done(((bf16[2048,256]{1,0:T(8,128)(2,1)}), bf16[32768,256]{1,0:T(8,128)(2,1)}) %all-gather.5.cloned.1.call-update) | async-done | bytes 16777232 | tf_op jit(solution)/shard_map/all_gather | solution.py:11
  275.4 0.0 copy-start.1
  275.4 8.6 %gather_fusion = bf16[64,128,256]{2,1,0:T(8,128)(2,1)} fusion(bf16[256,128,256]{2,1,0:T(8,128)(2,1)} %bitcast.20, s32[1024]{0:T(1024)S(1)} %pad_clamp_fusion), kind=kCustom, calls=%fused_computation | custom fusion | bytes 8388864 | tf_op jit(solution)/shard_map/gather | solution.py:13
  283.9 0.0 copy-done
  283.9 0.0 copy-done.1
  283.9 4.3 %fusion.5 = bf16[128,256]{1,0:T(8,128)(2,1)} fusion(bf16[256,256]{1,0:T(8,128)(2,1)S(1)} %copy-done.1, bf16[64,128,256]{2,1,0:T(8,128)(2,1)} %gather_fusion, bf16[1,64,128,128]{3,2,1,0:T(8,128)(2,1)S(1)} %copy-done), kind=kOutput, calls=%fused_computation.5 | convolution fusion | flops 553746432 | bytes 6488064 | tf_op jit(solution)/shard_map/dot_general | solution.py:16
  (1 shorter events, 0.0 us)
Async XLA Ops:
  6.5 277.4 %copy-start = (bf16[1,64,128,128]{3,2,1,0:T(8,128)(2,1)S(1)}, bf16[1,64,128,128]{3,2,1,0:T(8,128)(2,1)}, u32[]{:S(2)}) copy-start(bf16[1,64,128,128]{3,2,1,0:T(8,128)(2,1)} %param.5) | copy-start | bytes 6291460
  6.5 41.9 %all-gather.3.cloned.1.call-start = ((), (), s32[]{:S(2)}) async-start(), calls=%async_computation | async-start | bytes 1114112 | tf_op jit(solution)/shard_map/all_gather | solution.py:10
  7.3 268.1 %all-gather.5.cloned.1.call-start = ((), (), s32[]{:S(2)}) async-start(), calls=%async_computation.1 | async-start | bytes 17825792 | tf_op jit(solution)/shard_map/all_gather | solution.py:11
  275.4 8.6 %copy-start.1 = (bf16[256,256]{1,0:T(8,128)(2,1)S(1)}, bf16[256,256]{1,0:T(8,128)(2,1)}, u32[]{:S(2)}) copy-start(bf16[256,256]{1,0:T(8,128)(2,1)} %param.7) | copy-start | bytes 393220
Sparse Core Ops, SparseCore 0:
  9.2 39.1 all-gather.2
  51.0 224.3 all-gather.4
where the time goes:
time: 295 us
  waiting for transfers between devices  268 us (91%)
  between operations  13.4 us (5%)
  local copies, waits for them, and re-layouts  8.57 us (3%)
  matrix products  4.29 us (1%)
    all_gather x1, waiting for transfers between devices, on_device(): gathered = lax.all_gather(group, 'section', axis=0, tiled=True)  226 us
    all_gather x1, waiting for transfers between devices, on_device(): group = lax.all_gather(features, 'rep', axis=0, tiled=True)  41.1 us
    gather x1, local copies, waits for them, and re-layouts, on_device(): picked = blocks[columns]  8.56 us
  transfers between devices with their start and end apart: 2, of which 2 were waited for; matrix products, arithmetic and copies ran while one was open for 0% of the time, Pallas kernels for 0%

commit v1 on v0

v1 whole, which is shorter than its diff:
```python
import itertools

import jax
import jax.numpy as jnp
from jax import lax
from jax.experimental import pallas as pl
from jax.experimental.pallas import tpu as pltpu
from jax.sharding import Mesh, PartitionSpec as P

AXES = ("yh", "z", "x", "yl", "core")
DIMS = (2, 8, 4, 2, 2)
SIDE = 128
WIDTH = 256
TILES = 64
HALF = 16
BATCH = 4


def pairs(target):
    found = []
    for source, (yh, z, x, yl, core) in enumerate(itertools.product(*map(range, DIMS))):
        tx, ty, tz, tc = target(x, yh * 2 + yl, z, core)
        tx, ty, tz = tx % 4, ty % 4, tz % 8
        found.append((source, ((((ty // 2) * 8 + tz) * 4 + tx) * 2 + ty % 2) * 2 + tc))
    return found


def from_z(a, d):
    return lax.ppermute(a, AXES, pairs(lambda x, y, z, c: (x, y, z - d, c)))


def from_middle(a, d):
    return lax.ppermute(a, AXES, pairs(lambda x, y, z, c: (x, y - d, z, c) if c == 0 else (x - d, y, z, c)))


def from_last(a, d):
    return lax.ppermute(a, AXES, pairs(lambda x, y, z, c: (x - d, y, z, c) if c == 0 else (x, y - d, z, c)))


def from_core(a):
    return lax.ppermute(a, "core", [(0, 1), (1, 0)])


def places(columns):
    yh, z, x, yl, core = (lax.axis_index(a) for a in AXES)
    y = yh * 2 + yl
    dz = (((columns >> 4) & 7) - z) & 7
    dx = (((columns >> 2) & 3) - x) & 3
    dy = (((columns >> 7) * 2 + ((columns >> 1) & 1)) - y) & 3
    middle = jnp.where(core == 0, dy, dx)
    last = jnp.where(core == 0, dx, dy)
    return jnp.where((columns & 1) == core, last * 32 + middle * 8 + dz, -1)


def multiply_kernel(place_ref, tiles_ref, *rest):
    pieces, (out_ref, list_ref, count_ref) = rest[:-3], rest[-3:]
    for p in range(8):
        count_ref[p] = 0

    @pl.loop(0, TILES)
    def _(k):
        place = place_ref[0, k]

        @pl.when(place >= 0)
        def _():
            piece = place // HALF
            n = count_ref[piece]
            list_ref[piece, n] = k * HALF + place % HALF
            count_ref[piece] = n + 1

    out_ref[...] = jnp.zeros_like(out_ref)
    for p in range(8):
        ref = pieces[max(p - 1, 0)]
        base = HALF if p == 1 else 0
        n = count_ref[p]

        @pl.loop(0, (n + BATCH - 1) // BATCH)
        def _(i):
            left, right = [], []
            for j in range(BATCH):
                at = i * BATCH + j
                code = list_ref[p, jnp.minimum(at, n - 1)]
                tile = tiles_ref[pl.ds(pl.multiple_of((code // HALF) * SIDE, SIDE), SIDE), :]
                left.append(jnp.where(at < n, tile, jnp.zeros_like(tile)))
                right.append(ref[pl.ds(pl.multiple_of((base + code % HALF) * SIDE, SIDE), SIDE), :])
            out_ref[...] += jnp.dot(
                jnp.concatenate(left, axis=1), jnp.concatenate(right, axis=0), preferred_element_type=jnp.float32
            )


def multiply(place, tiles, pieces):
    vmem = pl.BlockSpec(memory_space=pltpu.VMEM)
    return pl.pallas_call(
        multiply_kernel,
        out_shape=jax.ShapeDtypeStruct((SIDE, WIDTH), jnp.float32),
        in_specs=[pl.BlockSpec(memory_space=pltpu.SMEM), vmem] + [vmem] * len(pieces),
        out_specs=vmem,
        scratch_shapes=[pltpu.SMEM((8, TILES), jnp.int32), pltpu.SMEM((8,), jnp.int32)],
        compiler_params=pltpu.CompilerParams(vmem_limit_bytes=24 * 1024 * 1024),
        cost_estimate=pl.CostEstimate(flops=32 * 2 * SIDE * SIDE * WIDTH, bytes_accessed=10 << 20, transcendentals=0),
    )(place, tiles, *pieces)


def gather(own):
    p1, m1, p2, m2 = (from_z(own, d) for d in (1, -1, 2, -2))
    p3, m3, p4 = from_z(p2, 1), from_z(m2, -1), from_z(p2, 2)
    line = jnp.concatenate([own, p1, p2, p3, p4, m3, m2, m1], axis=0)
    plane = jnp.concatenate([line] + [from_middle(line, d) for d in (1, 2, 3)], axis=0)
    half = HALF * SIDE
    low, high = plane[:half], plane[half:]
    next_low, prev_high = from_last(low, 1), from_last(high, -1)
    next_high, prev_low = from_last(high, 1), from_last(low, -1)
    far_low, far_high = from_last(next_low, 1), from_last(prev_high, -1)
    return [plane, next_low, next_high, far_low, far_high, prev_low, prev_high]


def on_device(features, tiles, columns, weight):
    mine = tiles.reshape(TILES * SIDE, SIDE)
    other = from_core(mine)
    pieces = gather(features)
    away = multiply(places(from_core(columns)), other, pieces)
    back = from_core(away)
    here = multiply(places(columns), mine, pieces)
    aggregated = (here + back).astype(jnp.bfloat16)
    product = jnp.dot(aggregated, weight, preferred_element_type=jnp.float32)
    return jnp.maximum(product, 0.0).astype(jnp.bfloat16)


def solution(mesh):
    grid = Mesh(mesh.devices.reshape(DIMS), AXES)
    return jax.shard_map(
        on_device,
        mesh=grid,
        in_specs=(P(AXES, None), P(AXES, None, None, None), P(AXES, None), P()),
        out_specs=P(AXES, None),
        check_vma=False,
    )
```

time: 295 us -> 99.7 us (0.34)
  waiting for transfers between devices: 268 us -> 34.6 us
  starting transfers between devices: 0.04 us -> 41.4 us
  Pallas kernels: 0 us -> 14.1 us
  between operations: 13.4 us -> 0.06 us
  matrix products: 4.29 us -> 0.8 us
    all_gather x2 -> x0, waiting for transfers between devices: 267 us -> none  [the longest x1 226 us: on_device(): gathered = lax.all_gather(group, 'section', axis=0, tiled=True)]
    ppermute x0 -> x19, starting transfers between devices: none -> 41.4 us  [the longest x3 18.5 us: from_core(): return lax.ppermute(a, 'core', [(0, 1), (1, 0)])]
    ppermute x0 -> x19, waiting for transfers between devices: none -> 34.6 us  [the longest x6 25 us: from_last(): lax.ppermute(a, AXES, pairs(lambda x, y, z, c: (x - d, y, z, c) if c == 0...]
    pallas_call x0 -> x2, Pallas kernels: none -> 14.1 us  [multiply(): pl.pallas_call(multiply_kernel, out_shape=jax.ShapeDtypeStruct((SIDE, WID...]
    gather x1 -> x0, local copies, waits for them, and re-layouts: 8.56 us -> none  [on_device(): picked = blocks[columns]]
    unnamed x4 -> x13, local copies, waits for them, and re-layouts: 0.01 us -> 6.91 us
    dot_general x1, matrix products: 4.29 us -> 0.8 us  [on_device(): product = jnp.dot(aggregated, weight, preferred_element_type=jnp.float32)]
  transfers between devices with their start and end apart: 2 -> 19, of which waited for: 2 -> 9; matrix products, arithmetic and copies ran while one was open for 0% -> 8% of each run, Pallas kernels for 0% -> 7%
where the time goes in v1:
time: 99.7 us
  starting transfers between devices  41.4 us (42%)
  waiting for transfers between devices  34.6 us (35%)
  Pallas kernels  14.1 us (14%)
  local copies, waits for them, and re-layouts  8.68 us (9%)
    ppermute x6, waiting for transfers between devices, from_last(): lax.ppermute(a, AXES, pairs(lambda x, y, z, c: (x - d, y, z, c) if c == 0...  25 us
    ppermute x3, starting transfers between devices, from_core(): return lax.ppermute(a, 'core', [(0, 1), (1, 0)])  18.5 us
    pallas_call x2, Pallas kernels, multiply(): pl.pallas_call(multiply_kernel, out_shape=jax.ShapeDtypeStruct((SIDE, WID...  14.1 us
    ppermute x7, starting transfers between devices, from_z(): return lax.ppermute(a, AXES, pairs(lambda x, y, z, c: (x, y, z - d, c)))  12.4 us
    ppermute x3, waiting for transfers between devices, from_middle(): lax.ppermute(a, AXES, pairs(lambda x, y, z, c: (x, y - d, z, c) if c == 0...  7.49 us
    unnamed x13, local copies, waits for them, and re-layouts  6.91 us
    ppermute x6, starting transfers between devices, from_last(): lax.ppermute(a, AXES, pairs(lambda x, y, z, c: (x - d, y, z, c) if c == 0...  6.88 us
    ppermute x3, starting transfers between devices, from_middle(): lax.ppermute(a, AXES, pairs(lambda x, y, z, c: (x, y - d, z, c) if c == 0...  3.6 us
  transfers between devices with their start and end apart: 19, of which 9 were waited for; matrix products, arithmetic and copies ran while one was open for 8% of the time, Pallas kernels for 7%

profile of v1, /device:TPU:1, one launch (start us, length us, event | category | flops | bytes accessed | tf_op | source)
XLA Modules:
  0.0 99.7 jit_solution(11513142938780795414)
XLA Ops:
  0.0 3.8 %collective-permute-start.4 = (bf16[128,256]{1,0:T(8,128)(2,1)}, bf16[128,256]{1,0:T(8,128)(2,1)S(1)}, u32[]{:S(2)}, u32[]{:S(2)}) collective-permute-start(bf16[128,256]{1,0:T(8,128)(2,1)} %param.4), channel_id=1, source_target_pairs={{0,32},{1,33},{2,34},{3,35},{4,36},{5,37},{6,38},{7,39},{8,40},{9,... | collective-permute-start | bytes 196616 | tf_op jit(solution)/shard_map/ppermute | solution.py:29
  3.8 3.1 %collective-permute-start.1 = (bf16[128,256]{1,0:T(8,128)(2,1)}, bf16[128,256]{1,0:T(8,128)(2,1)S(1)}, u32[]{:S(2)}, u32[]{:S(2)}) collective-permute-start(bf16[128,256]{1,0:T(8,128)(2,1)} %param.4), channel_id=1, source_target_pairs={{0,96},{1,97},{2,98},{3,99},{4,100},{5,101},{6,102},{7,103},{8,104... | collective-permute-start | bytes 196616 | tf_op jit(solution)/shard_map/ppermute | solution.py:29
  6.9 1.8 %collective-permute-start = (bf16[128,256]{1,0:T(8,128)(2,1)}, bf16[128,256]{1,0:T(8,128)(2,1)S(1)}, u32[]{:S(2)}, u32[]{:S(2)}) collective-permute-start(bf16[128,256]{1,0:T(8,128)(2,1)} %param.4), channel_id=1, source_target_pairs={{0,112},{1,113},{2,114},{3,115},{4,116},{5,117},{6,118},{7,119},{8... | collective-permute-start | bytes 196616 | tf_op jit(solution)/shard_map/ppermute | solution.py:29
  8.8 0.0 collective-permute-start.6
  8.8 1.5 %constant_dynamic-update-slice_fusion.27 = (bf16[2048,256]{1,0:T(8,128)(2,1)}, bf16[1024,256]{1,0:T(8,128)(2,1)S(1)}, bf16[4096,256]{1,0:T(8,128)(2,1)S(1)}) fusion(bf16[128,256]{1,0:T(8,128)(2,1)} %param.4), kind=kLoop, calls=%fused_computation.30 | loop fusion | bytes 262144
  10.3 0.7 collective-permute-done.1
  11.1 2.1 %collective-permute-start.3 = (bf16[128,256]{1,0:T(8,128)(2,1)S(1)}, bf16[128,256]{1,0:T(8,128)(2,1)S(1)}, u32[]{:S(2)}, u32[]{:S(2)}) collective-permute-start(bf16[128,256]{1,0:T(8,128)(2,1)S(1)} %collective-permute-done.1), channel_id=1, source_target_pairs={{0,96},{1,97},{2,98},{3,99},{4,100},{5,101},{6,102},{7,103},{8,104... | collective-permute-start | bytes 196616 | tf_op jit(solution)/shard_map/ppermute | solution.py:29
  13.2 0.9 collective-permute-start.2
  14.1 0.5 collective-permute-start.5
  14.7 0.0 collective-permute-done
  14.7 0.6 constant_dynamic-update-slice_fusion.26
  15.3 0.6 constant_dynamic-update-slice_fusion.25
  15.9 1.2 %collective-permute-done.2 = bf16[128,256]{1,0:T(8,128)(2,1)S(1)} collective-permute-done((bf16[128,256]{1,0:T(8,128)(2,1)S(1)}, bf16[128,256]{1,0:T(8,128)(2,1)S(1)}, u32[]{:S(2)}, u32[]{:S(2)}) %collective-permute-start.2) | collective-permute-done | bytes 65568 | tf_op jit(solution)/shard_map/ppermute | solution.py:29
  17.1 0.6 constant_dynamic-update-slice_fusion.24
  17.7 0.6 constant_dynamic-update-slice_fusion.23
  18.4 0.2 collective-permute-done.5
  18.6 0.6 constant_dynamic-update-slice_fusion.22
  19.2 0.6 constant_dynamic-update-slice_fusion.21
  19.9 0.0 collective-permute-done.6
  19.9 0.6 constant_dynamic-update-slice_fusion.20
  20.5 2.5 %collective-permute-start.7 = (bf16[1024,256]{1,0:T(8,128)(2,1)S(1)}, bf16[1024,256]{1,0:T(8,128)(2,1)S(1)}, u32[]{:S(2)}, u32[]{:S(2)}) collective-permute-start(bf16[1024,256]{1,0:T(8,128)(2,1)S(1)} %get-tuple-element.13), channel_id=1, source_target_pairs={{0,130},{1,13},{2,0},{3,15},{4,134},{5,1},{6,4},{7,3},{8,138},{9,5... | collective-permute-start | bytes 1572872 | tf_op jit(solution)/shard_map/ppermute | solution.py:33
  23.0 0.5 collective-permute-start.8
  23.5 0.6 collective-permute-start.9
  24.1 5.0 %collective-permute-start.17 = (bf16[8192,128]{1,0:T(8,128)(2,1)}, bf16[8192,128]{1,0:T(8,128)(2,1)}, u32[]{:S(2)}, u32[]{:S(2)}) collective-permute-start(bf16[8192,128]{1,0:T(8,128)(2,1)} %bitcast.tiles_ref), channel_id=1, source_target_pairs={{0,1},{1,0},{2,3},{3,2},{4,5},{5,4},{6,7},{7,6},{8,9},{9,8},{10,11... | collective-permute-start | bytes 6291464 | tf_op jit(solution)/shard_map/ppermute | solution.py:41
  29.1 5.6 %collective-permute-done.7 = bf16[1024,256]{1,0:T(8,128)(2,1)S(1)} collective-permute-done((bf16[1024,256]{1,0:T(8,128)(2,1)S(1)}, bf16[1024,256]{1,0:T(8,128)(2,1)S(1)}, u32[]{:S(2)}, u32[]{:S(2)}) %collective-permute-start.7) | collective-permute-done | bytes 524320 | tf_op jit(solution)/shard_map/ppermute | solution.py:33
  34.7 0.9 constant_dynamic-update-slice_fusion.19
  35.7 0.9 constant_dynamic-update-slice_fusion.29
  36.6 1.8 %collective-permute-done.9 = bf16[1024,256]{1,0:T(8,128)(2,1)S(1)} collective-permute-done((bf16[1024,256]{1,0:T(8,128)(2,1)S(1)}, bf16[1024,256]{1,0:T(8,128)(2,1)S(1)}, u32[]{:S(2)}, u32[]{:S(2)}) %collective-permute-start.9) | collective-permute-done | bytes 524320 | tf_op jit(solution)/shard_map/ppermute | solution.py:33
  38.4 0.9 constant_dynamic-update-slice_fusion.28
  39.3 1.1 %collective-permute-start.13 = (bf16[2048,256]{1,0:T(8,128)(2,1)}, bf16[2048,256]{1,0:T(8,128)(2,1)S(1)}, u32[]{:S(2)}, u32[]{:S(2)}) collective-permute-start(bf16[2048,256]{1,0:T(8,128)(2,1)} %get-tuple-element.5), channel_id=1, source_target_pairs={{0,4},{1,3},{2,6},{3,129},{4,8},{5,7},{6,10},{7,133},{8,12},{9,11}... | collective-permute-start | bytes 3145736 | tf_op jit(solution)/shard_map/ppermute | solution.py:37
  40.4 1.6 %collective-permute-start.10 = (bf16[2048,256]{1,0:T(8,128)(2,1)}, bf16[2048,256]{1,0:T(8,128)(2,1)}, u32[]{:S(2)}, u32[]{:S(2)}) collective-permute-start(bf16[2048,256]{1,0:T(8,128)(2,1)} %get-tuple-element.9), channel_id=1, source_target_pairs={{0,12},{1,131},{2,14},{3,1},{4,0},{5,135},{6,2},{7,5},{8,4},{9,139... | collective-permute-start | bytes 3145736 | tf_op jit(solution)/shard_map/ppermute | solution.py:37
  42.0 6.1 %collective-permute-start.16 = (s32[1,64]{1,0:T(1,128)S(1)}, s32[1,64]{1,0:T(1,128)S(1)}, u32[]{:S(2)}, u32[]{:S(2)}) collective-permute-start(s32[1,64]{1,0:T(1,128)S(1)} %copy-done.1), channel_id=1, source_target_pairs={{0,1},{1,0},{2,3},{3,2},{4,5},{5,4},{6,7},{7,6},{8,9},{9,8},{10,11... | collective-permute-start | bytes 776 | tf_op jit(solution)/shard_map/ppermute | solution.py:41
  48.2 1.0 %collective-permute-start.11 = (bf16[2048,256]{1,0:T(8,128)(2,1)}, bf16[2048,256]{1,0:T(8,128)(2,1)}, u32[]{:S(2)}, u32[]{:S(2)}) collective-permute-start(bf16[2048,256]{1,0:T(8,128)(2,1)} %get-tuple-element.5), channel_id=1, source_target_pairs={{0,12},{1,131},{2,14},{3,1},{4,0},{5,135},{6,2},{7,5},{8,4},{9,139... | collective-permute-start | bytes 3145736 | tf_op jit(solution)/shard_map/ppermute | solution.py:37
  49.2 0.0 collective-permute-done.16
  49.2 0.5 collective-permute-start.15
  49.6 5.1 %collective-permute-done.13.rest_6_ = bf16[2048,256]{1,0:T(8,128)(2,1)S(1)} collective-permute-done((bf16[2048,256]{1,0:T(8,128)(2,1)}, bf16[2048,256]{1,0:T(8,128)(2,1)S(1)}, u32[]{:S(2)}, u32[]{:S(2)}) %collective-permute-start.13) | collective-permute-done | bytes 1048608 | tf_op jit(solution)/shard_map/ppermute | solution.py:37
  54.7 0.0 collective-permute-start.14
  54.7 0.0 collective-permute-done.10.rest_1_
  54.7 2.7 %collective-permute-start.12 = (bf16[2048,256]{1,0:T(8,128)(2,1)}, bf16[2048,256]{1,0:T(8,128)(2,1)}, u32[]{:S(2)}, u32[]{:S(2)}) collective-permute-start(bf16[2048,256]{1,0:T(8,128)(2,1)} %collective-permute-done.10.rest_1_), channel_id=1, source_target_pairs={{0,12},{1,131},{2,14},{3,1},{4,0},{5,135},{6,2},{7,5},{8,4},{9,139... | collective-permute-start | bytes 3145736 | tf_op jit(solution)/shard_map/ppermute | solution.py:37
  57.4 8.5 %collective-permute-done.11.rest_2_ = bf16[2048,256]{1,0:T(8,128)(2,1)} collective-permute-done((bf16[2048,256]{1,0:T(8,128)(2,1)}, bf16[2048,256]{1,0:T(8,128)(2,1)}, u32[]{:S(2)}, u32[]{:S(2)}) %collective-permute-start.11) | collective-permute-done | bytes 1048608 | tf_op jit(solution)/shard_map/ppermute | solution.py:37
  65.9 0.1 collective-permute-done.15.rest_5_
  66.1 0.0 collective-permute-done.17.tiles_ref
  66.1 11.2 %collective-permute-done.14.rest_4_ = bf16[2048,256]{1,0:T(8,128)(2,1)} collective-permute-done((bf16[2048,256]{1,0:T(8,128)(2,1)S(1)}, bf16[2048,256]{1,0:T(8,128)(2,1)}, u32[]{:S(2)}, u32[]{:S(2)}) %collective-permute-start.14) | collective-permute-done | bytes 1048608 | tf_op jit(solution)/shard_map/ppermute | solution.py:37
  77.3 0.0 collective-permute-done.12.rest_3_
  77.3 7.2 %shard_map.47 = f32[128,256]{1,0:T(8,128)S(1)} custom-call(s32[1,64]{1,0:T(1,128)S(1)} %compare_select_fusion.place_ref, bf16[8192,128]{1,0:T(8,128)(2,1)} %collective-permute-done.17.tiles_ref, bf16[4096,256]{1,0:T(8,128)(2,1)S(1)} %get-tuple-element.6.rest_0_, bf16[2048,256]{1,0:T(8,128)(2,1)} %collective-permute-done.10.rest_1_, ...), custom_call_target="tpu_custom_call" | custom-call | flops 268435456 | bytes 10485760 | tf_op jit(solution)/shard_map/pallas_call | solution.py:93
  84.5 7.4 %collective-permute-start.18 = (f32[128,256]{1,0:T(8,128)S(1)}, f32[128,256]{1,0:T(8,128)S(1)}, u32[]{:S(2)}, u32[]{:S(2)}) collective-permute-start(f32[128,256]{1,0:T(8,128)S(1)} %shard_map.47), channel_id=1, source_target_pairs={{0,1},{1,0},{2,3},{3,2},{4,5},{5,4},{6,7},{7,6},{8,9},{9,8},{10,11... | collective-permute-start | bytes 393224 | tf_op jit(solution)/shard_map/ppermute | solution.py:41
  91.9 7.0 %shard_map.46 = f32[128,256]{1,0:T(8,128)S(1)} custom-call(s32[1,64]{1,0:T(1,128)S(1)} %compare_select_fusion.1.place_ref, bf16[8192,128]{1,0:T(8,128)(2,1)} %bitcast.tiles_ref, bf16[4096,256]{1,0:T(8,128)(2,1)S(1)} %get-tuple-element.6.rest_0_, bf16[2048,256]{1,0:T(8,128)(2,1)} %collective-permute-done.10.rest_1_, ...), custom_call_target="tpu_custom_call" | custom-call | flops 268435456 | bytes 10485760 | tf_op jit(solution)/shard_map/pallas_call | solution.py:93
  98.9 0.8 fusion
  (10 shorter events, 0.0 us)
Async XLA Ops:
  0.0 98.9 %copy-start = (bf16[256,256]{1,0:T(8,128)(2,1)S(1)}, bf16[256,256]{1,0:T(8,128)(2,1)}, u32[]{:S(2)}) copy-start(bf16[256,256]{1,0:T(8,128)(2,1)} %param.7) | copy-start | bytes 393220
  0.0 14.1 %collective-permute-start.4 = (bf16[128,256]{1,0:T(8,128)(2,1)}, bf16[128,256]{1,0:T(8,128)(2,1)S(1)}, u32[]{:S(2)}, u32[]{:S(2)}) collective-permute-start(bf16[128,256]{1,0:T(8,128)(2,1)} %param.4), channel_id=1, source_target_pairs={{0,32},{1,33},{2,34},{3,35},{4,36},{5,37},{6,38},{7,39},{8,40},{9,... | collective-permute-start | bytes 196616 | tf_op jit(solution)/shard_map/ppermute | solution.py:29
  3.8 7.2 %collective-permute-start.1 = (bf16[128,256]{1,0:T(8,128)(2,1)}, bf16[128,256]{1,0:T(8,128)(2,1)S(1)}, u32[]{:S(2)}, u32[]{:S(2)}) collective-permute-start(bf16[128,256]{1,0:T(8,128)(2,1)} %param.4), channel_id=1, source_target_pairs={{0,96},{1,97},{2,98},{3,99},{4,100},{5,101},{6,102},{7,103},{8,104... | collective-permute-start | bytes 196616 | tf_op jit(solution)/shard_map/ppermute | solution.py:29
  6.9 7.7 %collective-permute-start = (bf16[128,256]{1,0:T(8,128)(2,1)}, bf16[128,256]{1,0:T(8,128)(2,1)S(1)}, u32[]{:S(2)}, u32[]{:S(2)}) collective-permute-start(bf16[128,256]{1,0:T(8,128)(2,1)} %param.4), channel_id=1, source_target_pairs={{0,112},{1,113},{2,114},{3,115},{4,116},{5,117},{6,118},{7,119},{8... | collective-permute-start | bytes 196616 | tf_op jit(solution)/shard_map/ppermute | solution.py:29
  8.8 11.1 %collective-permute-start.6 = (bf16[128,256]{1,0:T(8,128)(2,1)}, bf16[128,256]{1,0:T(8,128)(2,1)S(1)}, u32[]{:S(2)}, u32[]{:S(2)}) collective-permute-start(bf16[128,256]{1,0:T(8,128)(2,1)} %param.4), channel_id=1, source_target_pairs={{0,16},{1,17},{2,18},{3,19},{4,20},{5,21},{6,22},{7,23},{8,24},{9,... | collective-permute-start | bytes 196616 | tf_op jit(solution)/shard_map/ppermute | solution.py:29
  11.1 6.7 %collective-permute-start.3 = (bf16[128,256]{1,0:T(8,128)(2,1)S(1)}, bf16[128,256]{1,0:T(8,128)(2,1)S(1)}, u32[]{:S(2)}, u32[]{:S(2)}) collective-permute-start(bf16[128,256]{1,0:T(8,128)(2,1)S(1)} %collective-permute-done.1), channel_id=1, source_target_pairs={{0,96},{1,97},{2,98},{3,99},{4,100},{5,101},{6,102},{7,103},{8,104... | collective-permute-start | bytes 196616 | tf_op jit(solution)/shard_map/ppermute | solution.py:29
  13.2 3.9 %collective-permute-start.2 = (bf16[128,256]{1,0:T(8,128)(2,1)S(1)}, bf16[128,256]{1,0:T(8,128)(2,1)S(1)}, u32[]{:S(2)}, u32[]{:S(2)}) collective-permute-start(bf16[128,256]{1,0:T(8,128)(2,1)S(1)} %collective-permute-done.1), channel_id=1, source_target_pairs={{0,112},{1,113},{2,114},{3,115},{4,116},{5,117},{6,118},{7,119},{8... | collective-permute-start | bytes 196616 | tf_op jit(solution)/shard_map/ppermute | solution.py:29
  14.1 4.5 %collective-permute-start.5 = (bf16[128,256]{1,0:T(8,128)(2,1)S(1)}, bf16[128,256]{1,0:T(8,128)(2,1)S(1)}, u32[]{:S(2)}, u32[]{:S(2)}) collective-permute-start(bf16[128,256]{1,0:T(8,128)(2,1)S(1)} %collective-permute-done.4), channel_id=1, source_target_pairs={{0,16},{1,17},{2,18},{3,19},{4,20},{5,21},{6,22},{7,23},{8,24},{9,... | collective-permute-start | bytes 196616 | tf_op jit(solution)/shard_map/ppermute | solution.py:29
  20.5 14.2 %collective-permute-start.7 = (bf16[1024,256]{1,0:T(8,128)(2,1)S(1)}, bf16[1024,256]{1,0:T(8,128)(2,1)S(1)}, u32[]{:S(2)}, u32[]{:S(2)}) collective-permute-start(bf16[1024,256]{1,0:T(8,128)(2,1)S(1)} %get-tuple-element.13), channel_id=1, source_target_pairs={{0,130},{1,13},{2,0},{3,15},{4,134},{5,1},{6,4},{7,3},{8,138},{9,5... | collective-permute-start | bytes 1572872 | tf_op jit(solution)/shard_map/ppermute | solution.py:33
  23.0 12.7 %collective-permute-start.8 = (bf16[1024,256]{1,0:T(8,128)(2,1)S(1)}, bf16[1024,256]{1,0:T(8,128)(2,1)S(1)}, u32[]{:S(2)}, u32[]{:S(2)}) collective-permute-start(bf16[1024,256]{1,0:T(8,128)(2,1)S(1)} %get-tuple-element.13), channel_id=1, source_target_pairs={{0,128},{1,9},{2,130},{3,11},{4,132},{5,13},{6,134},{7,15},{8,136}... | collective-permute-start | bytes 1572872 | tf_op jit(solution)/shard_map/ppermute | solution.py:33
  23.5 14.9 %collective-permute-start.9 = (bf16[1024,256]{1,0:T(8,128)(2,1)S(1)}, bf16[1024,256]{1,0:T(8,128)(2,1)S(1)}, u32[]{:S(2)}, u32[]{:S(2)}) collective-permute-start(bf16[1024,256]{1,0:T(8,128)(2,1)S(1)} %get-tuple-element.13), channel_id=1, source_target_pairs={{0,2},{1,5},{2,128},{3,7},{4,6},{5,9},{6,132},{7,11},{8,10},{9,13}... | collective-permute-start | bytes 1572872 | tf_op jit(solution)/shard_map/ppermute | solution.py:33
  24.1 42.0 %collective-permute-start.17 = (bf16[8192,128]{1,0:T(8,128)(2,1)}, bf16[8192,128]{1,0:T(8,128)(2,1)}, u32[]{:S(2)}, u32[]{:S(2)}) collective-permute-start(bf16[8192,128]{1,0:T(8,128)(2,1)} %bitcast.tiles_ref), channel_id=1, source_target_pairs={{0,1},{1,0},{2,3},{3,2},{4,5},{5,4},{6,7},{7,6},{8,9},{9,8},{10,11... | collective-permute-start | bytes 6291464 | tf_op jit(solution)/shard_map/ppermute | solution.py:41
  34.7 7.3 %copy-start.1 = (s32[1,64]{1,0:T(1,128)S(1)}, s32[1,64]{1,0:T(1,128)}, u32[]{:S(2)}) copy-start(s32[1,64]{1,0:T(1,128)} %param.6) | copy-start | bytes 772
  39.3 15.4 %collective-permute-start.13 = (bf16[2048,256]{1,0:T(8,128)(2,1)}, bf16[2048,256]{1,0:T(8,128)(2,1)S(1)}, u32[]{:S(2)}, u32[]{:S(2)}) collective-permute-start(bf16[2048,256]{1,0:T(8,128)(2,1)} %get-tuple-element.5), channel_id=1, source_target_pairs={{0,4},{1,3},{2,6},{3,129},{4,8},{5,7},{6,10},{7,133},{8,12},{9,11}... | collective-permute-start | bytes 3145736 | tf_op jit(solution)/shard_map/ppermute | solution.py:37
  40.4 14.3 %collective-permute-start.10 = (bf16[2048,256]{1,0:T(8,128)(2,1)}, bf16[2048,256]{1,0:T(8,128)(2,1)}, u32[]{:S(2)}, u32[]{:S(2)}) collective-permute-start(bf16[2048,256]{1,0:T(8,128)(2,1)} %get-tuple-element.9), channel_id=1, source_target_pairs={{0,12},{1,131},{2,14},{3,1},{4,0},{5,135},{6,2},{7,5},{8,4},{9,139... | collective-permute-start | bytes 3145736 | tf_op jit(solution)/shard_map/ppermute | solution.py:37
  42.0 7.1 %collective-permute-start.16 = (s32[1,64]{1,0:T(1,128)S(1)}, s32[1,64]{1,0:T(1,128)S(1)}, u32[]{:S(2)}, u32[]{:S(2)}) collective-permute-start(s32[1,64]{1,0:T(1,128)S(1)} %copy-done.1), channel_id=1, source_target_pairs={{0,1},{1,0},{2,3},{3,2},{4,5},{5,4},{6,7},{7,6},{8,9},{9,8},{10,11... | collective-permute-start | bytes 776 | tf_op jit(solution)/shard_map/ppermute | solution.py:41
  48.2 17.8 %collective-permute-start.11 = (bf16[2048,256]{1,0:T(8,128)(2,1)}, bf16[2048,256]{1,0:T(8,128)(2,1)}, u32[]{:S(2)}, u32[]{:S(2)}) collective-permute-start(bf16[2048,256]{1,0:T(8,128)(2,1)} %get-tuple-element.5), channel_id=1, source_target_pairs={{0,12},{1,131},{2,14},{3,1},{4,0},{5,135},{6,2},{7,5},{8,4},{9,139... | collective-permute-start | bytes 3145736 | tf_op jit(solution)/shard_map/ppermute | solution.py:37
  49.2 16.9 %collective-permute-start.15 = (bf16[2048,256]{1,0:T(8,128)(2,1)}, bf16[2048,256]{1,0:T(8,128)(2,1)}, u32[]{:S(2)}, u32[]{:S(2)}) collective-permute-start(bf16[2048,256]{1,0:T(8,128)(2,1)} %get-tuple-element.9), channel_id=1, source_target_pairs={{0,4},{1,3},{2,6},{3,129},{4,8},{5,7},{6,10},{7,133},{8,12},{9,11}... | collective-permute-start | bytes 3145736 | tf_op jit(solution)/shard_map/ppermute | solution.py:37
  54.7 22.6 %collective-permute-start.14 = (bf16[2048,256]{1,0:T(8,128)(2,1)S(1)}, bf16[2048,256]{1,0:T(8,128)(2,1)}, u32[]{:S(2)}, u32[]{:S(2)}) collective-permute-start(bf16[2048,256]{1,0:T(8,128)(2,1)S(1)} %collective-permute-done.13.rest_6_), channel_id=1, source_target_pairs={{0,4},{1,3},{2,6},{3,129},{4,8},{5,7},{6,10},{7,133},{8,12},{9,11}... | collective-permute-start | bytes 3145736 | tf_op jit(solution)/shard_map/ppermute | solution.py:37
  54.7 22.6 %collective-permute-start.12 = (bf16[2048,256]{1,0:T(8,128)(2,1)}, bf16[2048,256]{1,0:T(8,128)(2,1)}, u32[]{:S(2)}, u32[]{:S(2)}) collective-permute-start(bf16[2048,256]{1,0:T(8,128)(2,1)} %collective-permute-done.10.rest_1_), channel_id=1, source_target_pairs={{0,12},{1,131},{2,14},{3,1},{4,0},{5,135},{6,2},{7,5},{8,4},{9,139... | collective-permute-start | bytes 3145736 | tf_op jit(solution)/shard_map/ppermute | solution.py:37
  84.5 14.4 %collective-permute-start.18 = (f32[128,256]{1,0:T(8,128)S(1)}, f32[128,256]{1,0:T(8,128)S(1)}, u32[]{:S(2)}, u32[]{:S(2)}) collective-permute-start(f32[128,256]{1,0:T(8,128)S(1)} %shard_map.47), channel_id=1, source_target_pairs={{0,1},{1,0},{2,3},{3,2},{4,5},{5,4},{6,7},{7,6},{8,9},{9,8},{10,11... | collective-permute-start | bytes 393224 | tf_op jit(solution)/shard_map/ppermute | solution.py:41

commit v2 on v0

v2 whole, which is shorter than its diff:
```python
import itertools

import jax
import jax.numpy as jnp
from jax import lax
from jax.experimental import pallas as pl
from jax.experimental.pallas import tpu as pltpu
from jax.sharding import Mesh, PartitionSpec as P

AXES = ("yh", "zh", "zl", "x", "yl", "core")
DIMS = (2, 4, 2, 4, 2, 2)
SIDE = 128
WIDTH = 256
TILES = 64
PLANE = 16
BUFFERS = 8
AHEAD = 14
BATCH = 16


def move(a, target):
    found = []
    for source, (yh, zh, zl, x, yl, core) in enumerate(itertools.product(*map(range, DIMS))):
        tx, ty, tz, tc = target(x, yh * 2 + yl, zh * 2 + zl, core)
        tx, ty, tz = tx % 4, ty % 4, tz % 8
        found.append((source, ((((ty // 2) * 8 + tz) * 4 + tx) * 2 + ty % 2) * 2 + tc))
    return lax.ppermute(a, AXES, found)


def from_line(a, d):
    return move(a, lambda x, y, z, c: (x, y, z - 2 * d, c))


def from_middle(a, d):
    return move(a, lambda x, y, z, c: (x, y - d, z, c) if c == 0 else (x - d, y, z, c))


def from_last(a, d):
    return move(a, lambda x, y, z, c: (x - d, y, z, c) if c == 0 else (x, y - d, z, c))


def from_core(a):
    return move(a, lambda x, y, z, c: (x, y, z, 1 - c))


def from_pair(a):
    return move(a, lambda x, y, z, c: (x, y, z ^ 1, c))


def places(columns):
    yh, zh, zl, x, yl, core = (lax.axis_index(a) for a in AXES)
    y = yh * 2 + yl
    at = columns & 1
    dz = (((columns >> 5) & 3) - zh) & 3
    dx = (((columns >> 2) & 3) - x) & 3
    dy = (((columns >> 7) * 2 + ((columns >> 1) & 1)) - y) & 3
    middle = jnp.where(at == 0, dy, dx)
    last = jnp.where(at == 0, dx, dy)
    place = ((at ^ core) * 4 + last) * PLANE + middle * 4 + dz
    return jnp.where(((columns >> 4) & 1) == zl, place, -1)


def list_kernel(place_ref, list_ref):
    for r in range(2):

        def step(k, n):
            place = place_ref[r, k]
            list_ref[r, n] = (k << 7) + (place & 127)
            return jnp.where(place >= 0, n + 1, n)

        list_ref[r, TILES] = lax.fori_loop(0, TILES, step, 0)


def listed(place):
    smem = pl.BlockSpec(memory_space=pltpu.SMEM)
    return pl.pallas_call(
        list_kernel,
        out_shape=jax.ShapeDtypeStruct((2, TILES + 1), jnp.int32),
        in_specs=[smem],
        out_specs=smem,
        compiler_params=pltpu.CompilerParams(vmem_limit_bytes=1024 * 1024),
    )(place)


def rows(index):
    return pl.ds(pl.multiple_of(index << 7, SIDE), SIDE)


def multiply(row, lists, parts, buffers):
    vmem = pl.BlockSpec(memory_space=pltpu.VMEM)
    smem = pl.BlockSpec(memory_space=pltpu.SMEM)
    split = AHEAD

    def kernel(list_ref, *rest):
        part_refs, held, out_ref = rest[: len(parts)], rest[len(parts) : -1], rest[-1]
        out_ref[...] = jnp.zeros_like(out_ref)
        n = list_ref[row, TILES]

        @pl.loop(0, (n + BATCH - 1) // BATCH)
        def _(i):
            left, right = [], []
            for j in range(BATCH):
                at = i * BATCH + j
                code = list_ref[row, jnp.minimum(at, n - 1)]
                k = code >> 7
                if len(parts) == 1:
                    tile = part_refs[0][rows(k), :]
                else:
                    tile = part_refs[0][rows(jnp.minimum(k, split - 1)), :]
                    tile = jnp.where(k < split, tile, part_refs[1][rows(jnp.maximum(k - split, 0)), :])
                left.append(jnp.where(at < n, tile, jnp.zeros_like(tile)))
                here = rows(code & 15)
                buffer = (code >> 4) & 7
                block = held[0][here, :]
                for b in range(1, BUFFERS):
                    block = jnp.where(buffer == b, held[b][here, :], block)
                right.append(block)
            out_ref[...] += jnp.dot(
                jnp.concatenate(left, axis=1), jnp.concatenate(right, axis=0), preferred_element_type=jnp.float32
            )

    held = [pltpu.with_memory_space_constraint(a, pltpu.VMEM) for a in (*parts, *buffers)]
    return pl.pallas_call(
        kernel,
        out_shape=jax.ShapeDtypeStruct((SIDE, WIDTH), jnp.float32),
        in_specs=[smem] + [vmem] * len(held),
        out_specs=vmem,
        compiler_params=pltpu.CompilerParams(vmem_limit_bytes=16 * 1024 * 1024),
        cost_estimate=pl.CostEstimate(flops=32 * 2 * SIDE * SIDE * WIDTH, bytes_accessed=3 << 20, transcendentals=0),
    )(lists, *held)


def together(*arrays):
    return lax.optimization_barrier(arrays)


def on_device(features, tiles, columns, weight):
    mine = tiles.reshape(TILES * SIDE, SIDE)
    place = places(jnp.concatenate([columns, from_pair(columns)], axis=0))
    line = jnp.concatenate([features] + [from_line(features, d) for d in (1, 2, 3)], axis=0)
    line, place, ahead = together(line, place, mine[: AHEAD * SIDE])
    first = from_pair(ahead)
    plane = jnp.concatenate([line] + [from_middle(line, d) for d in (1, 2, 3)], axis=0)
    plane, lists, first, behind = together(plane, listed(place), first, mine[AHEAD * SIDE :])
    rest = from_pair(behind)
    buffers = [plane] + [from_last(plane, d) for d in (1, 2, 3)]
    buffers += [from_core(a) for a in buffers]
    across = from_pair(multiply(1, lists, [first, rest], buffers))
    here = multiply(0, lists, [mine], buffers)
    aggregated = (here + across).astype(jnp.bfloat16)
    product = jnp.dot(aggregated, weight, preferred_element_type=jnp.float32)
    return jnp.maximum(product, 0.0).astype(jnp.bfloat16)


def solution(mesh):
    grid = Mesh(mesh.devices.reshape(DIMS), AXES)
    return jax.shard_map(
        on_device,
        mesh=grid,
        in_specs=(P(AXES, None), P(AXES, None, None, None), P(AXES, None), P()),
        out_specs=P(AXES, None),
        check_vma=False,
    )
```

time: 295 us -> 80.1 us (0.27)
  the two profiles are of different devices: /device:TPU:1 before, /device:TPU:66 now
where the time goes in v2:
time: 80.1 us; the launch traced here: 79.7 us
  waiting for transfers between devices  43.6 us (54%)
  starting transfers between devices  25.1 us (31%)
  Pallas kernels  5.92 us (7%)
  local copies, waits for them, and re-layouts  2.59 us (3%)
  other arithmetic  1.6 us (2%)
    ppermute x17, waiting for transfers between devices, move(): return lax.ppermute(a, AXES, found)  43.6 us
    ppermute x17, starting transfers between devices, move(): return lax.ppermute(a, AXES, found)  25.1 us
    pallas_call x2, Pallas kernels, multiply(): pl.pallas_call(kernel, out_shape=jax.ShapeDtypeStruct((SIDE, WIDTH), jnp....  3.7 us
    pallas_call x1, Pallas kernels, listed(): pl.pallas_call(list_kernel, out_shape=jax.ShapeDtypeStruct((2, TILES + 1)...  2.23 us
  transfers between devices with their start and end apart: 17, of which 8 were waited for; matrix products, arithmetic and copies ran while one was open for 4% of the time, Pallas kernels for 5%

profile of v2, /device:TPU:66, one launch (start us, length us, event | category | flops | bytes accessed | tf_op | source)
XLA Modules:
  0.0 79.7 jit_solution(6416870505289453148)
XLA Ops:
  0.0 0.0 copy-start
  0.0 0.0 collective-permute-start
  0.0 6.8 %collective-permute-start.1 = (bf16[128,256]{1,0:T(8,128)(2,1)}, bf16[128,256]{1,0:T(8,128)(2,1)S(1)}, u32[]{:S(2)}, u32[]{:S(2)}) collective-permute-start(bf16[128,256]{1,0:T(8,128)(2,1)} %param.4), channel_id=1, source_target_pairs={{0,64},{1,65},{2,66},{3,67},{4,68},{5,69},{6,70},{7,71},{8,72},{9,... | collective-permute-start | bytes 196616 | tf_op jit(solution)/shard_map/ppermute | solution.py:27
  6.8 2.7 %collective-permute-start.2 = (bf16[128,256]{1,0:T(8,128)(2,1)}, bf16[128,256]{1,0:T(8,128)(2,1)S(1)}, u32[]{:S(2)}, u32[]{:S(2)}) collective-permute-start(bf16[128,256]{1,0:T(8,128)(2,1)} %param.4), channel_id=1, source_target_pairs={{0,32},{1,33},{2,34},{3,35},{4,36},{5,37},{6,38},{7,39},{8,40},{9,... | collective-permute-start | bytes 196616 | tf_op jit(solution)/shard_map/ppermute | solution.py:27
  9.5 1.0 %collective-permute-start.3 = (s32[1,64]{1,0:T(1,128)}, s32[1,64]{1,0:T(1,128)S(1)}, u32[]{:S(2)}, u32[]{:S(2)}) collective-permute-start(s32[1,64]{1,0:T(1,128)} %param.6), channel_id=1, source_target_pairs={{0,16},{1,17},{2,18},{3,19},{4,20},{5,21},{6,22},{7,23},{8,24},{9,... | collective-permute-start | bytes 776 | tf_op jit(solution)/shard_map/ppermute | solution.py:27
  10.6 1.0 %slice.12 = bf16[1,14,128,128]{3,2,1,0:T(8,128)(2,1)S(1)} slice(bf16[1,64,128,128]{3,2,1,0:T(8,128)(2,1)} %param.5), slice={[0:1], [0:14], [0:128], [0:128]} | slice | bytes 917504 | tf_op jit(solution)/shard_map/slice | solution.py:141
  11.6 1.6 %collective-permute-done.3 = s32[1,64]{1,0:T(1,128)S(1)} collective-permute-done((s32[1,64]{1,0:T(1,128)}, s32[1,64]{1,0:T(1,128)S(1)}, u32[]{:S(2)}, u32[]{:S(2)}) %collective-permute-start.3) | collective-permute-done | bytes 288 | tf_op jit(solution)/shard_map/ppermute | solution.py:27
  13.2 0.7 compare_select_fusion.place_ref
  13.9 0.0 collective-permute-done
  13.9 0.0 collective-permute-done.1
  13.9 0.0 collective-permute-done.2
  13.9 0.9 %pad_maximum_fusion.1 = bf16[512,256]{1,0:T(8,128)(2,1)S(1)} fusion(bf16[128,256]{1,0:T(8,128)(2,1)S(1)} %collective-permute-done.2, bf16[128,256]{1,0:T(8,128)(2,1)S(1)} %collective-permute-done.1, bf16[128,256]{1,0:T(8,128)(2,1)S(1)} %collective-permute-done, bf16[128,256]{1,0:T(8,128)(2,1)} %param.4), kind=kLoop, calls=%fused_computation.3 | loop fusion | flops 1048576 | bytes 524288 | tf_op jit(solution)/shard_map/concatenate | solution.py:140
  14.8 3.1 %collective-permute-start.4 = (bf16[512,256]{1,0:T(8,128)(2,1)S(1)}, bf16[512,256]{1,0:T(8,128)(2,1)S(1)}, u32[]{:S(2)}, u32[]{:S(2)}) collective-permute-start(bf16[512,256]{1,0:T(8,128)(2,1)S(1)} %pad_maximum_fusion.1), channel_id=1, source_target_pairs={{0,130},{1,13},{2,0},{3,15},{4,134},{5,1},{6,4},{7,3},{8,138},{9,5... | collective-permute-start | bytes 786440 | tf_op jit(solution)/shard_map/ppermute | solution.py:27
  17.9 0.6 collective-permute-start.5
  18.5 1.0 %collective-permute-start.6 = (bf16[512,256]{1,0:T(8,128)(2,1)S(1)}, bf16[512,256]{1,0:T(8,128)(2,1)S(1)}, u32[]{:S(2)}, u32[]{:S(2)}) collective-permute-start(bf16[512,256]{1,0:T(8,128)(2,1)S(1)} %pad_maximum_fusion.1), channel_id=1, source_target_pairs={{0,2},{1,5},{2,128},{3,7},{4,6},{5,9},{6,132},{7,11},{8,10},{9,13}... | collective-permute-start | bytes 786440 | tf_op jit(solution)/shard_map/ppermute | solution.py:27
  19.5 1.9 %collective-permute-start.7 = (bf16[1792,128]{1,0:T(8,128)(2,1)S(1)}, bf16[1792,128]{1,0:T(8,128)(2,1)S(1)}, u32[]{:S(2)}, u32[]{:S(2)}) collective-permute-start(bf16[1792,128]{1,0:T(8,128)(2,1)S(1)} %bitcast.6), channel_id=1, source_target_pairs={{0,16},{1,17},{2,18},{3,19},{4,20},{5,21},{6,22},{7,23},{8,24},{9,... | collective-permute-start | bytes 1376264 | tf_op jit(solution)/shard_map/ppermute | solution.py:27
  21.3 1.5 %slice.14 = bf16[1,50,128,128]{3,2,1,0:T(8,128)(2,1)S(1)} slice(bf16[1,64,128,128]{3,2,1,0:T(8,128)(2,1)} %param.5), slice={[0:1], [14:64], [0:128], [0:128]} | slice | bytes 3276800 | tf_op jit(solution)/shard_map/slice | solution.py:144
  22.9 2.2 %shard_map.46.list_ref = s32[2,65]{1,0:T(2,128)S(1)} custom-call(s32[2,64]{1,0:T(2,128)S(1)} %compare_select_fusion.place_ref), custom_call_target="tpu_custom_call" | custom-call | tf_op jit(solution)/shard_map/pallas_call | solution.py:76
  25.1 0.0 collective-permute-done.4
  25.1 0.7 collective-permute-done.5
  25.8 2.7 %collective-permute-done.6 = bf16[512,256]{1,0:T(8,128)(2,1)S(1)} collective-permute-done((bf16[512,256]{1,0:T(8,128)(2,1)S(1)}, bf16[512,256]{1,0:T(8,128)(2,1)S(1)}, u32[]{:S(2)}, u32[]{:S(2)}) %collective-permute-start.6) | collective-permute-done | bytes 262176 | tf_op jit(solution)/shard_map/ppermute | solution.py:27
  28.6 0.1 pad_maximum_fusion.rest_1_.rest_2_
  28.6 2.3 %collective-permute-done.7.rest_0_ = bf16[1792,128]{1,0:T(8,128)(2,1)S(1)} collective-permute-done((bf16[1792,128]{1,0:T(8,128)(2,1)S(1)}, bf16[1792,128]{1,0:T(8,128)(2,1)S(1)}, u32[]{:S(2)}, u32[]{:S(2)}) %collective-permute-start.7) | collective-permute-done | bytes 458784 | tf_op jit(solution)/shard_map/ppermute | solution.py:27
  30.9 0.0 copy-start.1
  30.9 0.2 collective-permute-start.8
  31.2 1.5 %collective-permute-start.9 = (bf16[2048,256]{1,0:T(8,128)(2,1)S(1)}, bf16[2048,256]{1,0:T(8,128)(2,1)S(1)}, u32[]{:S(2)}, u32[]{:S(2)}) collective-permute-start(bf16[2048,256]{1,0:T(8,128)(2,1)S(1)} %pad_maximum_fusion.rest_1_.rest_2_), channel_id=1, source_target_pairs={{0,8},{1,129},{2,10},{3,131},{4,12},{5,133},{6,14},{7,135},{8,0},{... | collective-permute-start | bytes 3145736 | tf_op jit(solution)/shard_map/ppermute | solution.py:27
  32.7 2.3 %collective-permute-start.10 = (bf16[2048,256]{1,0:T(8,128)(2,1)S(1)}, bf16[2048,256]{1,0:T(8,128)(2,1)S(1)}, u32[]{:S(2)}, u32[]{:S(2)}) collective-permute-start(bf16[2048,256]{1,0:T(8,128)(2,1)S(1)} %pad_maximum_fusion.rest_1_.rest_2_), channel_id=1, source_target_pairs={{0,4},{1,3},{2,6},{3,129},{4,8},{5,7},{6,10},{7,133},{8,12},{9,11}... | collective-permute-start | bytes 3145736 | tf_op jit(solution)/shard_map/ppermute | solution.py:27
  35.0 1.7 %collective-permute-start.15 = (bf16[6400,128]{1,0:T(8,128)(2,1)S(1)}, bf16[6400,128]{1,0:T(8,128)(2,1)S(1)}, u32[]{:S(2)}, u32[]{:S(2)}) collective-permute-start(bf16[6400,128]{1,0:T(8,128)(2,1)S(1)} %bitcast.5), channel_id=1, source_target_pairs={{0,16},{1,17},{2,18},{3,19},{4,20},{5,21},{6,22},{7,23},{8,24},{9,... | collective-permute-start | bytes 4915208 | tf_op jit(solution)/shard_map/ppermute | solution.py:27
  36.7 0.0 collective-permute-start.11
  36.7 20.2 %collective-permute-done.8.rest_2_.rest_3_ = bf16[2048,256]{1,0:T(8,128)(2,1)S(1)} collective-permute-done((bf16[2048,256]{1,0:T(8,128)(2,1)S(1)}, bf16[2048,256]{1,0:T(8,128)(2,1)S(1)}, u32[]{:S(2)}, u32[]{:S(2)}) %collective-permute-start.8) | collective-permute-done | bytes 1048608 | tf_op jit(solution)/shard_map/ppermute | solution.py:27
  57.0 0.0 collective-permute-start.12
  57.0 0.0 collective-permute-done.9.rest_3_.rest_4_
  57.0 0.5 collective-permute-start.13
  57.5 1.6 %collective-permute-done.10.rest_4_.rest_5_ = bf16[2048,256]{1,0:T(8,128)(2,1)S(1)} collective-permute-done((bf16[2048,256]{1,0:T(8,128)(2,1)S(1)}, bf16[2048,256]{1,0:T(8,128)(2,1)S(1)}, u32[]{:S(2)}, u32[]{:S(2)}) %collective-permute-start.10) | collective-permute-done | bytes 1048608 | tf_op jit(solution)/shard_map/ppermute | solution.py:27
  59.1 0.0 collective-permute-start.14
  59.1 0.0 collective-permute-done.11.rest_5_.rest_6_
  59.1 12.8 %collective-permute-done.15.rest_1_ = bf16[6400,128]{1,0:T(8,128)(2,1)S(1)} collective-permute-done((bf16[6400,128]{1,0:T(8,128)(2,1)S(1)}, bf16[6400,128]{1,0:T(8,128)(2,1)S(1)}, u32[]{:S(2)}, u32[]{:S(2)}) %collective-permute-start.15) | collective-permute-done | bytes 1638432 | tf_op jit(solution)/shard_map/ppermute | solution.py:27
  71.9 0.0 collective-permute-done.12.rest_6_.rest_7_
  71.9 0.0 collective-permute-done.13.rest_7_.rest_8_
  71.9 0.0 collective-permute-done.14.rest_8_.rest_9_
  71.9 2.0 %shard_map.48 = f32[128,256]{1,0:T(8,128)S(1)} custom-call(s32[2,65]{1,0:T(2,128)S(1)} %shard_map.46.list_ref, bf16[1792,128]{1,0:T(8,128)(2,1)S(1)} %collective-permute-done.7.rest_0_, bf16[6400,128]{1,0:T(8,128)(2,1)S(1)} %collective-permute-done.15.rest_1_, bf16[2048,256]{1,0:T(8,128)(2,1)S(1)} %pad_maximum_fusion.rest_1_.rest_2_, ...), custom_call_target="tpu_custom_call" | custom-call | flops 268435456 | bytes 3145728 | tf_op jit(solution)/shard_map/pallas_call | solution.py:123
  73.9 1.7 %collective-permute-start.16 = (f32[128,256]{1,0:T(8,128)S(1)}, f32[128,256]{1,0:T(8,128)S(1)}, u32[]{:S(2)}, u32[]{:S(2)}) collective-permute-start(f32[128,256]{1,0:T(8,128)S(1)} %shard_map.48), channel_id=1, source_target_pairs={{0,16},{1,17},{2,18},{3,19},{4,20},{5,21},{6,22},{7,23},{8,24},{9,... | collective-permute-start | bytes 393224 | tf_op jit(solution)/shard_map/ppermute | solution.py:27
  75.6 0.0 copy-done.1
  75.6 1.7 %shard_map.47 = f32[128,256]{1,0:T(8,128)S(1)} custom-call(s32[2,65]{1,0:T(2,128)S(1)} %shard_map.46.list_ref, bf16[8192,128]{1,0:T(8,128)(2,1)S(1)} %bitcast.4, bf16[2048,256]{1,0:T(8,128)(2,1)S(1)} %pad_maximum_fusion.rest_1_.rest_2_, bf16[2048,256]{1,0:T(8,128)(2,1)S(1)} %collective-permute-done.8.rest_2_.rest_3_, ...), custom_call_target="tpu_custom_call" | custom-call | flops 268435456 | bytes 3145728 | tf_op jit(solution)/shard_map/pallas_call | solution.py:123
  77.3 1.6 %collective-permute-done.16 = f32[128,256]{1,0:T(8,128)S(1)} collective-permute-done((f32[128,256]{1,0:T(8,128)S(1)}, f32[128,256]{1,0:T(8,128)S(1)}, u32[]{:S(2)}, u32[]{:S(2)}) %collective-permute-start.16) | collective-permute-done | bytes 131104 | tf_op jit(solution)/shard_map/ppermute | solution.py:27
  78.9 0.0 copy-done
  78.9 0.8 fusion
Async XLA Ops:
  0.0 78.9 %copy-start = (bf16[256,256]{1,0:T(8,128)(2,1)S(1)}, bf16[256,256]{1,0:T(8,128)(2,1)}, u32[]{:S(2)}) copy-start(bf16[256,256]{1,0:T(8,128)(2,1)} %param.7) | copy-start | bytes 393220
  0.0 13.9 %collective-permute-start = (bf16[128,256]{1,0:T(8,128)(2,1)}, bf16[128,256]{1,0:T(8,128)(2,1)S(1)}, u32[]{:S(2)}, u32[]{:S(2)}) collective-permute-start(bf16[128,256]{1,0:T(8,128)(2,1)} %param.4), channel_id=1, source_target_pairs={{0,96},{1,97},{2,98},{3,99},{4,100},{5,101},{6,102},{7,103},{8,104... | collective-permute-start | bytes 196616 | tf_op jit(solution)/shard_map/ppermute | solution.py:27
  0.0 13.9 %collective-permute-start.1 = (bf16[128,256]{1,0:T(8,128)(2,1)}, bf16[128,256]{1,0:T(8,128)(2,1)S(1)}, u32[]{:S(2)}, u32[]{:S(2)}) collective-permute-start(bf16[128,256]{1,0:T(8,128)(2,1)} %param.4), channel_id=1, source_target_pairs={{0,64},{1,65},{2,66},{3,67},{4,68},{5,69},{6,70},{7,71},{8,72},{9,... | collective-permute-start | bytes 196616 | tf_op jit(solution)/shard_map/ppermute | solution.py:27
  6.8 7.1 %collective-permute-start.2 = (bf16[128,256]{1,0:T(8,128)(2,1)}, bf16[128,256]{1,0:T(8,128)(2,1)S(1)}, u32[]{:S(2)}, u32[]{:S(2)}) collective-permute-start(bf16[128,256]{1,0:T(8,128)(2,1)} %param.4), channel_id=1, source_target_pairs={{0,32},{1,33},{2,34},{3,35},{4,36},{5,37},{6,38},{7,39},{8,40},{9,... | collective-permute-start | bytes 196616 | tf_op jit(solution)/shard_map/ppermute | solution.py:27
  9.5 3.7 %collective-permute-start.3 = (s32[1,64]{1,0:T(1,128)}, s32[1,64]{1,0:T(1,128)S(1)}, u32[]{:S(2)}, u32[]{:S(2)}) collective-permute-start(s32[1,64]{1,0:T(1,128)} %param.6), channel_id=1, source_target_pairs={{0,16},{1,17},{2,18},{3,19},{4,20},{5,21},{6,22},{7,23},{8,24},{9,... | collective-permute-start | bytes 776 | tf_op jit(solution)/shard_map/ppermute | solution.py:27
  14.8 10.4 %collective-permute-start.4 = (bf16[512,256]{1,0:T(8,128)(2,1)S(1)}, bf16[512,256]{1,0:T(8,128)(2,1)S(1)}, u32[]{:S(2)}, u32[]{:S(2)}) collective-permute-start(bf16[512,256]{1,0:T(8,128)(2,1)S(1)} %pad_maximum_fusion.1), channel_id=1, source_target_pairs={{0,130},{1,13},{2,0},{3,15},{4,134},{5,1},{6,4},{7,3},{8,138},{9,5... | collective-permute-start | bytes 786440 | tf_op jit(solution)/shard_map/ppermute | solution.py:27
  17.9 8.0 %collective-permute-start.5 = (bf16[512,256]{1,0:T(8,128)(2,1)S(1)}, bf16[512,256]{1,0:T(8,128)(2,1)S(1)}, u32[]{:S(2)}, u32[]{:S(2)}) collective-permute-start(bf16[512,256]{1,0:T(8,128)(2,1)S(1)} %pad_maximum_fusion.1), channel_id=1, source_target_pairs={{0,128},{1,9},{2,130},{3,11},{4,132},{5,13},{6,134},{7,15},{8,136}... | collective-permute-start | bytes 786440 | tf_op jit(solution)/shard_map/ppermute | solution.py:27
  18.5 10.1 %collective-permute-start.6 = (bf16[512,256]{1,0:T(8,128)(2,1)S(1)}, bf16[512,256]{1,0:T(8,128)(2,1)S(1)}, u32[]{:S(2)}, u32[]{:S(2)}) collective-permute-start(bf16[512,256]{1,0:T(8,128)(2,1)S(1)} %pad_maximum_fusion.1), channel_id=1, source_target_pairs={{0,2},{1,5},{2,128},{3,7},{4,6},{5,9},{6,132},{7,11},{8,10},{9,13}... | collective-permute-start | bytes 786440 | tf_op jit(solution)/shard_map/ppermute | solution.py:27
  19.5 11.5 %collective-permute-start.7 = (bf16[1792,128]{1,0:T(8,128)(2,1)S(1)}, bf16[1792,128]{1,0:T(8,128)(2,1)S(1)}, u32[]{:S(2)}, u32[]{:S(2)}) collective-permute-start(bf16[1792,128]{1,0:T(8,128)(2,1)S(1)} %bitcast.6), channel_id=1, source_target_pairs={{0,16},{1,17},{2,18},{3,19},{4,20},{5,21},{6,22},{7,23},{8,24},{9,... | collective-permute-start | bytes 1376264 | tf_op jit(solution)/shard_map/ppermute | solution.py:27
  30.9 44.6 %copy-start.1 = (bf16[1,64,128,128]{3,2,1,0:T(8,128)(2,1)S(1)}, bf16[1,64,128,128]{3,2,1,0:T(8,128)(2,1)}, u32[]{:S(2)}) copy-start(bf16[1,64,128,128]{3,2,1,0:T(8,128)(2,1)} %param.5) | copy-start | bytes 6291460
  30.9 26.0 %collective-permute-start.8 = (bf16[2048,256]{1,0:T(8,128)(2,1)S(1)}, bf16[2048,256]{1,0:T(8,128)(2,1)S(1)}, u32[]{:S(2)}, u32[]{:S(2)}) collective-permute-start(bf16[2048,256]{1,0:T(8,128)(2,1)S(1)} %pad_maximum_fusion.rest_1_.rest_2_), channel_id=1, source_target_pairs={{0,12},{1,131},{2,14},{3,1},{4,0},{5,135},{6,2},{7,5},{8,4},{9,139... | collective-permute-start | bytes 3145736 | tf_op jit(solution)/shard_map/ppermute | solution.py:27
  31.2 25.8 %collective-permute-start.9 = (bf16[2048,256]{1,0:T(8,128)(2,1)S(1)}, bf16[2048,256]{1,0:T(8,128)(2,1)S(1)}, u32[]{:S(2)}, u32[]{:S(2)}) collective-permute-start(bf16[2048,256]{1,0:T(8,128)(2,1)S(1)} %pad_maximum_fusion.rest_1_.rest_2_), channel_id=1, source_target_pairs={{0,8},{1,129},{2,10},{3,131},{4,12},{5,133},{6,14},{7,135},{8,0},{... | collective-permute-start | bytes 3145736 | tf_op jit(solution)/shard_map/ppermute | solution.py:27
  32.7 26.4 %collective-permute-start.10 = (bf16[2048,256]{1,0:T(8,128)(2,1)S(1)}, bf16[2048,256]{1,0:T(8,128)(2,1)S(1)}, u32[]{:S(2)}, u32[]{:S(2)}) collective-permute-start(bf16[2048,256]{1,0:T(8,128)(2,1)S(1)} %pad_maximum_fusion.rest_1_.rest_2_), channel_id=1, source_target_pairs={{0,4},{1,3},{2,6},{3,129},{4,8},{5,7},{6,10},{7,133},{8,12},{9,11}... | collective-permute-start | bytes 3145736 | tf_op jit(solution)/shard_map/ppermute | solution.py:27
  35.0 36.9 %collective-permute-start.15 = (bf16[6400,128]{1,0:T(8,128)(2,1)S(1)}, bf16[6400,128]{1,0:T(8,128)(2,1)S(1)}, u32[]{:S(2)}, u32[]{:S(2)}) collective-permute-start(bf16[6400,128]{1,0:T(8,128)(2,1)S(1)} %bitcast.5), channel_id=1, source_target_pairs={{0,16},{1,17},{2,18},{3,19},{4,20},{5,21},{6,22},{7,23},{8,24},{9,... | collective-permute-start | bytes 4915208 | tf_op jit(solution)/shard_map/ppermute | solution.py:27
  36.7 22.4 %collective-permute-start.11 = (bf16[2048,256]{1,0:T(8,128)(2,1)S(1)}, bf16[2048,256]{1,0:T(8,128)(2,1)S(1)}, u32[]{:S(2)}, u32[]{:S(2)}) collective-permute-start(bf16[2048,256]{1,0:T(8,128)(2,1)S(1)} %pad_maximum_fusion.rest_1_.rest_2_), channel_id=1, source_target_pairs={{0,1},{1,0},{2,3},{3,2},{4,5},{5,4},{6,7},{7,6},{8,9},{9,8},{10,11... | collective-permute-start | bytes 3145736 | tf_op jit(solution)/shard_map/ppermute | solution.py:27
  57.0 14.9 %collective-permute-start.12 = (bf16[2048,256]{1,0:T(8,128)(2,1)S(1)}, bf16[2048,256]{1,0:T(8,128)(2,1)S(1)}, u32[]{:S(2)}, u32[]{:S(2)}) collective-permute-start(bf16[2048,256]{1,0:T(8,128)(2,1)S(1)} %collective-permute-done.8.rest_2_.rest_3_), channel_id=1, source_target_pairs={{0,1},{1,0},{2,3},{3,2},{4,5},{5,4},{6,7},{7,6},{8,9},{9,8},{10,11... | collective-permute-start | bytes 3145736 | tf_op jit(solution)/shard_map/ppermute | solution.py:27
  57.0 14.9 %collective-permute-start.13 = (bf16[2048,256]{1,0:T(8,128)(2,1)S(1)}, bf16[2048,256]{1,0:T(8,128)(2,1)S(1)}, u32[]{:S(2)}, u32[]{:S(2)}) collective-permute-start(bf16[2048,256]{1,0:T(8,128)(2,1)S(1)} %collective-permute-done.9.rest_3_.rest_4_), channel_id=1, source_target_pairs={{0,1},{1,0},{2,3},{3,2},{4,5},{5,4},{6,7},{7,6},{8,9},{9,8},{10,11... | collective-permute-start | bytes 3145736 | tf_op jit(solution)/shard_map/ppermute | solution.py:27
  59.1 12.8 %collective-permute-start.14 = (bf16[2048,256]{1,0:T(8,128)(2,1)S(1)}, bf16[2048,256]{1,0:T(8,128)(2,1)S(1)}, u32[]{:S(2)}, u32[]{:S(2)}) collective-permute-start(bf16[2048,256]{1,0:T(8,128)(2,1)S(1)} %collective-permute-done.10.rest_4_.rest_5_), channel_id=1, source_target_pairs={{0,1},{1,0},{2,3},{3,2},{4,5},{5,4},{6,7},{7,6},{8,9},{9,8},{10,11... | collective-permute-start | bytes 3145736 | tf_op jit(solution)/shard_map/ppermute | solution.py:27
  73.9 5.1 %collective-permute-start.16 = (f32[128,256]{1,0:T(8,128)S(1)}, f32[128,256]{1,0:T(8,128)S(1)}, u32[]{:S(2)}, u32[]{:S(2)}) collective-permute-start(f32[128,256]{1,0:T(8,128)S(1)} %shard_map.48), channel_id=1, source_target_pairs={{0,16},{1,17},{2,18},{3,19},{4,20},{5,21},{6,22},{7,23},{8,24},{9,... | collective-permute-start | bytes 393224 | tf_op jit(solution)/shard_map/ppermute | solution.py:27

commit v3 on v2

--- a/solution.py
+++ b/solution.py
@@ -137,15 +137,18 @@
 def on_device(features, tiles, columns, weight):
     mine = tiles.reshape(TILES * SIDE, SIDE)
     place = places(jnp.concatenate([columns, from_pair(columns)], axis=0))
-    line = jnp.concatenate([features] + [from_line(features, d) for d in (1, 2, 3)], axis=0)
-    line, place, ahead = together(line, place, mine[: AHEAD * SIDE])
-    first = from_pair(ahead)
+    lines = [features] + [from_line(features, d) for d in (1, 2, 3)]
+    lines[1], sent = together(lines[1], mine)
+    line = jnp.concatenate(lines, axis=0)
+    line, place = together(line, place)
+    paired = from_pair(sent)
     plane = jnp.concatenate([line] + [from_middle(line, d) for d in (1, 2, 3)], axis=0)
-    plane, lists, first, behind = together(plane, listed(place), first, mine[AHEAD * SIDE :])
-    rest = from_pair(behind)
+    plane, place = together(plane, place)
+    lists = listed(place)
     buffers = [plane] + [from_last(plane, d) for d in (1, 2, 3)]
     buffers += [from_core(a) for a in buffers]
-    across = from_pair(multiply(1, lists, [first, rest], buffers))
+    paired = together(paired)[0]
+    across = from_pair(multiply(1, lists, [paired], buffers))
     here = multiply(0, lists, [mine], buffers)
     aggregated = (here + across).astype(jnp.bfloat16)
     product = jnp.dot(aggregated, weight, preferred_element_type=jnp.float32)

time: 80.1 us -> 74.9 us (0.935)
  the two profiles are of different devices: /device:TPU:66 before, /device:TPU:10 now
where the time goes in v3:
time: 74.9 us; the launch traced here: 74.8 us
  waiting for transfers between devices  42.5 us (57%)
  starting transfers between devices  22.9 us (31%)
  Pallas kernels  6.91 us (9%)
  other arithmetic  1.6 us (2%)
  matrix products  0.8 us (1%)
    ppermute x16, waiting for transfers between devices, move(): return lax.ppermute(a, AXES, found)  42.5 us
    ppermute x16, starting transfers between devices, move(): return lax.ppermute(a, AXES, found)  22.9 us
    pallas_call x2, Pallas kernels, multiply(): pl.pallas_call(kernel, out_shape=jax.ShapeDtypeStruct((SIDE, WIDTH), jnp....  4.68 us
    pallas_call x1, Pallas kernels, listed(): pl.pallas_call(list_kernel, out_shape=jax.ShapeDtypeStruct((2, TILES + 1)...  2.23 us
  transfers between devices with their start and end apart: 16, of which 10 were waited for; matrix products, arithmetic and copies ran while one was open for 1% of the time, Pallas kernels for 6%

profile of v3, /device:TPU:10, one launch (start us, length us, event | category | flops | bytes accessed | tf_op | source)
XLA Modules:
  0.0 74.8 jit_solution(8057868641887308263)
XLA Ops:
  0.0 0.0 copy-start
  0.0 6.3 %collective-permute-start = (bf16[128,256]{1,0:T(8,128)(2,1)}, bf16[128,256]{1,0:T(8,128)(2,1)S(1)}, u32[]{:S(2)}, u32[]{:S(2)}) collective-permute-start(bf16[128,256]{1,0:T(8,128)(2,1)} %param.4), channel_id=1, source_target_pairs={{0,96},{1,97},{2,98},{3,99},{4,100},{5,101},{6,102},{7,103},{8,104... | collective-permute-start | bytes 196616 | tf_op jit(solution)/shard_map/ppermute | solution.py:27
  6.3 1.0 %collective-permute-start.1 = (bf16[128,256]{1,0:T(8,128)(2,1)}, bf16[128,256]{1,0:T(8,128)(2,1)S(1)}, u32[]{:S(2)}, u32[]{:S(2)}) collective-permute-start(bf16[128,256]{1,0:T(8,128)(2,1)} %param.4), channel_id=1, source_target_pairs={{0,64},{1,65},{2,66},{3,67},{4,68},{5,69},{6,70},{7,71},{8,72},{9,... | collective-permute-start | bytes 196616 | tf_op jit(solution)/shard_map/ppermute | solution.py:27
  7.3 2.8 %collective-permute-start.2 = (bf16[128,256]{1,0:T(8,128)(2,1)}, bf16[128,256]{1,0:T(8,128)(2,1)S(1)}, u32[]{:S(2)}, u32[]{:S(2)}) collective-permute-start(bf16[128,256]{1,0:T(8,128)(2,1)} %param.4), channel_id=1, source_target_pairs={{0,32},{1,33},{2,34},{3,35},{4,36},{5,37},{6,38},{7,39},{8,40},{9,... | collective-permute-start | bytes 196616 | tf_op jit(solution)/shard_map/ppermute | solution.py:27
  10.1 1.0 %collective-permute-start.3 = (s32[1,64]{1,0:T(1,128)}, s32[1,64]{1,0:T(1,128)S(1)}, u32[]{:S(2)}, u32[]{:S(2)}) collective-permute-start(s32[1,64]{1,0:T(1,128)} %param.6), channel_id=1, source_target_pairs={{0,16},{1,17},{2,18},{3,19},{4,20},{5,21},{6,22},{7,23},{8,24},{9,... | collective-permute-start | bytes 776 | tf_op jit(solution)/shard_map/ppermute | solution.py:27
  11.1 2.7 %collective-permute-done.3 = s32[1,64]{1,0:T(1,128)S(1)} collective-permute-done((s32[1,64]{1,0:T(1,128)}, s32[1,64]{1,0:T(1,128)S(1)}, u32[]{:S(2)}, u32[]{:S(2)}) %collective-permute-start.3) | collective-permute-done | bytes 288 | tf_op jit(solution)/shard_map/ppermute | solution.py:27
  13.8 0.7 compare_select_fusion.place_ref
  14.5 0.0 collective-permute-done
  14.5 1.3 %collective-permute-done.1 = bf16[128,256]{1,0:T(8,128)(2,1)S(1)} collective-permute-done((bf16[128,256]{1,0:T(8,128)(2,1)}, bf16[128,256]{1,0:T(8,128)(2,1)S(1)}, u32[]{:S(2)}, u32[]{:S(2)}) %collective-permute-start.1) | collective-permute-done | bytes 65568 | tf_op jit(solution)/shard_map/ppermute | solution.py:27
  15.8 0.0 collective-permute-done.2
  15.8 0.9 %pad_maximum_fusion.1 = bf16[512,256]{1,0:T(8,128)(2,1)S(1)} fusion(bf16[128,256]{1,0:T(8,128)(2,1)S(1)} %collective-permute-done.2, bf16[128,256]{1,0:T(8,128)(2,1)S(1)} %collective-permute-done.1, bf16[128,256]{1,0:T(8,128)(2,1)S(1)} %collective-permute-done, bf16[128,256]{1,0:T(8,128)(2,1)} %param.4), kind=kLoop, calls=%fused_computation.3 | loop fusion | flops 1048576 | bytes 524288 | tf_op jit(solution)/shard_map/concatenate | solution.py:142
  16.7 0.5 collective-permute-start.4
  17.2 2.6 %collective-permute-start.5 = (bf16[512,256]{1,0:T(8,128)(2,1)S(1)}, bf16[512,256]{1,0:T(8,128)(2,1)S(1)}, u32[]{:S(2)}, u32[]{:S(2)}) collective-permute-start(bf16[512,256]{1,0:T(8,128)(2,1)S(1)} %pad_maximum_fusion.1), channel_id=1, source_target_pairs={{0,128},{1,9},{2,130},{3,11},{4,132},{5,13},{6,134},{7,15},{8,136}... | collective-permute-start | bytes 786440 | tf_op jit(solution)/shard_map/ppermute | solution.py:27
  19.8 1.9 %collective-permute-start.6 = (bf16[512,256]{1,0:T(8,128)(2,1)S(1)}, bf16[512,256]{1,0:T(8,128)(2,1)S(1)}, u32[]{:S(2)}, u32[]{:S(2)}) collective-permute-start(bf16[512,256]{1,0:T(8,128)(2,1)S(1)} %pad_maximum_fusion.1), channel_id=1, source_target_pairs={{0,2},{1,5},{2,128},{3,7},{4,6},{5,9},{6,132},{7,11},{8,10},{9,13}... | collective-permute-start | bytes 786440 | tf_op jit(solution)/shard_map/ppermute | solution.py:27
  21.7 1.1 %collective-permute-start.14 = (bf16[8192,128]{1,0:T(8,128)(2,1)}, bf16[8192,128]{1,0:T(8,128)(2,1)S(1)}, u32[]{:S(2)}, u32[]{:S(2)}) collective-permute-start(bf16[8192,128]{1,0:T(8,128)(2,1)} %bitcast.2), channel_id=1, source_target_pairs={{0,16},{1,17},{2,18},{3,19},{4,20},{5,21},{6,22},{7,23},{8,24},{9,... | collective-permute-start | bytes 6291464 | tf_op jit(solution)/shard_map/ppermute | solution.py:27
  22.7 0.4 collective-permute-done.4
  23.1 3.8 %collective-permute-done.5 = bf16[512,256]{1,0:T(8,128)(2,1)S(1)} collective-permute-done((bf16[512,256]{1,0:T(8,128)(2,1)S(1)}, bf16[512,256]{1,0:T(8,128)(2,1)S(1)}, u32[]{:S(2)}, u32[]{:S(2)}) %collective-permute-start.5) | collective-permute-done | bytes 262176 | tf_op jit(solution)/shard_map/ppermute | solution.py:27
  26.9 1.1 %collective-permute-done.6 = bf16[512,256]{1,0:T(8,128)(2,1)S(1)} collective-permute-done((bf16[512,256]{1,0:T(8,128)(2,1)S(1)}, bf16[512,256]{1,0:T(8,128)(2,1)S(1)}, u32[]{:S(2)}, u32[]{:S(2)}) %collective-permute-start.6) | collective-permute-done | bytes 262176 | tf_op jit(solution)/shard_map/ppermute | solution.py:27
  28.0 0.1 pad_maximum_fusion.rest_1_
  28.1 0.6 collective-permute-start.7
  28.7 2.4 %collective-permute-start.8 = (bf16[2048,256]{1,0:T(8,128)(2,1)S(1)}, bf16[2048,256]{1,0:T(8,128)(2,1)S(1)}, u32[]{:S(2)}, u32[]{:S(2)}) collective-permute-start(bf16[2048,256]{1,0:T(8,128)(2,1)S(1)} %pad_maximum_fusion.rest_1_), channel_id=1, source_target_pairs={{0,8},{1,129},{2,10},{3,131},{4,12},{5,133},{6,14},{7,135},{8,0},{... | collective-permute-start | bytes 3145736 | tf_op jit(solution)/shard_map/ppermute | solution.py:27
  31.1 1.8 %collective-permute-start.9 = (bf16[2048,256]{1,0:T(8,128)(2,1)S(1)}, bf16[2048,256]{1,0:T(8,128)(2,1)S(1)}, u32[]{:S(2)}, u32[]{:S(2)}) collective-permute-start(bf16[2048,256]{1,0:T(8,128)(2,1)S(1)} %pad_maximum_fusion.rest_1_), channel_id=1, source_target_pairs={{0,4},{1,3},{2,6},{3,129},{4,8},{5,7},{6,10},{7,133},{8,12},{9,11}... | collective-permute-start | bytes 3145736 | tf_op jit(solution)/shard_map/ppermute | solution.py:27
  32.9 0.0 collective-permute-start.10
  32.9 10.0 %collective-permute-done.7.rest_2_ = bf16[2048,256]{1,0:T(8,128)(2,1)S(1)} collective-permute-done((bf16[2048,256]{1,0:T(8,128)(2,1)S(1)}, bf16[2048,256]{1,0:T(8,128)(2,1)S(1)}, u32[]{:S(2)}, u32[]{:S(2)}) %collective-permute-start.7) | collective-permute-done | bytes 1048608 | tf_op jit(solution)/shard_map/ppermute | solution.py:27
  42.9 0.0 collective-permute-start.11
  42.9 12.2 %collective-permute-done.8.rest_3_ = bf16[2048,256]{1,0:T(8,128)(2,1)S(1)} collective-permute-done((bf16[2048,256]{1,0:T(8,128)(2,1)S(1)}, bf16[2048,256]{1,0:T(8,128)(2,1)S(1)}, u32[]{:S(2)}, u32[]{:S(2)}) %collective-permute-start.8) | collective-permute-done | bytes 1048608 | tf_op jit(solution)/shard_map/ppermute | solution.py:27
  55.1 0.0 collective-permute-start.12
  55.1 1.2 %collective-permute-done.9.rest_4_ = bf16[2048,256]{1,0:T(8,128)(2,1)S(1)} collective-permute-done((bf16[2048,256]{1,0:T(8,128)(2,1)S(1)}, bf16[2048,256]{1,0:T(8,128)(2,1)S(1)}, u32[]{:S(2)}, u32[]{:S(2)}) %collective-permute-start.9) | collective-permute-done | bytes 1048608 | tf_op jit(solution)/shard_map/ppermute | solution.py:27
  56.3 0.0 collective-permute-start.13
  56.3 2.2 %shard_map.46.list_ref = s32[2,65]{1,0:T(2,128)S(1)} custom-call(s32[2,64]{1,0:T(2,128)S(1)} %compare_select_fusion.place_ref), custom_call_target="tpu_custom_call" | custom-call | tf_op jit(solution)/shard_map/pallas_call | solution.py:76
  58.5 0.0 copy-start.1
  58.5 8.0 %collective-permute-done.14.rest_0_ = bf16[8192,128]{1,0:T(8,128)(2,1)S(1)} collective-permute-done((bf16[8192,128]{1,0:T(8,128)(2,1)}, bf16[8192,128]{1,0:T(8,128)(2,1)S(1)}, u32[]{:S(2)}, u32[]{:S(2)}) %collective-permute-start.14) | collective-permute-done | bytes 2097184 | tf_op jit(solution)/shard_map/ppermute | solution.py:27
  66.5 0.0 collective-permute-done.10.rest_5_
  66.5 0.0 collective-permute-done.11.rest_6_
  66.5 0.0 collective-permute-done.12.rest_7_
  66.5 0.0 collective-permute-done.13.rest_8_
  66.5 2.3 %shard_map.48 = f32[128,256]{1,0:T(8,128)S(1)} custom-call(s32[2,65]{1,0:T(2,128)S(1)} %shard_map.46.list_ref, bf16[8192,128]{1,0:T(8,128)(2,1)S(1)} %collective-permute-done.14.rest_0_, bf16[2048,256]{1,0:T(8,128)(2,1)S(1)} %pad_maximum_fusion.rest_1_, bf16[2048,256]{1,0:T(8,128)(2,1)S(1)} %collective-permute-done.7.rest_2_, ...), custom_call_target="tpu_custom_call" | custom-call | flops 268435456 | bytes 3145728 | tf_op jit(solution)/shard_map/pallas_call | solution.py:123
  68.9 0.8 %collective-permute-start.15 = (f32[128,256]{1,0:T(8,128)S(1)}, f32[128,256]{1,0:T(8,128)S(1)}, u32[]{:S(2)}, u32[]{:S(2)}) collective-permute-start(f32[128,256]{1,0:T(8,128)S(1)} %shard_map.48), channel_id=1, source_target_pairs={{0,16},{1,17},{2,18},{3,19},{4,20},{5,21},{6,22},{7,23},{8,24},{9,... | collective-permute-start | bytes 393224 | tf_op jit(solution)/shard_map/ppermute | solution.py:27
  69.7 0.0 copy-done.1
  69.7 2.3 %shard_map.47 = f32[128,256]{1,0:T(8,128)S(1)} custom-call(s32[2,65]{1,0:T(2,128)S(1)} %shard_map.46.list_ref, bf16[8192,128]{1,0:T(8,128)(2,1)S(1)} %bitcast.3, bf16[2048,256]{1,0:T(8,128)(2,1)S(1)} %pad_maximum_fusion.rest_1_, bf16[2048,256]{1,0:T(8,128)(2,1)S(1)} %collective-permute-done.7.rest_2_, bf16[2048,256]{1,0:T(8,128)(2,1)S(1)} %collective-permute-done.8.rest_3_, ...), custom_call_target="tpu_custom_call" | custom-call | flops 268435456 | bytes 3145728 | tf_op jit(solution)/shard_map/pallas_call | solution.py:123
  72.1 1.9 %collective-permute-done.15 = f32[128,256]{1,0:T(8,128)S(1)} collective-permute-done((f32[128,256]{1,0:T(8,128)S(1)}, f32[128,256]{1,0:T(8,128)S(1)}, u32[]{:S(2)}, u32[]{:S(2)}) %collective-permute-start.15) | collective-permute-done | bytes 131104 | tf_op jit(solution)/shard_map/ppermute | solution.py:27
  74.0 0.0 copy-done
  74.0 0.8 %fusion = bf16[128,256]{1,0:T(8,128)(2,1)} fusion(bf16[256,256]{1,0:T(8,128)(2,1)S(1)} %copy-done, f32[128,256]{1,0:T(8,128)S(1)} %shard_map.47, f32[128,256]{1,0:T(8,128)S(1)} %collective-permute-done.15), kind=kOutput, calls=%fused_computation.1 | convolution fusion | flops 16908288 | bytes 458752 | tf_op jit(solution)/shard_map/dot_general | solution.py:154
Async XLA Ops:
  0.0 74.0 %copy-start = (bf16[256,256]{1,0:T(8,128)(2,1)S(1)}, bf16[256,256]{1,0:T(8,128)(2,1)}, u32[]{:S(2)}) copy-start(bf16[256,256]{1,0:T(8,128)(2,1)} %param.7) | copy-start | bytes 393220
  0.0 14.5 %collective-permute-start = (bf16[128,256]{1,0:T(8,128)(2,1)}, bf16[128,256]{1,0:T(8,128)(2,1)S(1)}, u32[]{:S(2)}, u32[]{:S(2)}) collective-permute-start(bf16[128,256]{1,0:T(8,128)(2,1)} %param.4), channel_id=1, source_target_pairs={{0,96},{1,97},{2,98},{3,99},{4,100},{5,101},{6,102},{7,103},{8,104... | collective-permute-start | bytes 196616 | tf_op jit(solution)/shard_map/ppermute | solution.py:27
  6.3 9.5 %collective-permute-start.1 = (bf16[128,256]{1,0:T(8,128)(2,1)}, bf16[128,256]{1,0:T(8,128)(2,1)S(1)}, u32[]{:S(2)}, u32[]{:S(2)}) collective-permute-start(bf16[128,256]{1,0:T(8,128)(2,1)} %param.4), channel_id=1, source_target_pairs={{0,64},{1,65},{2,66},{3,67},{4,68},{5,69},{6,70},{7,71},{8,72},{9,... | collective-permute-start | bytes 196616 | tf_op jit(solution)/shard_map/ppermute | solution.py:27
  7.3 8.5 %collective-permute-start.2 = (bf16[128,256]{1,0:T(8,128)(2,1)}, bf16[128,256]{1,0:T(8,128)(2,1)S(1)}, u32[]{:S(2)}, u32[]{:S(2)}) collective-permute-start(bf16[128,256]{1,0:T(8,128)(2,1)} %param.4), channel_id=1, source_target_pairs={{0,32},{1,33},{2,34},{3,35},{4,36},{5,37},{6,38},{7,39},{8,40},{9,... | collective-permute-start | bytes 196616 | tf_op jit(solution)/shard_map/ppermute | solution.py:27
  10.1 3.7 %collective-permute-start.3 = (s32[1,64]{1,0:T(1,128)}, s32[1,64]{1,0:T(1,128)S(1)}, u32[]{:S(2)}, u32[]{:S(2)}) collective-permute-start(s32[1,64]{1,0:T(1,128)} %param.6), channel_id=1, source_target_pairs={{0,16},{1,17},{2,18},{3,19},{4,20},{5,21},{6,22},{7,23},{8,24},{9,... | collective-permute-start | bytes 776 | tf_op jit(solution)/shard_map/ppermute | solution.py:27
  16.7 6.4 %collective-permute-start.4 = (bf16[512,256]{1,0:T(8,128)(2,1)S(1)}, bf16[512,256]{1,0:T(8,128)(2,1)S(1)}, u32[]{:S(2)}, u32[]{:S(2)}) collective-permute-start(bf16[512,256]{1,0:T(8,128)(2,1)S(1)} %pad_maximum_fusion.1), channel_id=1, source_target_pairs={{0,130},{1,13},{2,0},{3,15},{4,134},{5,1},{6,4},{7,3},{8,138},{9,5... | collective-permute-start | bytes 786440 | tf_op jit(solution)/shard_map/ppermute | solution.py:27
  17.2 9.7 %collective-permute-start.5 = (bf16[512,256]{1,0:T(8,128)(2,1)S(1)}, bf16[512,256]{1,0:T(8,128)(2,1)S(1)}, u32[]{:S(2)}, u32[]{:S(2)}) collective-permute-start(bf16[512,256]{1,0:T(8,128)(2,1)S(1)} %pad_maximum_fusion.1), channel_id=1, source_target_pairs={{0,128},{1,9},{2,130},{3,11},{4,132},{5,13},{6,134},{7,15},{8,136}... | collective-permute-start | bytes 786440 | tf_op jit(solution)/shard_map/ppermute | solution.py:27
  19.8 8.2 %collective-permute-start.6 = (bf16[512,256]{1,0:T(8,128)(2,1)S(1)}, bf16[512,256]{1,0:T(8,128)(2,1)S(1)}, u32[]{:S(2)}, u32[]{:S(2)}) collective-permute-start(bf16[512,256]{1,0:T(8,128)(2,1)S(1)} %pad_maximum_fusion.1), channel_id=1, source_target_pairs={{0,2},{1,5},{2,128},{3,7},{4,6},{5,9},{6,132},{7,11},{8,10},{9,13}... | collective-permute-start | bytes 786440 | tf_op jit(solution)/shard_map/ppermute | solution.py:27
  21.7 44.8 %collective-permute-start.14 = (bf16[8192,128]{1,0:T(8,128)(2,1)}, bf16[8192,128]{1,0:T(8,128)(2,1)S(1)}, u32[]{:S(2)}, u32[]{:S(2)}) collective-permute-start(bf16[8192,128]{1,0:T(8,128)(2,1)} %bitcast.2), channel_id=1, source_target_pairs={{0,16},{1,17},{2,18},{3,19},{4,20},{5,21},{6,22},{7,23},{8,24},{9,... | collective-permute-start | bytes 6291464 | tf_op jit(solution)/shard_map/ppermute | solution.py:27
  28.1 14.9 %collective-permute-start.7 = (bf16[2048,256]{1,0:T(8,128)(2,1)S(1)}, bf16[2048,256]{1,0:T(8,128)(2,1)S(1)}, u32[]{:S(2)}, u32[]{:S(2)}) collective-permute-start(bf16[2048,256]{1,0:T(8,128)(2,1)S(1)} %pad_maximum_fusion.rest_1_), channel_id=1, source_target_pairs={{0,12},{1,131},{2,14},{3,1},{4,0},{5,135},{6,2},{7,5},{8,4},{9,139... | collective-permute-start | bytes 3145736 | tf_op jit(solution)/shard_map/ppermute | solution.py:27
  28.7 26.4 %collective-permute-start.8 = (bf16[2048,256]{1,0:T(8,128)(2,1)S(1)}, bf16[2048,256]{1,0:T(8,128)(2,1)S(1)}, u32[]{:S(2)}, u32[]{:S(2)}) collective-permute-start(bf16[2048,256]{1,0:T(8,128)(2,1)S(1)} %pad_maximum_fusion.rest_1_), channel_id=1, source_target_pairs={{0,8},{1,129},{2,10},{3,131},{4,12},{5,133},{6,14},{7,135},{8,0},{... | collective-permute-start | bytes 3145736 | tf_op jit(solution)/shard_map/ppermute | solution.py:27
  31.1 25.2 %collective-permute-start.9 = (bf16[2048,256]{1,0:T(8,128)(2,1)S(1)}, bf16[2048,256]{1,0:T(8,128)(2,1)S(1)}, u32[]{:S(2)}, u32[]{:S(2)}) collective-permute-start(bf16[2048,256]{1,0:T(8,128)(2,1)S(1)} %pad_maximum_fusion.rest_1_), channel_id=1, source_target_pairs={{0,4},{1,3},{2,6},{3,129},{4,8},{5,7},{6,10},{7,133},{8,12},{9,11}... | collective-permute-start | bytes 3145736 | tf_op jit(solution)/shard_map/ppermute | solution.py:27
  32.9 33.6 %collective-permute-start.10 = (bf16[2048,256]{1,0:T(8,128)(2,1)S(1)}, bf16[2048,256]{1,0:T(8,128)(2,1)S(1)}, u32[]{:S(2)}, u32[]{:S(2)}) collective-permute-start(bf16[2048,256]{1,0:T(8,128)(2,1)S(1)} %pad_maximum_fusion.rest_1_), channel_id=1, source_target_pairs={{0,1},{1,0},{2,3},{3,2},{4,5},{5,4},{6,7},{7,6},{8,9},{9,8},{10,11... | collective-permute-start | bytes 3145736 | tf_op jit(solution)/shard_map/ppermute | solution.py:27
  42.9 23.6 %collective-permute-start.11 = (bf16[2048,256]{1,0:T(8,128)(2,1)S(1)}, bf16[2048,256]{1,0:T(8,128)(2,1)S(1)}, u32[]{:S(2)}, u32[]{:S(2)}) collective-permute-start(bf16[2048,256]{1,0:T(8,128)(2,1)S(1)} %collective-permute-done.7.rest_2_), channel_id=1, source_target_pairs={{0,1},{1,0},{2,3},{3,2},{4,5},{5,4},{6,7},{7,6},{8,9},{9,8},{10,11... | collective-permute-start | bytes 3145736 | tf_op jit(solution)/shard_map/ppermute | solution.py:27
  55.1 11.4 %collective-permute-start.12 = (bf16[2048,256]{1,0:T(8,128)(2,1)S(1)}, bf16[2048,256]{1,0:T(8,128)(2,1)S(1)}, u32[]{:S(2)}, u32[]{:S(2)}) collective-permute-start(bf16[2048,256]{1,0:T(8,128)(2,1)S(1)} %collective-permute-done.8.rest_3_), channel_id=1, source_target_pairs={{0,1},{1,0},{2,3},{3,2},{4,5},{5,4},{6,7},{7,6},{8,9},{9,8},{10,11... | collective-permute-start | bytes 3145736 | tf_op jit(solution)/shard_map/ppermute | solution.py:27
  56.3 10.2 %collective-permute-start.13 = (bf16[2048,256]{1,0:T(8,128)(2,1)S(1)}, bf16[2048,256]{1,0:T(8,128)(2,1)S(1)}, u32[]{:S(2)}, u32[]{:S(2)}) collective-permute-start(bf16[2048,256]{1,0:T(8,128)(2,1)S(1)} %collective-permute-done.9.rest_4_), channel_id=1, source_target_pairs={{0,1},{1,0},{2,3},{3,2},{4,5},{5,4},{6,7},{7,6},{8,9},{9,8},{10,11... | collective-permute-start | bytes 3145736 | tf_op jit(solution)/shard_map/ppermute | solution.py:27
  58.5 11.2 %copy-start.1 = (bf16[1,64,128,128]{3,2,1,0:T(8,128)(2,1)S(1)}, bf16[1,64,128,128]{3,2,1,0:T(8,128)(2,1)}, u32[]{:S(2)}) copy-start(bf16[1,64,128,128]{3,2,1,0:T(8,128)(2,1)} %param.5) | copy-start | bytes 6291460
  68.9 5.1 %collective-permute-start.15 = (f32[128,256]{1,0:T(8,128)S(1)}, f32[128,256]{1,0:T(8,128)S(1)}, u32[]{:S(2)}, u32[]{:S(2)}) collective-permute-start(f32[128,256]{1,0:T(8,128)S(1)} %shard_map.48), channel_id=1, source_target_pairs={{0,16},{1,17},{2,18},{3,19},{4,20},{5,21},{6,22},{7,23},{8,24},{9,... | collective-permute-start | bytes 393224 | tf_op jit(solution)/shard_map/ppermute | solution.py:27

commit v4 on v3

--- a/solution.py
+++ b/solution.py
@@ -13,8 +13,6 @@
 WIDTH = 256
 TILES = 64
 PLANE = 16
-BUFFERS = 8
-AHEAD = 14
 BATCH = 16
 
 
@@ -43,8 +41,12 @@
     return move(a, lambda x, y, z, c: (x, y, z, 1 - c))
 
 
-def from_pair(a):
-    return move(a, lambda x, y, z, c: (x, y, z ^ 1, c))
+def from_lender(a):
+    return move(a, lambda x, y, z, c: (x, y, z + 1 - 2 * c, c))
+
+
+def from_borrower(a):
+    return move(a, lambda x, y, z, c: (x, y, z - 1 + 2 * c, c))
 
 
 def places(columns):
@@ -56,7 +58,9 @@
     dy = (((columns >> 7) * 2 + ((columns >> 1) & 1)) - y) & 3
     middle = jnp.where(at == 0, dy, dx)
     last = jnp.where(at == 0, dx, dy)
-    place = ((at ^ core) * 4 + last) * PLANE + middle * 4 + dz
+    inner = middle * 4 + dz
+    buffer = jnp.where(last == 0, 0, last * 2 - 1 + (inner >> 3))
+    place = ((at ^ core) * 7 + buffer) * PLANE + inner
     return jnp.where(((columns >> 4) & 1) == zl, place, -1)
 
 
@@ -65,7 +69,7 @@
 
         def step(k, n):
             place = place_ref[r, k]
-            list_ref[r, n] = (k << 7) + (place & 127)
+            list_ref[r, n] = (k << 8) + (place & 255)
             return jnp.where(place >= 0, n + 1, n)
 
         list_ref[r, TILES] = lax.fori_loop(0, TILES, step, 0)
@@ -86,13 +90,11 @@
     return pl.ds(pl.multiple_of(index << 7, SIDE), SIDE)
 
 
-def multiply(row, lists, parts, buffers):
+def multiply(row, lists, tiles, buffers):
     vmem = pl.BlockSpec(memory_space=pltpu.VMEM)
-    smem = pl.BlockSpec(memory_space=pltpu.SMEM)
-    split = AHEAD
 
-    def kernel(list_ref, *rest):
-        part_refs, held, out_ref = rest[: len(parts)], rest[len(parts) : -1], rest[-1]
+    def kernel(list_ref, tiles_ref, *rest):
+        held, out_ref = rest[:-1], rest[-1]
         out_ref[...] = jnp.zeros_like(out_ref)
         n = list_ref[row, TILES]
 
@@ -102,28 +104,25 @@
             for j in range(BATCH):
                 at = i * BATCH + j
                 code = list_ref[row, jnp.minimum(at, n - 1)]
-                k = code >> 7
-                if len(parts) == 1:
-                    tile = part_refs[0][rows(k), :]
-                else:
-                    tile = part_refs[0][rows(jnp.minimum(k, split - 1)), :]
-                    tile = jnp.where(k < split, tile, part_refs[1][rows(jnp.maximum(k - split, 0)), :])
+                tile = tiles_ref[rows(code >> 8), :]
                 left.append(jnp.where(at < n, tile, jnp.zeros_like(tile)))
                 here = rows(code & 15)
-                buffer = (code >> 4) & 7
-                block = held[0][here, :]
-                for b in range(1, BUFFERS):
-                    block = jnp.where(buffer == b, held[b][here, :], block)
+                buffer = (code >> 4) & 15
+                block = None
+                for b, ref in enumerate(held):
+                    within = here if ref.shape[0] == PLANE * SIDE else rows(code & 7)
+                    found = ref[within, :]
+                    block = found if block is None else jnp.where(buffer == b, found, block)
                 right.append(block)
             out_ref[...] += jnp.dot(
                 jnp.concatenate(left, axis=1), jnp.concatenate(right, axis=0), preferred_element_type=jnp.float32
             )
 
-    held = [pltpu.with_memory_space_constraint(a, pltpu.VMEM) for a in (*parts, *buffers)]
+    held = [pltpu.with_memory_space_constraint(a, pltpu.VMEM) for a in (tiles, *buffers)]
     return pl.pallas_call(
         kernel,
         out_shape=jax.ShapeDtypeStruct((SIDE, WIDTH), jnp.float32),
-        in_specs=[smem] + [vmem] * len(held),
+        in_specs=[pl.BlockSpec(memory_space=pltpu.SMEM)] + [vmem] * len(held),
         out_specs=vmem,
         compiler_params=pltpu.CompilerParams(vmem_limit_bytes=16 * 1024 * 1024),
         cost_estimate=pl.CostEstimate(flops=32 * 2 * SIDE * SIDE * WIDTH, bytes_accessed=3 << 20, transcendentals=0),
@@ -136,21 +135,26 @@
 
 def on_device(features, tiles, columns, weight):
     mine = tiles.reshape(TILES * SIDE, SIDE)
-    place = places(jnp.concatenate([columns, from_pair(columns)], axis=0))
+    place = places(jnp.concatenate([columns, from_lender(columns)], axis=0))
     lines = [features] + [from_line(features, d) for d in (1, 2, 3)]
     lines[1], sent = together(lines[1], mine)
     line = jnp.concatenate(lines, axis=0)
     line, place = together(line, place)
-    paired = from_pair(sent)
+    lent = from_lender(sent)
     plane = jnp.concatenate([line] + [from_middle(line, d) for d in (1, 2, 3)], axis=0)
     plane, place = together(plane, place)
     lists = listed(place)
-    buffers = [plane] + [from_last(plane, d) for d in (1, 2, 3)]
+    half = PLANE // 2 * SIDE
+    low, high = plane[:half], plane[half:]
+    after_low, before_high = from_last(low, 1), from_last(high, -1)
+    after_low, before_high, lists = together(after_low, before_high, lists)
+    after_high, before_low = from_last(high, 1), from_last(low, -1)
+    buffers = [plane, after_low, after_high, from_last(after_low, 1), from_last(before_high, -1), before_low, before_high]
     buffers += [from_core(a) for a in buffers]
-    paired = together(paired)[0]
-    across = from_pair(multiply(1, lists, [paired], buffers))
-    here = multiply(0, lists, [mine], buffers)
-    aggregated = (here + across).astype(jnp.bfloat16)
+    lent = together(lent)[0]
+    back = from_borrower(multiply(1, lists, lent, buffers))
+    here = multiply(0, lists, mine, buffers)
+    aggregated = (here + back).astype(jnp.bfloat16)
     product = jnp.dot(aggregated, weight, preferred_element_type=jnp.float32)
     return jnp.maximum(product, 0.0).astype(jnp.bfloat16)
 

time: 74.9 us -> 70.2 us (0.937)
  the two profiles are of different devices: /device:TPU:10 before, /device:TPU:1 now
where the time goes in v4:
time: 70.2 us; the launch traced here: 69.8 us
  starting transfers between devices  40.5 us (58%)
  waiting for transfers between devices  18.9 us (27%)
  Pallas kernels  7.74 us (11%)
  other arithmetic  1.6 us (2%)
  matrix products  0.8 us (1%)
    ppermute x22, starting transfers between devices, move(): return lax.ppermute(a, AXES, found)  40.5 us
    ppermute x22, waiting for transfers between devices, move(): return lax.ppermute(a, AXES, found)  18.9 us
    pallas_call x2, Pallas kernels, multiply(): pl.pallas_call(kernel, out_shape=jax.ShapeDtypeStruct((SIDE, WIDTH), jnp....  5.51 us
    pallas_call x1, Pallas kernels, listed(): pl.pallas_call(list_kernel, out_shape=jax.ShapeDtypeStruct((2, TILES + 1)...  2.22 us
  transfers between devices with their start and end apart: 22, of which 14 were waited for; matrix products, arithmetic and copies ran while one was open for 1% of the time, Pallas kernels for 7%

profile of v4, /device:TPU:1, one launch (start us, length us, event | category | flops | bytes accessed | tf_op | source)
XLA Modules:
  0.0 69.8 jit_solution(9644636805922609654)
XLA Ops:
  0.0 6.8 %collective-permute-start = (bf16[128,256]{1,0:T(8,128)(2,1)}, bf16[128,256]{1,0:T(8,128)(2,1)S(1)}, u32[]{:S(2)}, u32[]{:S(2)}) collective-permute-start(bf16[128,256]{1,0:T(8,128)(2,1)} %param.4), channel_id=1, source_target_pairs={{0,96},{1,97},{2,98},{3,99},{4,100},{5,101},{6,102},{7,103},{8,104... | collective-permute-start | bytes 196616 | tf_op jit(solution)/shard_map/ppermute | solution.py:25
  6.9 1.0 %collective-permute-start.1 = (bf16[128,256]{1,0:T(8,128)(2,1)}, bf16[128,256]{1,0:T(8,128)(2,1)S(1)}, u32[]{:S(2)}, u32[]{:S(2)}) collective-permute-start(bf16[128,256]{1,0:T(8,128)(2,1)} %param.4), channel_id=1, source_target_pairs={{0,64},{1,65},{2,66},{3,67},{4,68},{5,69},{6,70},{7,71},{8,72},{9,... | collective-permute-start | bytes 196616 | tf_op jit(solution)/shard_map/ppermute | solution.py:25
  7.8 2.3 %collective-permute-start.2 = (bf16[128,256]{1,0:T(8,128)(2,1)}, bf16[128,256]{1,0:T(8,128)(2,1)S(1)}, u32[]{:S(2)}, u32[]{:S(2)}) collective-permute-start(bf16[128,256]{1,0:T(8,128)(2,1)} %param.4), channel_id=1, source_target_pairs={{0,32},{1,33},{2,34},{3,35},{4,36},{5,37},{6,38},{7,39},{8,40},{9,... | collective-permute-start | bytes 196616 | tf_op jit(solution)/shard_map/ppermute | solution.py:25
  10.1 1.0 %collective-permute-start.3 = (s32[1,64]{1,0:T(1,128)}, s32[1,64]{1,0:T(1,128)S(1)}, u32[]{:S(2)}, u32[]{:S(2)}) collective-permute-start(s32[1,64]{1,0:T(1,128)} %param.6), channel_id=1, source_target_pairs={{0,16},{1,113},{2,18},{3,115},{4,20},{5,117},{6,22},{7,119},{8,24}... | collective-permute-start | bytes 776 | tf_op jit(solution)/shard_map/ppermute | solution.py:25
  11.1 1.5 %collective-permute-done.3 = s32[1,64]{1,0:T(1,128)S(1)} collective-permute-done((s32[1,64]{1,0:T(1,128)}, s32[1,64]{1,0:T(1,128)S(1)}, u32[]{:S(2)}, u32[]{:S(2)}) %collective-permute-start.3) | collective-permute-done | bytes 288 | tf_op jit(solution)/shard_map/ppermute | solution.py:25
  12.7 0.7 compare_select_fusion.1.place_ref
  13.4 0.0 collective-permute-done
  13.4 0.9 %collective-permute-done.1 = bf16[128,256]{1,0:T(8,128)(2,1)S(1)} collective-permute-done((bf16[128,256]{1,0:T(8,128)(2,1)}, bf16[128,256]{1,0:T(8,128)(2,1)S(1)}, u32[]{:S(2)}, u32[]{:S(2)}) %collective-permute-start.1) | collective-permute-done | bytes 65568 | tf_op jit(solution)/shard_map/ppermute | solution.py:25
  14.3 0.6 collective-permute-done.2
  14.9 0.9 %pad_maximum_fusion.1 = bf16[512,256]{1,0:T(8,128)(2,1)S(1)} fusion(bf16[128,256]{1,0:T(8,128)(2,1)S(1)} %collective-permute-done.2, bf16[128,256]{1,0:T(8,128)(2,1)S(1)} %collective-permute-done.1, bf16[128,256]{1,0:T(8,128)(2,1)S(1)} %collective-permute-done, bf16[128,256]{1,0:T(8,128)(2,1)} %param.4), kind=kLoop, calls=%fused_computation.3 | loop fusion | flops 1048576 | bytes 524288 | tf_op jit(solution)/shard_map/concatenate | solution.py:141
  15.8 2.6 %collective-permute-start.4 = (bf16[512,256]{1,0:T(8,128)(2,1)S(1)}, bf16[512,256]{1,0:T(8,128)(2,1)S(1)}, u32[]{:S(2)}, u32[]{:S(2)}) collective-permute-start(bf16[512,256]{1,0:T(8,128)(2,1)S(1)} %pad_maximum_fusion.1), channel_id=1, source_target_pairs={{0,130},{1,13},{2,0},{3,15},{4,134},{5,1},{6,4},{7,3},{8,138},{9,5... | collective-permute-start | bytes 786440 | tf_op jit(solution)/shard_map/ppermute | solution.py:25
  18.3 0.5 collective-permute-start.5
  18.9 0.6 collective-permute-start.6
  19.5 3.6 %collective-permute-start.20 = (bf16[8192,128]{1,0:T(8,128)(2,1)}, bf16[8192,128]{1,0:T(8,128)(2,1)S(1)}, u32[]{:S(2)}, u32[]{:S(2)}) collective-permute-start(bf16[8192,128]{1,0:T(8,128)(2,1)} %bitcast.2), channel_id=1, source_target_pairs={{0,16},{1,113},{2,18},{3,115},{4,20},{5,117},{6,22},{7,119},{8,24}... | collective-permute-start | bytes 6291464 | tf_op jit(solution)/shard_map/ppermute | solution.py:25
  23.1 1.4 %collective-permute-done.4 = bf16[512,256]{1,0:T(8,128)(2,1)S(1)} collective-permute-done((bf16[512,256]{1,0:T(8,128)(2,1)S(1)}, bf16[512,256]{1,0:T(8,128)(2,1)S(1)}, u32[]{:S(2)}, u32[]{:S(2)}) %collective-permute-start.4) | collective-permute-done | bytes 262176 | tf_op jit(solution)/shard_map/ppermute | solution.py:25
  24.5 0.7 %collective-permute-done.5 = bf16[512,256]{1,0:T(8,128)(2,1)S(1)} collective-permute-done((bf16[512,256]{1,0:T(8,128)(2,1)S(1)}, bf16[512,256]{1,0:T(8,128)(2,1)S(1)}, u32[]{:S(2)}, u32[]{:S(2)}) %collective-permute-start.5) | collective-permute-done | bytes 262176 | tf_op jit(solution)/shard_map/ppermute | solution.py:25
  25.2 3.0 %collective-permute-done.6 = bf16[512,256]{1,0:T(8,128)(2,1)S(1)} collective-permute-done((bf16[512,256]{1,0:T(8,128)(2,1)S(1)}, bf16[512,256]{1,0:T(8,128)(2,1)S(1)}, u32[]{:S(2)}, u32[]{:S(2)}) %collective-permute-start.6) | collective-permute-done | bytes 262176 | tf_op jit(solution)/shard_map/ppermute | solution.py:25
  28.2 0.1 pad_maximum_fusion.rest_0_
  28.2 0.1 fusion.4
  28.3 2.8 %collective-permute-start.7 = (bf16[1024,256]{1,0:T(8,128)(2,1)S(1)}, bf16[1024,256]{1,0:T(8,128)(2,1)S(1)}, u32[]{:S(2)}, u32[]{:S(2)}) collective-permute-start(bf16[1024,256]{1,0:T(8,128)(2,1)S(1)} %get-tuple-element.24), channel_id=1, source_target_pairs={{0,12},{1,131},{2,14},{3,1},{4,0},{5,135},{6,2},{7,5},{8,4},{9,139... | collective-permute-start | bytes 1572872 | tf_op jit(solution)/shard_map/ppermute | solution.py:25
  31.1 2.7 %collective-permute-start.9 = (bf16[1024,256]{1,0:T(8,128)(2,1)S(1)}, bf16[1024,256]{1,0:T(8,128)(2,1)S(1)}, u32[]{:S(2)}, u32[]{:S(2)}) collective-permute-start(bf16[1024,256]{1,0:T(8,128)(2,1)S(1)} %get-tuple-element.23), channel_id=1, source_target_pairs={{0,12},{1,131},{2,14},{3,1},{4,0},{5,135},{6,2},{7,5},{8,4},{9,139... | collective-permute-start | bytes 1572872 | tf_op jit(solution)/shard_map/ppermute | solution.py:25
  33.8 0.0 collective-permute-start.12
  33.8 2.2 %shard_map.46.list_ref = s32[2,65]{1,0:T(2,128)S(1)} custom-call(s32[2,64]{1,0:T(2,128)S(1)} %compare_select_fusion.1.place_ref), custom_call_target="tpu_custom_call" | custom-call | tf_op jit(solution)/shard_map/pallas_call | solution.py:80
  36.0 0.0 copy-start.1
  36.1 1.2 %collective-permute-done.7.rest_1_ = bf16[1024,256]{1,0:T(8,128)(2,1)S(1)} collective-permute-done((bf16[1024,256]{1,0:T(8,128)(2,1)S(1)}, bf16[1024,256]{1,0:T(8,128)(2,1)S(1)}, u32[]{:S(2)}, u32[]{:S(2)}) %collective-permute-start.7) | collective-permute-done | bytes 524320 | tf_op jit(solution)/shard_map/ppermute | solution.py:25
  37.3 3.4 %collective-permute-done.8.rest_6_ = bf16[1024,256]{1,0:T(8,128)(2,1)S(1)} collective-permute-done((bf16[1024,256]{1,0:T(8,128)(2,1)S(1)}, bf16[1024,256]{1,0:T(8,128)(2,1)S(1)}, u32[]{:S(2)}, u32[]{:S(2)}) %collective-permute-start.8) | collective-permute-done | bytes 524320 | tf_op jit(solution)/shard_map/ppermute | solution.py:25
  40.7 0.0 collective-permute-start.10
  40.7 1.5 %collective-permute-start.11 = (bf16[1024,256]{1,0:T(8,128)(2,1)S(1)}, bf16[1024,256]{1,0:T(8,128)(2,1)S(1)}, u32[]{:S(2)}, u32[]{:S(2)}) collective-permute-start(bf16[1024,256]{1,0:T(8,128)(2,1)S(1)} %collective-permute-done.8.rest_6_), channel_id=1, source_target_pairs={{0,4},{1,3},{2,6},{3,129},{4,8},{5,7},{6,10},{7,133},{8,12},{9,11}... | collective-permute-start | bytes 1572872 | tf_op jit(solution)/shard_map/ppermute | solution.py:25
  42.1 0.7 %collective-permute-done.9.rest_2_ = bf16[1024,256]{1,0:T(8,128)(2,1)S(1)} collective-permute-done((bf16[1024,256]{1,0:T(8,128)(2,1)S(1)}, bf16[1024,256]{1,0:T(8,128)(2,1)S(1)}, u32[]{:S(2)}, u32[]{:S(2)}) %collective-permute-start.9) | collective-permute-done | bytes 524320 | tf_op jit(solution)/shard_map/ppermute | solution.py:25
  42.9 4.8 %collective-permute-start.14 = (bf16[1024,256]{1,0:T(8,128)(2,1)S(1)}, bf16[1024,256]{1,0:T(8,128)(2,1)S(1)}, u32[]{:S(2)}, u32[]{:S(2)}) collective-permute-start(bf16[1024,256]{1,0:T(8,128)(2,1)S(1)} %collective-permute-done.7.rest_1_), channel_id=1, source_target_pairs={{0,1},{1,0},{2,3},{3,2},{4,5},{5,4},{6,7},{7,6},{8,9},{9,8},{10,11... | collective-permute-start | bytes 1572872 | tf_op jit(solution)/shard_map/ppermute | solution.py:25
  47.7 0.0 collective-permute-done.12.rest_5_
  47.7 3.6 %collective-permute-start.19 = (bf16[1024,256]{1,0:T(8,128)(2,1)S(1)}, bf16[1024,256]{1,0:T(8,128)(2,1)S(1)}, u32[]{:S(2)}, u32[]{:S(2)}) collective-permute-start(bf16[1024,256]{1,0:T(8,128)(2,1)S(1)} %collective-permute-done.8.rest_6_), channel_id=1, source_target_pairs={{0,1},{1,0},{2,3},{3,2},{4,5},{5,4},{6,7},{7,6},{8,9},{9,8},{10,11... | collective-permute-start | bytes 1572872 | tf_op jit(solution)/shard_map/ppermute | solution.py:25
  51.2 3.6 %collective-permute-start.13 = (bf16[2048,256]{1,0:T(8,128)(2,1)S(1)}, bf16[2048,256]{1,0:T(8,128)(2,1)S(1)}, u32[]{:S(2)}, u32[]{:S(2)}) collective-permute-start(bf16[2048,256]{1,0:T(8,128)(2,1)S(1)} %pad_maximum_fusion.rest_0_), channel_id=1, source_target_pairs={{0,1},{1,0},{2,3},{3,2},{4,5},{5,4},{6,7},{7,6},{8,9},{9,8},{10,11... | collective-permute-start | bytes 3145736 | tf_op jit(solution)/shard_map/ppermute | solution.py:25
  54.8 2.1 %collective-permute-start.15 = (bf16[1024,256]{1,0:T(8,128)(2,1)S(1)}, bf16[1024,256]{1,0:T(8,128)(2,1)S(1)}, u32[]{:S(2)}, u32[]{:S(2)}) collective-permute-start(bf16[1024,256]{1,0:T(8,128)(2,1)S(1)} %collective-permute-done.9.rest_2_), channel_id=1, source_target_pairs={{0,1},{1,0},{2,3},{3,2},{4,5},{5,4},{6,7},{7,6},{8,9},{9,8},{10,11... | collective-permute-start | bytes 1572872 | tf_op jit(solution)/shard_map/ppermute | solution.py:25
  56.9 0.0 collective-permute-done.14.rest_8_
  56.9 0.0 collective-permute-start.18
  56.9 0.0 collective-permute-done.19.rest_13_
  56.9 0.5 collective-permute-start.16
  57.4 0.1 collective-permute-start.17
  57.5 0.9 %collective-permute-done.15.rest_9_ = bf16[1024,256]{1,0:T(8,128)(2,1)S(1)} collective-permute-done((bf16[1024,256]{1,0:T(8,128)(2,1)S(1)}, bf16[1024,256]{1,0:T(8,128)(2,1)S(1)}, u32[]{:S(2)}, u32[]{:S(2)}) %collective-permute-start.15) | collective-permute-done | bytes 524320 | tf_op jit(solution)/shard_map/ppermute | solution.py:25
  58.4 0.7 %collective-permute-done.18.rest_12_ = bf16[1024,256]{1,0:T(8,128)(2,1)S(1)} collective-permute-done((bf16[1024,256]{1,0:T(8,128)(2,1)S(1)}, bf16[1024,256]{1,0:T(8,128)(2,1)S(1)}, u32[]{:S(2)}, u32[]{:S(2)}) %collective-permute-start.18) | collective-permute-done | bytes 524320 | tf_op jit(solution)/shard_map/ppermute | solution.py:25
  59.1 0.7 %collective-permute-done.16.rest_10_ = bf16[1024,256]{1,0:T(8,128)(2,1)S(1)} collective-permute-done((bf16[1024,256]{1,0:T(8,128)(2,1)S(1)}, bf16[1024,256]{1,0:T(8,128)(2,1)S(1)}, u32[]{:S(2)}, u32[]{:S(2)}) %collective-permute-start.16) | collective-permute-done | bytes 524320 | tf_op jit(solution)/shard_map/ppermute | solution.py:25
  59.9 0.7 %collective-permute-done.17.rest_11_ = bf16[1024,256]{1,0:T(8,128)(2,1)S(1)} collective-permute-done((bf16[1024,256]{1,0:T(8,128)(2,1)S(1)}, bf16[1024,256]{1,0:T(8,128)(2,1)S(1)}, u32[]{:S(2)}, u32[]{:S(2)}) %collective-permute-start.17) | collective-permute-done | bytes 524320 | tf_op jit(solution)/shard_map/ppermute | solution.py:25
  60.6 2.8 %shard_map.48 = f32[128,256]{1,0:T(8,128)S(1)} custom-call(s32[2,65]{1,0:T(2,128)S(1)} %shard_map.46.list_ref, bf16[8192,128]{1,0:T(8,128)(2,1)S(1)} %collective-permute-done.20.tiles_ref, bf16[2048,256]{1,0:T(8,128)(2,1)S(1)} %pad_maximum_fusion.rest_0_, bf16[1024,256]{1,0:T(8,128)(2,1)S(1)} %collective-permute-done.7.rest_1_, ...), custom_call_target="tpu_custom_call" | custom-call | flops 268435456 | bytes 3145728 | tf_op jit(solution)/shard_map/pallas_call | solution.py:122
  63.4 0.6 collective-permute-start.21
  64.0 2.7 %shard_map.47 = f32[128,256]{1,0:T(8,128)S(1)} custom-call(s32[2,65]{1,0:T(2,128)S(1)} %shard_map.46.list_ref, bf16[8192,128]{1,0:T(8,128)(2,1)S(1)} %bitcast.3, bf16[2048,256]{1,0:T(8,128)(2,1)S(1)} %pad_maximum_fusion.rest_0_, bf16[1024,256]{1,0:T(8,128)(2,1)S(1)} %collective-permute-done.7.rest_1_, bf16[1024,256]{1,0:T(8,128)(2,1)S(1)} %collective-permute-done.9.rest_2_, ...), custom_call_target="tpu_custom_call" | custom-call | flops 268435456 | bytes 3145728 | tf_op jit(solution)/shard_map/pallas_call | solution.py:122
  66.7 2.2 %collective-permute-done.21 = f32[128,256]{1,0:T(8,128)S(1)} collective-permute-done((f32[128,256]{1,0:T(8,128)S(1)}, f32[128,256]{1,0:T(8,128)S(1)}, u32[]{:S(2)}, u32[]{:S(2)}) %collective-permute-start.21) | collective-permute-done | bytes 131104 | tf_op jit(solution)/shard_map/ppermute | solution.py:25
  69.0 0.8 %fusion = bf16[128,256]{1,0:T(8,128)(2,1)} fusion(bf16[256,256]{1,0:T(8,128)(2,1)S(1)} %copy-done, f32[128,256]{1,0:T(8,128)S(1)} %shard_map.47, f32[128,256]{1,0:T(8,128)S(1)} %collective-permute-done.21), kind=kOutput, calls=%fused_computation.1 | convolution fusion | flops 16908288 | bytes 458752 | tf_op jit(solution)/shard_map/dot_general | solution.py:158
  (8 shorter events, 0.0 us)
Async XLA Ops:
  0.0 69.0 %copy-start = (bf16[256,256]{1,0:T(8,128)(2,1)S(1)}, bf16[256,256]{1,0:T(8,128)(2,1)}, u32[]{:S(2)}) copy-start(bf16[256,256]{1,0:T(8,128)(2,1)} %param.7) | copy-start | bytes 393220
  0.0 13.4 %collective-permute-start = (bf16[128,256]{1,0:T(8,128)(2,1)}, bf16[128,256]{1,0:T(8,128)(2,1)S(1)}, u32[]{:S(2)}, u32[]{:S(2)}) collective-permute-start(bf16[128,256]{1,0:T(8,128)(2,1)} %param.4), channel_id=1, source_target_pairs={{0,96},{1,97},{2,98},{3,99},{4,100},{5,101},{6,102},{7,103},{8,104... | collective-permute-start | bytes 196616 | tf_op jit(solution)/shard_map/ppermute | solution.py:25
  6.9 7.4 %collective-permute-start.1 = (bf16[128,256]{1,0:T(8,128)(2,1)}, bf16[128,256]{1,0:T(8,128)(2,1)S(1)}, u32[]{:S(2)}, u32[]{:S(2)}) collective-permute-start(bf16[128,256]{1,0:T(8,128)(2,1)} %param.4), channel_id=1, source_target_pairs={{0,64},{1,65},{2,66},{3,67},{4,68},{5,69},{6,70},{7,71},{8,72},{9,... | collective-permute-start | bytes 196616 | tf_op jit(solution)/shard_map/ppermute | solution.py:25
  7.8 7.1 %collective-permute-start.2 = (bf16[128,256]{1,0:T(8,128)(2,1)}, bf16[128,256]{1,0:T(8,128)(2,1)S(1)}, u32[]{:S(2)}, u32[]{:S(2)}) collective-permute-start(bf16[128,256]{1,0:T(8,128)(2,1)} %param.4), channel_id=1, source_target_pairs={{0,32},{1,33},{2,34},{3,35},{4,36},{5,37},{6,38},{7,39},{8,40},{9,... | collective-permute-start | bytes 196616 | tf_op jit(solution)/shard_map/ppermute | solution.py:25
  10.1 2.6 %collective-permute-start.3 = (s32[1,64]{1,0:T(1,128)}, s32[1,64]{1,0:T(1,128)S(1)}, u32[]{:S(2)}, u32[]{:S(2)}) collective-permute-start(s32[1,64]{1,0:T(1,128)} %param.6), channel_id=1, source_target_pairs={{0,16},{1,113},{2,18},{3,115},{4,20},{5,117},{6,22},{7,119},{8,24}... | collective-permute-start | bytes 776 | tf_op jit(solution)/shard_map/ppermute | solution.py:25
  15.8 8.7 %collective-permute-start.4 = (bf16[512,256]{1,0:T(8,128)(2,1)S(1)}, bf16[512,256]{1,0:T(8,128)(2,1)S(1)}, u32[]{:S(2)}, u32[]{:S(2)}) collective-permute-start(bf16[512,256]{1,0:T(8,128)(2,1)S(1)} %pad_maximum_fusion.1), channel_id=1, source_target_pairs={{0,130},{1,13},{2,0},{3,15},{4,134},{5,1},{6,4},{7,3},{8,138},{9,5... | collective-permute-start | bytes 786440 | tf_op jit(solution)/shard_map/ppermute | solution.py:25
  18.3 6.8 %collective-permute-start.5 = (bf16[512,256]{1,0:T(8,128)(2,1)S(1)}, bf16[512,256]{1,0:T(8,128)(2,1)S(1)}, u32[]{:S(2)}, u32[]{:S(2)}) collective-permute-start(bf16[512,256]{1,0:T(8,128)(2,1)S(1)} %pad_maximum_fusion.1), channel_id=1, source_target_pairs={{0,128},{1,9},{2,130},{3,11},{4,132},{5,13},{6,134},{7,15},{8,136}... | collective-permute-start | bytes 786440 | tf_op jit(solution)/shard_map/ppermute | solution.py:25
  18.9 9.3 %collective-permute-start.6 = (bf16[512,256]{1,0:T(8,128)(2,1)S(1)}, bf16[512,256]{1,0:T(8,128)(2,1)S(1)}, u32[]{:S(2)}, u32[]{:S(2)}) collective-permute-start(bf16[512,256]{1,0:T(8,128)(2,1)S(1)} %pad_maximum_fusion.1), channel_id=1, source_target_pairs={{0,2},{1,5},{2,128},{3,7},{4,6},{5,9},{6,132},{7,11},{8,10},{9,13}... | collective-permute-start | bytes 786440 | tf_op jit(solution)/shard_map/ppermute | solution.py:25
  19.5 37.9 %collective-permute-start.20 = (bf16[8192,128]{1,0:T(8,128)(2,1)}, bf16[8192,128]{1,0:T(8,128)(2,1)S(1)}, u32[]{:S(2)}, u32[]{:S(2)}) collective-permute-start(bf16[8192,128]{1,0:T(8,128)(2,1)} %bitcast.2), channel_id=1, source_target_pairs={{0,16},{1,113},{2,18},{3,115},{4,20},{5,117},{6,22},{7,119},{8,24}... | collective-permute-start | bytes 6291464 | tf_op jit(solution)/shard_map/ppermute | solution.py:25
  28.3 8.9 %collective-permute-start.7 = (bf16[1024,256]{1,0:T(8,128)(2,1)S(1)}, bf16[1024,256]{1,0:T(8,128)(2,1)S(1)}, u32[]{:S(2)}, u32[]{:S(2)}) collective-permute-start(bf16[1024,256]{1,0:T(8,128)(2,1)S(1)} %get-tuple-element.24), channel_id=1, source_target_pairs={{0,12},{1,131},{2,14},{3,1},{4,0},{5,135},{6,2},{7,5},{8,4},{9,139... | collective-permute-start | bytes 1572872 | tf_op jit(solution)/shard_map/ppermute | solution.py:25
  31.1 9.5 %collective-permute-start.8 = (bf16[1024,256]{1,0:T(8,128)(2,1)S(1)}, bf16[1024,256]{1,0:T(8,128)(2,1)S(1)}, u32[]{:S(2)}, u32[]{:S(2)}) collective-permute-start(bf16[1024,256]{1,0:T(8,128)(2,1)S(1)} %get-tuple-element.23), channel_id=1, source_target_pairs={{0,4},{1,3},{2,6},{3,129},{4,8},{5,7},{6,10},{7,133},{8,12},{9,11}... | collective-permute-start | bytes 1572872 | tf_op jit(solution)/shard_map/ppermute | solution.py:25
  31.1 11.7 %collective-permute-start.9 = (bf16[1024,256]{1,0:T(8,128)(2,1)S(1)}, bf16[1024,256]{1,0:T(8,128)(2,1)S(1)}, u32[]{:S(2)}, u32[]{:S(2)}) collective-permute-start(bf16[1024,256]{1,0:T(8,128)(2,1)S(1)} %get-tuple-element.23), channel_id=1, source_target_pairs={{0,12},{1,131},{2,14},{3,1},{4,0},{5,135},{6,2},{7,5},{8,4},{9,139... | collective-permute-start | bytes 1572872 | tf_op jit(solution)/shard_map/ppermute | solution.py:25
  33.8 13.9 %collective-permute-start.12 = (bf16[1024,256]{1,0:T(8,128)(2,1)S(1)}, bf16[1024,256]{1,0:T(8,128)(2,1)S(1)}, u32[]{:S(2)}, u32[]{:S(2)}) collective-permute-start(bf16[1024,256]{1,0:T(8,128)(2,1)S(1)} %get-tuple-element.24), channel_id=1, source_target_pairs={{0,4},{1,3},{2,6},{3,129},{4,8},{5,7},{6,10},{7,133},{8,12},{9,11}... | collective-permute-start | bytes 1572872 | tf_op jit(solution)/shard_map/ppermute | solution.py:25
  36.0 27.9 %copy-start.1 = (bf16[1,64,128,128]{3,2,1,0:T(8,128)(2,1)S(1)}, bf16[1,64,128,128]{3,2,1,0:T(8,128)(2,1)}, u32[]{:S(2)}) copy-start(bf16[1,64,128,128]{3,2,1,0:T(8,128)(2,1)} %param.5) | copy-start | bytes 6291460
  40.7 10.6 %collective-permute-start.10 = (bf16[1024,256]{1,0:T(8,128)(2,1)S(1)}, bf16[1024,256]{1,0:T(8,128)(2,1)S(1)}, u32[]{:S(2)}, u32[]{:S(2)}) collective-permute-start(bf16[1024,256]{1,0:T(8,128)(2,1)S(1)} %collective-permute-done.7.rest_1_), channel_id=1, source_target_pairs={{0,12},{1,131},{2,14},{3,1},{4,0},{5,135},{6,2},{7,5},{8,4},{9,139... | collective-permute-start | bytes 1572872 | tf_op jit(solution)/shard_map/ppermute | solution.py:25
  40.7 14.1 %collective-permute-start.11 = (bf16[1024,256]{1,0:T(8,128)(2,1)S(1)}, bf16[1024,256]{1,0:T(8,128)(2,1)S(1)}, u32[]{:S(2)}, u32[]{:S(2)}) collective-permute-start(bf16[1024,256]{1,0:T(8,128)(2,1)S(1)} %collective-permute-done.8.rest_6_), channel_id=1, source_target_pairs={{0,4},{1,3},{2,6},{3,129},{4,8},{5,7},{6,10},{7,133},{8,12},{9,11}... | collective-permute-start | bytes 1572872 | tf_op jit(solution)/shard_map/ppermute | solution.py:25
  42.9 14.0 %collective-permute-start.14 = (bf16[1024,256]{1,0:T(8,128)(2,1)S(1)}, bf16[1024,256]{1,0:T(8,128)(2,1)S(1)}, u32[]{:S(2)}, u32[]{:S(2)}) collective-permute-start(bf16[1024,256]{1,0:T(8,128)(2,1)S(1)} %collective-permute-done.7.rest_1_), channel_id=1, source_target_pairs={{0,1},{1,0},{2,3},{3,2},{4,5},{5,4},{6,7},{7,6},{8,9},{9,8},{10,11... | collective-permute-start | bytes 1572872 | tf_op jit(solution)/shard_map/ppermute | solution.py:25
  47.7 9.2 %collective-permute-start.19 = (bf16[1024,256]{1,0:T(8,128)(2,1)S(1)}, bf16[1024,256]{1,0:T(8,128)(2,1)S(1)}, u32[]{:S(2)}, u32[]{:S(2)}) collective-permute-start(bf16[1024,256]{1,0:T(8,128)(2,1)S(1)} %collective-permute-done.8.rest_6_), channel_id=1, source_target_pairs={{0,1},{1,0},{2,3},{3,2},{4,5},{5,4},{6,7},{7,6},{8,9},{9,8},{10,11... | collective-permute-start | bytes 1572872 | tf_op jit(solution)/shard_map/ppermute | solution.py:25
  51.2 7.9 %collective-permute-start.13 = (bf16[2048,256]{1,0:T(8,128)(2,1)S(1)}, bf16[2048,256]{1,0:T(8,128)(2,1)S(1)}, u32[]{:S(2)}, u32[]{:S(2)}) collective-permute-start(bf16[2048,256]{1,0:T(8,128)(2,1)S(1)} %pad_maximum_fusion.rest_0_), channel_id=1, source_target_pairs={{0,1},{1,0},{2,3},{3,2},{4,5},{5,4},{6,7},{7,6},{8,9},{9,8},{10,11... | collective-permute-start | bytes 3145736 | tf_op jit(solution)/shard_map/ppermute | solution.py:25
  54.8 3.6 %collective-permute-start.15 = (bf16[1024,256]{1,0:T(8,128)(2,1)S(1)}, bf16[1024,256]{1,0:T(8,128)(2,1)S(1)}, u32[]{:S(2)}, u32[]{:S(2)}) collective-permute-start(bf16[1024,256]{1,0:T(8,128)(2,1)S(1)} %collective-permute-done.9.rest_2_), channel_id=1, source_target_pairs={{0,1},{1,0},{2,3},{3,2},{4,5},{5,4},{6,7},{7,6},{8,9},{9,8},{10,11... | collective-permute-start | bytes 1572872 | tf_op jit(solution)/shard_map/ppermute | solution.py:25
  56.9 2.3 %collective-permute-start.18 = (bf16[1024,256]{1,0:T(8,128)(2,1)S(1)}, bf16[1024,256]{1,0:T(8,128)(2,1)S(1)}, u32[]{:S(2)}, u32[]{:S(2)}) collective-permute-start(bf16[1024,256]{1,0:T(8,128)(2,1)S(1)} %collective-permute-done.12.rest_5_), channel_id=1, source_target_pairs={{0,1},{1,0},{2,3},{3,2},{4,5},{5,4},{6,7},{7,6},{8,9},{9,8},{10,11... | collective-permute-start | bytes 1572872 | tf_op jit(solution)/shard_map/ppermute | solution.py:25
  56.9 3.0 %collective-permute-start.16 = (bf16[1024,256]{1,0:T(8,128)(2,1)S(1)}, bf16[1024,256]{1,0:T(8,128)(2,1)S(1)}, u32[]{:S(2)}, u32[]{:S(2)}) collective-permute-start(bf16[1024,256]{1,0:T(8,128)(2,1)S(1)} %collective-permute-done.10.rest_3_), channel_id=1, source_target_pairs={{0,1},{1,0},{2,3},{3,2},{4,5},{5,4},{6,7},{7,6},{8,9},{9,8},{10,11... | collective-permute-start | bytes 1572872 | tf_op jit(solution)/shard_map/ppermute | solution.py:25
  57.4 3.3 %collective-permute-start.17 = (bf16[1024,256]{1,0:T(8,128)(2,1)S(1)}, bf16[1024,256]{1,0:T(8,128)(2,1)S(1)}, u32[]{:S(2)}, u32[]{:S(2)}) collective-permute-start(bf16[1024,256]{1,0:T(8,128)(2,1)S(1)} %collective-permute-done.11.rest_4_), channel_id=1, source_target_pairs={{0,1},{1,0},{2,3},{3,2},{4,5},{5,4},{6,7},{7,6},{8,9},{9,8},{10,11... | collective-permute-start | bytes 1572872 | tf_op jit(solution)/shard_map/ppermute | solution.py:25
  63.4 5.5 %collective-permute-start.21 = (f32[128,256]{1,0:T(8,128)S(1)}, f32[128,256]{1,0:T(8,128)S(1)}, u32[]{:S(2)}, u32[]{:S(2)}) collective-permute-start(f32[128,256]{1,0:T(8,128)S(1)} %shard_map.48), channel_id=1, source_target_pairs={{0,112},{1,17},{2,114},{3,19},{4,116},{5,21},{6,118},{7,23},{8,120... | collective-permute-start | bytes 393224 | tf_op jit(solution)/shard_map/ppermute | solution.py:25

commit v5 on v4

--- a/solution.py
+++ b/solution.py
@@ -137,9 +137,8 @@
     mine = tiles.reshape(TILES * SIDE, SIDE)
     place = places(jnp.concatenate([columns, from_lender(columns)], axis=0))
     lines = [features] + [from_line(features, d) for d in (1, 2, 3)]
-    lines[1], sent = together(lines[1], mine)
     line = jnp.concatenate(lines, axis=0)
-    line, place = together(line, place)
+    line, place, sent = together(line, place, mine)
     lent = from_lender(sent)
     plane = jnp.concatenate([line] + [from_middle(line, d) for d in (1, 2, 3)], axis=0)
     plane, place = together(plane, place)
@@ -149,9 +148,9 @@
     after_low, before_high = from_last(low, 1), from_last(high, -1)
     after_low, before_high, lists = together(after_low, before_high, lists)
     after_high, before_low = from_last(high, 1), from_last(low, -1)
+    after_high, before_low, lent = together(after_high, before_low, lent)
     buffers = [plane, after_low, after_high, from_last(after_low, 1), from_last(before_high, -1), before_low, before_high]
     buffers += [from_core(a) for a in buffers]
-    lent = together(lent)[0]
     back = from_borrower(multiply(1, lists, lent, buffers))
     here = multiply(0, lists, mine, buffers)
     aggregated = (here + back).astype(jnp.bfloat16)

time: 70.2 us -> 67.2 us (0.957); the launches traced: 69.8 us -> 67.6 us
  starting transfers between devices: 40.5 us -> 36.6 us
  Pallas kernels: 7.74 us -> 9.95 us
    ppermute x22, starting transfers between devices: 40.5 us -> 36.6 us  [move(): return lax.ppermute(a, AXES, found)]
    pallas_call x2, Pallas kernels: 5.51 us -> 7.73 us  [multiply(): pl.pallas_call(kernel, out_shape=jax.ShapeDtypeStruct((SIDE, WIDTH), jnp....]
  transfers between devices with their start and end apart: 22 -> 22, of which waited for: 14 -> 11; matrix products, arithmetic and copies ran while one was open for 1% -> 1% of each run, Pallas kernels for 7% -> 9%
where the time goes in v5:
time: 67.2 us; the launch traced here: 67.6 us
  starting transfers between devices  36.6 us (54%)
  waiting for transfers between devices  18.4 us (27%)
  Pallas kernels  9.95 us (15%)
  other arithmetic  1.6 us (2%)
  matrix products  0.8 us (1%)
    ppermute x22, starting transfers between devices, move(): return lax.ppermute(a, AXES, found)  36.6 us
    ppermute x22, waiting for transfers between devices, move(): return lax.ppermute(a, AXES, found)  18.4 us
    pallas_call x2, Pallas kernels, multiply(): pl.pallas_call(kernel, out_shape=jax.ShapeDtypeStruct((SIDE, WIDTH), jnp....  7.73 us
    pallas_call x1, Pallas kernels, listed(): pl.pallas_call(list_kernel, out_shape=jax.ShapeDtypeStruct((2, TILES + 1)...  2.22 us
  transfers between devices with their start and end apart: 22, of which 11 were waited for; matrix products, arithmetic and copies ran while one was open for 1% of the time, Pallas kernels for 9%

profile of v5, /device:TPU:1, one launch (start us, length us, event | category | flops | bytes accessed | tf_op | source)
XLA Modules:
  0.0 67.6 jit_solution(7447436924763124608)
XLA Ops:
  0.0 7.7 %collective-permute-start.1 = (bf16[128,256]{1,0:T(8,128)(2,1)}, bf16[128,256]{1,0:T(8,128)(2,1)S(1)}, u32[]{:S(2)}, u32[]{:S(2)}) collective-permute-start(bf16[128,256]{1,0:T(8,128)(2,1)} %param.4), channel_id=1, source_target_pairs={{0,64},{1,65},{2,66},{3,67},{4,68},{5,69},{6,70},{7,71},{8,72},{9,... | collective-permute-start | bytes 196616 | tf_op jit(solution)/shard_map/ppermute | solution.py:25
  7.7 0.0 collective-permute-start
  7.7 2.4 %collective-permute-start.2 = (bf16[128,256]{1,0:T(8,128)(2,1)}, bf16[128,256]{1,0:T(8,128)(2,1)S(1)}, u32[]{:S(2)}, u32[]{:S(2)}) collective-permute-start(bf16[128,256]{1,0:T(8,128)(2,1)} %param.4), channel_id=1, source_target_pairs={{0,32},{1,33},{2,34},{3,35},{4,36},{5,37},{6,38},{7,39},{8,40},{9,... | collective-permute-start | bytes 196616 | tf_op jit(solution)/shard_map/ppermute | solution.py:25
  10.1 1.0 %collective-permute-start.3 = (s32[1,64]{1,0:T(1,128)}, s32[1,64]{1,0:T(1,128)S(1)}, u32[]{:S(2)}, u32[]{:S(2)}) collective-permute-start(s32[1,64]{1,0:T(1,128)} %param.6), channel_id=1, source_target_pairs={{0,16},{1,113},{2,18},{3,115},{4,20},{5,117},{6,22},{7,119},{8,24}... | collective-permute-start | bytes 776 | tf_op jit(solution)/shard_map/ppermute | solution.py:25
  11.1 1.6 %collective-permute-done.3 = s32[1,64]{1,0:T(1,128)S(1)} collective-permute-done((s32[1,64]{1,0:T(1,128)}, s32[1,64]{1,0:T(1,128)S(1)}, u32[]{:S(2)}, u32[]{:S(2)}) %collective-permute-start.3) | collective-permute-done | bytes 288 | tf_op jit(solution)/shard_map/ppermute | solution.py:25
  12.7 0.7 %compare_select_fusion.1.place_ref = s32[2,64]{1,0:T(2,128)S(1)} fusion(s32[1,64]{1,0:T(1,128)S(1)} %collective-permute-done.3, s32[1,64]{1,0:T(1,128)} %param.6, s32[]{:T(128)S(6)} %axis_index.77, s32[]{:T(128)S(6)} %add.23, s32[]{:T(128)S(6)} %axis_index.68, s32[]{:T(128)S(6)} %axis_index.65, s32[]{:T(128)S(6)} %axis_index.63), kind=kLoop, calls=%fused_computation.6 | loop fusion | flops 4736 | bytes 1044 | tf_op jit(solution)/shard_map/jit(_where)/select_n | solution.py:64
  13.4 1.9 %collective-permute-done = bf16[128,256]{1,0:T(8,128)(2,1)S(1)} collective-permute-done((bf16[128,256]{1,0:T(8,128)(2,1)}, bf16[128,256]{1,0:T(8,128)(2,1)S(1)}, u32[]{:S(2)}, u32[]{:S(2)}) %collective-permute-start) | collective-permute-done | bytes 65568 | tf_op jit(solution)/shard_map/ppermute | solution.py:25
  15.3 0.0 collective-permute-done.2
  15.3 0.9 %pad_maximum_fusion.1 = bf16[512,256]{1,0:T(8,128)(2,1)S(1)} fusion(bf16[128,256]{1,0:T(8,128)(2,1)S(1)} %collective-permute-done.2, bf16[128,256]{1,0:T(8,128)(2,1)S(1)} %collective-permute-done.1, bf16[128,256]{1,0:T(8,128)(2,1)S(1)} %collective-permute-done, bf16[128,256]{1,0:T(8,128)(2,1)} %param.4), kind=kLoop, calls=%fused_computation.3 | loop fusion | flops 1048576 | bytes 524288 | tf_op jit(solution)/shard_map/concatenate | solution.py:140
  16.2 1.3 %collective-permute-start.6 = (bf16[512,256]{1,0:T(8,128)(2,1)S(1)}, bf16[512,256]{1,0:T(8,128)(2,1)S(1)}, u32[]{:S(2)}, u32[]{:S(2)}) collective-permute-start(bf16[512,256]{1,0:T(8,128)(2,1)S(1)} %pad_maximum_fusion.1), channel_id=1, source_target_pairs={{0,2},{1,5},{2,128},{3,7},{4,6},{5,9},{6,132},{7,11},{8,10},{9,13}... | collective-permute-start | bytes 786440 | tf_op jit(solution)/shard_map/ppermute | solution.py:25
  17.5 2.5 %collective-permute-start.5 = (bf16[512,256]{1,0:T(8,128)(2,1)S(1)}, bf16[512,256]{1,0:T(8,128)(2,1)S(1)}, u32[]{:S(2)}, u32[]{:S(2)}) collective-permute-start(bf16[512,256]{1,0:T(8,128)(2,1)S(1)} %pad_maximum_fusion.1), channel_id=1, source_target_pairs={{0,128},{1,9},{2,130},{3,11},{4,132},{5,13},{6,134},{7,15},{8,136}... | collective-permute-start | bytes 786440 | tf_op jit(solution)/shard_map/ppermute | solution.py:25
  19.9 1.2 %collective-permute-start.4 = (bf16[512,256]{1,0:T(8,128)(2,1)S(1)}, bf16[512,256]{1,0:T(8,128)(2,1)S(1)}, u32[]{:S(2)}, u32[]{:S(2)}) collective-permute-start(bf16[512,256]{1,0:T(8,128)(2,1)S(1)} %pad_maximum_fusion.1), channel_id=1, source_target_pairs={{0,130},{1,13},{2,0},{3,15},{4,134},{5,1},{6,4},{7,3},{8,138},{9,5... | collective-permute-start | bytes 786440 | tf_op jit(solution)/shard_map/ppermute | solution.py:25
  21.1 2.2 %collective-permute-start.11 = (bf16[8192,128]{1,0:T(8,128)(2,1)}, bf16[8192,128]{1,0:T(8,128)(2,1)S(1)}, u32[]{:S(2)}, u32[]{:S(2)}) collective-permute-start(bf16[8192,128]{1,0:T(8,128)(2,1)} %bitcast.2), channel_id=1, source_target_pairs={{0,16},{1,113},{2,18},{3,115},{4,20},{5,117},{6,22},{7,119},{8,24}... | collective-permute-start | bytes 6291464 | tf_op jit(solution)/shard_map/ppermute | solution.py:25
  23.3 0.0 collective-permute-done.6
  23.3 3.5 %collective-permute-done.5 = bf16[512,256]{1,0:T(8,128)(2,1)S(1)} collective-permute-done((bf16[512,256]{1,0:T(8,128)(2,1)S(1)}, bf16[512,256]{1,0:T(8,128)(2,1)S(1)}, u32[]{:S(2)}, u32[]{:S(2)}) %collective-permute-start.5) | collective-permute-done | bytes 262176 | tf_op jit(solution)/shard_map/ppermute | solution.py:25
  26.8 0.1 pad_maximum_fusion.rest_0_
  26.9 0.1 fusion.4
  26.9 1.1 %collective-permute-start.8 = (bf16[1024,256]{1,0:T(8,128)(2,1)S(1)}, bf16[1024,256]{1,0:T(8,128)(2,1)S(1)}, u32[]{:S(2)}, u32[]{:S(2)}) collective-permute-start(bf16[1024,256]{1,0:T(8,128)(2,1)S(1)} %get-tuple-element.27), channel_id=1, source_target_pairs={{0,4},{1,3},{2,6},{3,129},{4,8},{5,7},{6,10},{7,133},{8,12},{9,11}... | collective-permute-start | bytes 1572872 | tf_op jit(solution)/shard_map/ppermute | solution.py:25
  28.0 1.7 %collective-permute-start.7 = (bf16[1024,256]{1,0:T(8,128)(2,1)S(1)}, bf16[1024,256]{1,0:T(8,128)(2,1)S(1)}, u32[]{:S(2)}, u32[]{:S(2)}) collective-permute-start(bf16[1024,256]{1,0:T(8,128)(2,1)S(1)} %get-tuple-element.28), channel_id=1, source_target_pairs={{0,12},{1,131},{2,14},{3,1},{4,0},{5,135},{6,2},{7,5},{8,4},{9,139... | collective-permute-start | bytes 1572872 | tf_op jit(solution)/shard_map/ppermute | solution.py:25
  29.7 1.2 %collective-permute-start.9 = (bf16[1024,256]{1,0:T(8,128)(2,1)S(1)}, bf16[1024,256]{1,0:T(8,128)(2,1)S(1)}, u32[]{:S(2)}, u32[]{:S(2)}) collective-permute-start(bf16[1024,256]{1,0:T(8,128)(2,1)S(1)} %get-tuple-element.27), channel_id=1, source_target_pairs={{0,12},{1,131},{2,14},{3,1},{4,0},{5,135},{6,2},{7,5},{8,4},{9,139... | collective-permute-start | bytes 1572872 | tf_op jit(solution)/shard_map/ppermute | solution.py:25
  30.9 0.2 collective-permute-start.10
  31.2 2.2 %shard_map.46.list_ref = s32[2,65]{1,0:T(2,128)S(1)} custom-call(s32[2,64]{1,0:T(2,128)S(1)} %compare_select_fusion.1.place_ref), custom_call_target="tpu_custom_call" | custom-call | tf_op jit(solution)/shard_map/pallas_call | solution.py:80
  33.4 0.0 copy-start.1
  33.4 3.1 %collective-permute-done.8.rest_6_ = bf16[1024,256]{1,0:T(8,128)(2,1)S(1)} collective-permute-done((bf16[1024,256]{1,0:T(8,128)(2,1)S(1)}, bf16[1024,256]{1,0:T(8,128)(2,1)S(1)}, u32[]{:S(2)}, u32[]{:S(2)}) %collective-permute-start.8) | collective-permute-done | bytes 524320 | tf_op jit(solution)/shard_map/ppermute | solution.py:25
  36.6 0.0 collective-permute-done.7.rest_1_
  36.6 2.7 %collective-permute-start.12 = (bf16[1024,256]{1,0:T(8,128)(2,1)S(1)}, bf16[1024,256]{1,0:T(8,128)(2,1)S(1)}, u32[]{:S(2)}, u32[]{:S(2)}) collective-permute-start(bf16[1024,256]{1,0:T(8,128)(2,1)S(1)} %collective-permute-done.7.rest_1_), channel_id=1, source_target_pairs={{0,12},{1,131},{2,14},{3,1},{4,0},{5,135},{6,2},{7,5},{8,4},{9,139... | collective-permute-start | bytes 1572872 | tf_op jit(solution)/shard_map/ppermute | solution.py:25
  39.2 0.0 collective-permute-start.13
  39.2 2.7 %collective-permute-done.9.rest_2_ = bf16[1024,256]{1,0:T(8,128)(2,1)S(1)} collective-permute-done((bf16[1024,256]{1,0:T(8,128)(2,1)S(1)}, bf16[1024,256]{1,0:T(8,128)(2,1)S(1)}, u32[]{:S(2)}, u32[]{:S(2)}) %collective-permute-start.9) | collective-permute-done | bytes 524320 | tf_op jit(solution)/shard_map/ppermute | solution.py:25
  42.0 4.3 %collective-permute-start.15 = (bf16[1024,256]{1,0:T(8,128)(2,1)S(1)}, bf16[1024,256]{1,0:T(8,128)(2,1)S(1)}, u32[]{:S(2)}, u32[]{:S(2)}) collective-permute-start(bf16[1024,256]{1,0:T(8,128)(2,1)S(1)} %collective-permute-done.7.rest_1_), channel_id=1, source_target_pairs={{0,1},{1,0},{2,3},{3,2},{4,5},{5,4},{6,7},{7,6},{8,9},{9,8},{10,11... | collective-permute-start | bytes 1572872 | tf_op jit(solution)/shard_map/ppermute | solution.py:25
  46.3 0.0 collective-permute-done.10.rest_5_
  46.3 0.0 collective-permute-start.14
  46.3 1.3 %collective-permute-done.12.rest_3_ = bf16[1024,256]{1,0:T(8,128)(2,1)S(1)} collective-permute-done((bf16[1024,256]{1,0:T(8,128)(2,1)S(1)}, bf16[1024,256]{1,0:T(8,128)(2,1)S(1)}, u32[]{:S(2)}, u32[]{:S(2)}) %collective-permute-start.12) | collective-permute-done | bytes 524320 | tf_op jit(solution)/shard_map/ppermute | solution.py:25
  47.6 4.3 %collective-permute-start.20 = (bf16[1024,256]{1,0:T(8,128)(2,1)S(1)}, bf16[1024,256]{1,0:T(8,128)(2,1)S(1)}, u32[]{:S(2)}, u32[]{:S(2)}) collective-permute-start(bf16[1024,256]{1,0:T(8,128)(2,1)S(1)} %collective-permute-done.8.rest_6_), channel_id=1, source_target_pairs={{0,1},{1,0},{2,3},{3,2},{4,5},{5,4},{6,7},{7,6},{8,9},{9,8},{10,11... | collective-permute-start | bytes 1572872 | tf_op jit(solution)/shard_map/ppermute | solution.py:25
  51.9 0.0 collective-permute-done.13.rest_4_
  51.9 2.1 %collective-permute-start.17 = (bf16[1024,256]{1,0:T(8,128)(2,1)S(1)}, bf16[1024,256]{1,0:T(8,128)(2,1)S(1)}, u32[]{:S(2)}, u32[]{:S(2)}) collective-permute-start(bf16[1024,256]{1,0:T(8,128)(2,1)S(1)} %collective-permute-done.12.rest_3_), channel_id=1, source_target_pairs={{0,1},{1,0},{2,3},{3,2},{4,5},{5,4},{6,7},{7,6},{8,9},{9,8},{10,11... | collective-permute-start | bytes 1572872 | tf_op jit(solution)/shard_map/ppermute | solution.py:25
  54.0 0.0 collective-permute-start.18
  54.1 0.0 collective-permute-done.15.rest_8_
  54.1 0.5 collective-permute-start.16
  54.6 0.1 collective-permute-start.19
  54.7 0.9 %collective-permute-done.17.rest_10_ = bf16[1024,256]{1,0:T(8,128)(2,1)S(1)} collective-permute-done((bf16[1024,256]{1,0:T(8,128)(2,1)S(1)}, bf16[1024,256]{1,0:T(8,128)(2,1)S(1)}, u32[]{:S(2)}, u32[]{:S(2)}) %collective-permute-start.17) | collective-permute-done | bytes 524320 | tf_op jit(solution)/shard_map/ppermute | solution.py:25
  55.6 0.7 %collective-permute-done.18.rest_11_ = bf16[1024,256]{1,0:T(8,128)(2,1)S(1)} collective-permute-done((bf16[1024,256]{1,0:T(8,128)(2,1)S(1)}, bf16[1024,256]{1,0:T(8,128)(2,1)S(1)}, u32[]{:S(2)}, u32[]{:S(2)}) %collective-permute-start.18) | collective-permute-done | bytes 524320 | tf_op jit(solution)/shard_map/ppermute | solution.py:25
  56.3 0.7 %collective-permute-done.16.rest_9_ = bf16[1024,256]{1,0:T(8,128)(2,1)S(1)} collective-permute-done((bf16[1024,256]{1,0:T(8,128)(2,1)S(1)}, bf16[1024,256]{1,0:T(8,128)(2,1)S(1)}, u32[]{:S(2)}, u32[]{:S(2)}) %collective-permute-start.16) | collective-permute-done | bytes 524320 | tf_op jit(solution)/shard_map/ppermute | solution.py:25
  57.1 0.7 %collective-permute-done.19.rest_12_ = bf16[1024,256]{1,0:T(8,128)(2,1)S(1)} collective-permute-done((bf16[1024,256]{1,0:T(8,128)(2,1)S(1)}, bf16[1024,256]{1,0:T(8,128)(2,1)S(1)}, u32[]{:S(2)}, u32[]{:S(2)}) %collective-permute-start.19) | collective-permute-done | bytes 524320 | tf_op jit(solution)/shard_map/ppermute | solution.py:25
  57.8 3.9 %shard_map.48 = f32[128,256]{1,0:T(8,128)S(1)} custom-call(s32[2,65]{1,0:T(2,128)S(1)} %shard_map.46.list_ref, bf16[8192,128]{1,0:T(8,128)(2,1)S(1)} %collective-permute-done.11.tiles_ref, bf16[2048,256]{1,0:T(8,128)(2,1)S(1)} %pad_maximum_fusion.rest_0_, bf16[1024,256]{1,0:T(8,128)(2,1)S(1)} %collective-permute-done.7.rest_1_, ...), custom_call_target="tpu_custom_call" | custom-call | flops 268435456 | bytes 3145728 | tf_op jit(solution)/shard_map/pallas_call | solution.py:122
  61.7 0.1 collective-permute-start.21
  61.8 3.9 %shard_map.47 = f32[128,256]{1,0:T(8,128)S(1)} custom-call(s32[2,65]{1,0:T(2,128)S(1)} %shard_map.46.list_ref, bf16[8192,128]{1,0:T(8,128)(2,1)S(1)} %bitcast.3, bf16[2048,256]{1,0:T(8,128)(2,1)S(1)} %pad_maximum_fusion.rest_0_, bf16[1024,256]{1,0:T(8,128)(2,1)S(1)} %collective-permute-done.7.rest_1_, bf16[1024,256]{1,0:T(8,128)(2,1)S(1)} %collective-permute-done.9.rest_2_, ...), custom_call_target="tpu_custom_call" | custom-call | flops 268435456 | bytes 3145728 | tf_op jit(solution)/shard_map/pallas_call | solution.py:122
  65.7 1.1 %collective-permute-done.21 = f32[128,256]{1,0:T(8,128)S(1)} collective-permute-done((f32[128,256]{1,0:T(8,128)S(1)}, f32[128,256]{1,0:T(8,128)S(1)}, u32[]{:S(2)}, u32[]{:S(2)}) %collective-permute-start.21) | collective-permute-done | bytes 131104 | tf_op jit(solution)/shard_map/ppermute | solution.py:25
  66.8 0.8 %fusion = bf16[128,256]{1,0:T(8,128)(2,1)} fusion(bf16[256,256]{1,0:T(8,128)(2,1)S(1)} %copy-done, f32[128,256]{1,0:T(8,128)S(1)} %shard_map.47, f32[128,256]{1,0:T(8,128)S(1)} %collective-permute-done.21), kind=kOutput, calls=%fused_computation.1 | convolution fusion | flops 16908288 | bytes 458752 | tf_op jit(solution)/shard_map/dot_general | solution.py:157
  (8 shorter events, 0.0 us)
Async XLA Ops:
  0.0 66.8 %copy-start = (bf16[256,256]{1,0:T(8,128)(2,1)S(1)}, bf16[256,256]{1,0:T(8,128)(2,1)}, u32[]{:S(2)}) copy-start(bf16[256,256]{1,0:T(8,128)(2,1)} %param.7) | copy-start | bytes 393220
  0.0 13.4 %collective-permute-start.1 = (bf16[128,256]{1,0:T(8,128)(2,1)}, bf16[128,256]{1,0:T(8,128)(2,1)S(1)}, u32[]{:S(2)}, u32[]{:S(2)}) collective-permute-start(bf16[128,256]{1,0:T(8,128)(2,1)} %param.4), channel_id=1, source_target_pairs={{0,64},{1,65},{2,66},{3,67},{4,68},{5,69},{6,70},{7,71},{8,72},{9,... | collective-permute-start | bytes 196616 | tf_op jit(solution)/shard_map/ppermute | solution.py:25
  7.7 7.6 %collective-permute-start = (bf16[128,256]{1,0:T(8,128)(2,1)}, bf16[128,256]{1,0:T(8,128)(2,1)S(1)}, u32[]{:S(2)}, u32[]{:S(2)}) collective-permute-start(bf16[128,256]{1,0:T(8,128)(2,1)} %param.4), channel_id=1, source_target_pairs={{0,96},{1,97},{2,98},{3,99},{4,100},{5,101},{6,102},{7,103},{8,104... | collective-permute-start | bytes 196616 | tf_op jit(solution)/shard_map/ppermute | solution.py:25
  7.7 7.6 %collective-permute-start.2 = (bf16[128,256]{1,0:T(8,128)(2,1)}, bf16[128,256]{1,0:T(8,128)(2,1)S(1)}, u32[]{:S(2)}, u32[]{:S(2)}) collective-permute-start(bf16[128,256]{1,0:T(8,128)(2,1)} %param.4), channel_id=1, source_target_pairs={{0,32},{1,33},{2,34},{3,35},{4,36},{5,37},{6,38},{7,39},{8,40},{9,... | collective-permute-start | bytes 196616 | tf_op jit(solution)/shard_map/ppermute | solution.py:25
  10.1 2.6 %collective-permute-start.3 = (s32[1,64]{1,0:T(1,128)}, s32[1,64]{1,0:T(1,128)S(1)}, u32[]{:S(2)}, u32[]{:S(2)}) collective-permute-start(s32[1,64]{1,0:T(1,128)} %param.6), channel_id=1, source_target_pairs={{0,16},{1,113},{2,18},{3,115},{4,20},{5,117},{6,22},{7,119},{8,24}... | collective-permute-start | bytes 776 | tf_op jit(solution)/shard_map/ppermute | solution.py:25
  16.2 7.1 %collective-permute-start.6 = (bf16[512,256]{1,0:T(8,128)(2,1)S(1)}, bf16[512,256]{1,0:T(8,128)(2,1)S(1)}, u32[]{:S(2)}, u32[]{:S(2)}) collective-permute-start(bf16[512,256]{1,0:T(8,128)(2,1)S(1)} %pad_maximum_fusion.1), channel_id=1, source_target_pairs={{0,2},{1,5},{2,128},{3,7},{4,6},{5,9},{6,132},{7,11},{8,10},{9,13}... | collective-permute-start | bytes 786440 | tf_op jit(solution)/shard_map/ppermute | solution.py:25
  17.5 9.3 %collective-permute-start.5 = (bf16[512,256]{1,0:T(8,128)(2,1)S(1)}, bf16[512,256]{1,0:T(8,128)(2,1)S(1)}, u32[]{:S(2)}, u32[]{:S(2)}) collective-permute-start(bf16[512,256]{1,0:T(8,128)(2,1)S(1)} %pad_maximum_fusion.1), channel_id=1, source_target_pairs={{0,128},{1,9},{2,130},{3,11},{4,132},{5,13},{6,134},{7,15},{8,136}... | collective-permute-start | bytes 786440 | tf_op jit(solution)/shard_map/ppermute | solution.py:25
  19.9 6.9 %collective-permute-start.4 = (bf16[512,256]{1,0:T(8,128)(2,1)S(1)}, bf16[512,256]{1,0:T(8,128)(2,1)S(1)}, u32[]{:S(2)}, u32[]{:S(2)}) collective-permute-start(bf16[512,256]{1,0:T(8,128)(2,1)S(1)} %pad_maximum_fusion.1), channel_id=1, source_target_pairs={{0,130},{1,13},{2,0},{3,15},{4,134},{5,1},{6,4},{7,3},{8,138},{9,5... | collective-permute-start | bytes 786440 | tf_op jit(solution)/shard_map/ppermute | solution.py:25
  21.1 33.0 %collective-permute-start.11 = (bf16[8192,128]{1,0:T(8,128)(2,1)}, bf16[8192,128]{1,0:T(8,128)(2,1)S(1)}, u32[]{:S(2)}, u32[]{:S(2)}) collective-permute-start(bf16[8192,128]{1,0:T(8,128)(2,1)} %bitcast.2), channel_id=1, source_target_pairs={{0,16},{1,113},{2,18},{3,115},{4,20},{5,117},{6,22},{7,119},{8,24}... | collective-permute-start | bytes 6291464 | tf_op jit(solution)/shard_map/ppermute | solution.py:25
  26.9 9.6 %collective-permute-start.8 = (bf16[1024,256]{1,0:T(8,128)(2,1)S(1)}, bf16[1024,256]{1,0:T(8,128)(2,1)S(1)}, u32[]{:S(2)}, u32[]{:S(2)}) collective-permute-start(bf16[1024,256]{1,0:T(8,128)(2,1)S(1)} %get-tuple-element.27), channel_id=1, source_target_pairs={{0,4},{1,3},{2,6},{3,129},{4,8},{5,7},{6,10},{7,133},{8,12},{9,11}... | collective-permute-start | bytes 1572872 | tf_op jit(solution)/shard_map/ppermute | solution.py:25
  28.0 8.5 %collective-permute-start.7 = (bf16[1024,256]{1,0:T(8,128)(2,1)S(1)}, bf16[1024,256]{1,0:T(8,128)(2,1)S(1)}, u32[]{:S(2)}, u32[]{:S(2)}) collective-permute-start(bf16[1024,256]{1,0:T(8,128)(2,1)S(1)} %get-tuple-element.28), channel_id=1, source_target_pairs={{0,12},{1,131},{2,14},{3,1},{4,0},{5,135},{6,2},{7,5},{8,4},{9,139... | collective-permute-start | bytes 1572872 | tf_op jit(solution)/shard_map/ppermute | solution.py:25
  29.7 12.3 %collective-permute-start.9 = (bf16[1024,256]{1,0:T(8,128)(2,1)S(1)}, bf16[1024,256]{1,0:T(8,128)(2,1)S(1)}, u32[]{:S(2)}, u32[]{:S(2)}) collective-permute-start(bf16[1024,256]{1,0:T(8,128)(2,1)S(1)} %get-tuple-element.27), channel_id=1, source_target_pairs={{0,12},{1,131},{2,14},{3,1},{4,0},{5,135},{6,2},{7,5},{8,4},{9,139... | collective-permute-start | bytes 1572872 | tf_op jit(solution)/shard_map/ppermute | solution.py:25
  30.9 15.4 %collective-permute-start.10 = (bf16[1024,256]{1,0:T(8,128)(2,1)S(1)}, bf16[1024,256]{1,0:T(8,128)(2,1)S(1)}, u32[]{:S(2)}, u32[]{:S(2)}) collective-permute-start(bf16[1024,256]{1,0:T(8,128)(2,1)S(1)} %get-tuple-element.28), channel_id=1, source_target_pairs={{0,4},{1,3},{2,6},{3,129},{4,8},{5,7},{6,10},{7,133},{8,12},{9,11}... | collective-permute-start | bytes 1572872 | tf_op jit(solution)/shard_map/ppermute | solution.py:25
  33.4 28.4 %copy-start.1 = (bf16[1,64,128,128]{3,2,1,0:T(8,128)(2,1)S(1)}, bf16[1,64,128,128]{3,2,1,0:T(8,128)(2,1)}, u32[]{:S(2)}) copy-start(bf16[1,64,128,128]{3,2,1,0:T(8,128)(2,1)} %param.5) | copy-start | bytes 6291460
  36.6 11.0 %collective-permute-start.12 = (bf16[1024,256]{1,0:T(8,128)(2,1)S(1)}, bf16[1024,256]{1,0:T(8,128)(2,1)S(1)}, u32[]{:S(2)}, u32[]{:S(2)}) collective-permute-start(bf16[1024,256]{1,0:T(8,128)(2,1)S(1)} %collective-permute-done.7.rest_1_), channel_id=1, source_target_pairs={{0,12},{1,131},{2,14},{3,1},{4,0},{5,135},{6,2},{7,5},{8,4},{9,139... | collective-permute-start | bytes 1572872 | tf_op jit(solution)/shard_map/ppermute | solution.py:25
  39.2 12.7 %collective-permute-start.13 = (bf16[1024,256]{1,0:T(8,128)(2,1)S(1)}, bf16[1024,256]{1,0:T(8,128)(2,1)S(1)}, u32[]{:S(2)}, u32[]{:S(2)}) collective-permute-start(bf16[1024,256]{1,0:T(8,128)(2,1)S(1)} %collective-permute-done.8.rest_6_), channel_id=1, source_target_pairs={{0,4},{1,3},{2,6},{3,129},{4,8},{5,7},{6,10},{7,133},{8,12},{9,11}... | collective-permute-start | bytes 1572872 | tf_op jit(solution)/shard_map/ppermute | solution.py:25
  42.0 12.1 %collective-permute-start.15 = (bf16[1024,256]{1,0:T(8,128)(2,1)S(1)}, bf16[1024,256]{1,0:T(8,128)(2,1)S(1)}, u32[]{:S(2)}, u32[]{:S(2)}) collective-permute-start(bf16[1024,256]{1,0:T(8,128)(2,1)S(1)} %collective-permute-done.7.rest_1_), channel_id=1, source_target_pairs={{0,1},{1,0},{2,3},{3,2},{4,5},{5,4},{6,7},{7,6},{8,9},{9,8},{10,11... | collective-permute-start | bytes 1572872 | tf_op jit(solution)/shard_map/ppermute | solution.py:25
  46.3 8.3 %collective-permute-start.14 = (bf16[2048,256]{1,0:T(8,128)(2,1)S(1)}, bf16[2048,256]{1,0:T(8,128)(2,1)S(1)}, u32[]{:S(2)}, u32[]{:S(2)}) collective-permute-start(bf16[2048,256]{1,0:T(8,128)(2,1)S(1)} %pad_maximum_fusion.rest_0_), channel_id=1, source_target_pairs={{0,1},{1,0},{2,3},{3,2},{4,5},{5,4},{6,7},{7,6},{8,9},{9,8},{10,11... | collective-permute-start | bytes 3145736 | tf_op jit(solution)/shard_map/ppermute | solution.py:25
  47.6 7.0 %collective-permute-start.20 = (bf16[1024,256]{1,0:T(8,128)(2,1)S(1)}, bf16[1024,256]{1,0:T(8,128)(2,1)S(1)}, u32[]{:S(2)}, u32[]{:S(2)}) collective-permute-start(bf16[1024,256]{1,0:T(8,128)(2,1)S(1)} %collective-permute-done.8.rest_6_), channel_id=1, source_target_pairs={{0,1},{1,0},{2,3},{3,2},{4,5},{5,4},{6,7},{7,6},{8,9},{9,8},{10,11... | collective-permute-start | bytes 1572872 | tf_op jit(solution)/shard_map/ppermute | solution.py:25
  51.9 3.6 %collective-permute-start.17 = (bf16[1024,256]{1,0:T(8,128)(2,1)S(1)}, bf16[1024,256]{1,0:T(8,128)(2,1)S(1)}, u32[]{:S(2)}, u32[]{:S(2)}) collective-permute-start(bf16[1024,256]{1,0:T(8,128)(2,1)S(1)} %collective-permute-done.12.rest_3_), channel_id=1, source_target_pairs={{0,1},{1,0},{2,3},{3,2},{4,5},{5,4},{6,7},{7,6},{8,9},{9,8},{10,11... | collective-permute-start | bytes 1572872 | tf_op jit(solution)/shard_map/ppermute | solution.py:25
  54.0 2.3 %collective-permute-start.18 = (bf16[1024,256]{1,0:T(8,128)(2,1)S(1)}, bf16[1024,256]{1,0:T(8,128)(2,1)S(1)}, u32[]{:S(2)}, u32[]{:S(2)}) collective-permute-start(bf16[1024,256]{1,0:T(8,128)(2,1)S(1)} %collective-permute-done.13.rest_4_), channel_id=1, source_target_pairs={{0,1},{1,0},{2,3},{3,2},{4,5},{5,4},{6,7},{7,6},{8,9},{9,8},{10,11... | collective-permute-start | bytes 1572872 | tf_op jit(solution)/shard_map/ppermute | solution.py:25
  54.1 3.0 %collective-permute-start.16 = (bf16[1024,256]{1,0:T(8,128)(2,1)S(1)}, bf16[1024,256]{1,0:T(8,128)(2,1)S(1)}, u32[]{:S(2)}, u32[]{:S(2)}) collective-permute-start(bf16[1024,256]{1,0:T(8,128)(2,1)S(1)} %collective-permute-done.9.rest_2_), channel_id=1, source_target_pairs={{0,1},{1,0},{2,3},{3,2},{4,5},{5,4},{6,7},{7,6},{8,9},{9,8},{10,11... | collective-permute-start | bytes 1572872 | tf_op jit(solution)/shard_map/ppermute | solution.py:25
  54.6 3.3 %collective-permute-start.19 = (bf16[1024,256]{1,0:T(8,128)(2,1)S(1)}, bf16[1024,256]{1,0:T(8,128)(2,1)S(1)}, u32[]{:S(2)}, u32[]{:S(2)}) collective-permute-start(bf16[1024,256]{1,0:T(8,128)(2,1)S(1)} %collective-permute-done.10.rest_5_), channel_id=1, source_target_pairs={{0,1},{1,0},{2,3},{3,2},{4,5},{5,4},{6,7},{7,6},{8,9},{9,8},{10,11... | collective-permute-start | bytes 1572872 | tf_op jit(solution)/shard_map/ppermute | solution.py:25
  61.7 5.1 %collective-permute-start.21 = (f32[128,256]{1,0:T(8,128)S(1)}, f32[128,256]{1,0:T(8,128)S(1)}, u32[]{:S(2)}, u32[]{:S(2)}) collective-permute-start(f32[128,256]{1,0:T(8,128)S(1)} %shard_map.48), channel_id=1, source_target_pairs={{0,112},{1,17},{2,114},{3,19},{4,116},{5,21},{6,118},{7,23},{8,120... | collective-permute-start | bytes 393224 | tf_op jit(solution)/shard_map/ppermute | solution.py:25

commit v6 on v5

--- a/solution.py
+++ b/solution.py
@@ -13,7 +13,8 @@
 WIDTH = 256
 TILES = 64
 PLANE = 16
-BATCH = 16
+BUFFERS = 7
+BATCH = 8
 
 
 def move(a, target):
@@ -60,26 +61,30 @@
     last = jnp.where(at == 0, dx, dy)
     inner = middle * 4 + dz
     buffer = jnp.where(last == 0, 0, last * 2 - 1 + (inner >> 3))
-    place = ((at ^ core) * 7 + buffer) * PLANE + inner
+    place = ((at ^ core) * BUFFERS + buffer) * PLANE + inner
     return jnp.where(((columns >> 4) & 1) == zl, place, -1)
 
 
 def list_kernel(place_ref, list_ref):
     for r in range(2):
 
-        def step(k, n):
+        def step(k, counts):
             place = place_ref[r, k]
-            list_ref[r, n] = (k << 8) + (place & 255)
-            return jnp.where(place >= 0, n + 1, n)
+            held, far = place >= 0, place >= BUFFERS * PLANE
+            list_ref[2 * r, counts[0]] = (k << 8) + (place & 255)
+            list_ref[2 * r + 1, counts[1]] = (k << 8) + ((place - BUFFERS * PLANE) & 255)
+            return jnp.where(held & ~far, counts[0] + 1, counts[0]), jnp.where(far, counts[1] + 1, counts[1])
 
-        list_ref[r, TILES] = lax.fori_loop(0, TILES, step, 0)
+        counts = lax.fori_loop(0, TILES, step, (0, 0))
+        list_ref[2 * r, TILES] = counts[0]
+        list_ref[2 * r + 1, TILES] = counts[1]
 
 
 def listed(place):
     smem = pl.BlockSpec(memory_space=pltpu.SMEM)
     return pl.pallas_call(
         list_kernel,
-        out_shape=jax.ShapeDtypeStruct((2, TILES + 1), jnp.int32),
+        out_shape=jax.ShapeDtypeStruct((4, TILES + 1), jnp.int32),
         in_specs=[smem],
         out_specs=smem,
         compiler_params=pltpu.CompilerParams(vmem_limit_bytes=1024 * 1024),
@@ -94,29 +99,29 @@
     vmem = pl.BlockSpec(memory_space=pltpu.VMEM)
 
     def kernel(list_ref, tiles_ref, *rest):
-        held, out_ref = rest[:-1], rest[-1]
+        out_ref = rest[-1]
         out_ref[...] = jnp.zeros_like(out_ref)
-        n = list_ref[row, TILES]
+        for side in range(2):
+            held = rest[side * BUFFERS : (side + 1) * BUFFERS]
+            which = 2 * row + side
+            n = list_ref[which, TILES]
 
-        @pl.loop(0, (n + BATCH - 1) // BATCH)
-        def _(i):
-            left, right = [], []
-            for j in range(BATCH):
-                at = i * BATCH + j
-                code = list_ref[row, jnp.minimum(at, n - 1)]
-                tile = tiles_ref[rows(code >> 8), :]
-                left.append(jnp.where(at < n, tile, jnp.zeros_like(tile)))
-                here = rows(code & 15)
-                buffer = (code >> 4) & 15
-                block = None
-                for b, ref in enumerate(held):
-                    within = here if ref.shape[0] == PLANE * SIDE else rows(code & 7)
-                    found = ref[within, :]
-                    block = found if block is None else jnp.where(buffer == b, found, block)
-                right.append(block)
-            out_ref[...] += jnp.dot(
-                jnp.concatenate(left, axis=1), jnp.concatenate(right, axis=0), preferred_element_type=jnp.float32
-            )
+            @pl.loop(0, (n + BATCH - 1) // BATCH)
+            def _(i):
+                left, right = [], []
+                for j in range(BATCH):
+                    at = i * BATCH + j
+                    code = list_ref[which, jnp.minimum(at, n - 1)]
+                    tile = tiles_ref[rows(code >> 8), :]
+                    left.append(jnp.where(at < n, tile, jnp.zeros_like(tile)))
+                    buffer = (code >> 4) & 15
+                    block = held[0][rows(code & 15), :]
+                    for b in range(1, BUFFERS):
+                        block = jnp.where(buffer == b, held[b][rows(code & 7), :], block)
+                    right.append(block)
+                out_ref[...] += jnp.dot(
+                    jnp.concatenate(left, axis=1), jnp.concatenate(right, axis=0), preferred_element_type=jnp.float32
+                )
 
     held = [pltpu.with_memory_space_constraint(a, pltpu.VMEM) for a in (tiles, *buffers)]
     return pl.pallas_call(

time: 67.2 us -> 66 us (0.982)
  Pallas kernels: 9.95 us -> 7.01 us
  waiting for transfers between devices: 18.4 us -> 19.8 us
    pallas_call x2, Pallas kernels: 7.73 us -> 4.3 us  [multiply(): pl.pallas_call(kernel, out_shape=jax.ShapeDtypeStruct((SIDE, WIDTH), jnp....]
    ppermute x22, waiting for transfers between devices: 18.4 us -> 19.8 us  [move(): return lax.ppermute(a, AXES, found)]
  transfers between devices with their start and end apart: 22 -> 22, of which waited for: 11 -> 11; matrix products, arithmetic and copies ran while one was open for 1% -> 1% of each run, Pallas kernels for 9% -> 7%
where the time goes in v6:
time: 66 us; the launch traced here: 66.1 us
  starting transfers between devices  36.6 us (55%)
  waiting for transfers between devices  19.8 us (30%)
  Pallas kernels  7.01 us (11%)
  other arithmetic  1.6 us (2%)
  matrix products  0.8 us (1%)
    ppermute x22, starting transfers between devices, move(): return lax.ppermute(a, AXES, found)  36.6 us
    ppermute x22, waiting for transfers between devices, move(): return lax.ppermute(a, AXES, found)  19.8 us
    pallas_call x2, Pallas kernels, multiply(): pl.pallas_call(kernel, out_shape=jax.ShapeDtypeStruct((SIDE, WIDTH), jnp....  4.3 us
    pallas_call x1, Pallas kernels, listed(): pl.pallas_call(list_kernel, out_shape=jax.ShapeDtypeStruct((4, TILES + 1)...  2.71 us
  transfers between devices with their start and end apart: 22, of which 11 were waited for; matrix products, arithmetic and copies ran while one was open for 1% of the time, Pallas kernels for 7%

profile of v6, /device:TPU:1, one launch (start us, length us, event | category | flops | bytes accessed | tf_op | source)
XLA Modules:
  0.0 66.1 jit_solution(8798745176966678280)
XLA Ops:
  0.0 7.7 %collective-permute-start.1 = (bf16[128,256]{1,0:T(8,128)(2,1)}, bf16[128,256]{1,0:T(8,128)(2,1)S(1)}, u32[]{:S(2)}, u32[]{:S(2)}) collective-permute-start(bf16[128,256]{1,0:T(8,128)(2,1)} %param.4), channel_id=1, source_target_pairs={{0,64},{1,65},{2,66},{3,67},{4,68},{5,69},{6,70},{7,71},{8,72},{9,... | collective-permute-start | bytes 196616 | tf_op jit(solution)/shard_map/ppermute | solution.py:26
  7.7 0.0 collective-permute-start
  7.7 2.4 %collective-permute-start.2 = (bf16[128,256]{1,0:T(8,128)(2,1)}, bf16[128,256]{1,0:T(8,128)(2,1)S(1)}, u32[]{:S(2)}, u32[]{:S(2)}) collective-permute-start(bf16[128,256]{1,0:T(8,128)(2,1)} %param.4), channel_id=1, source_target_pairs={{0,32},{1,33},{2,34},{3,35},{4,36},{5,37},{6,38},{7,39},{8,40},{9,... | collective-permute-start | bytes 196616 | tf_op jit(solution)/shard_map/ppermute | solution.py:26
  10.1 1.0 %collective-permute-start.3 = (s32[1,64]{1,0:T(1,128)}, s32[1,64]{1,0:T(1,128)S(1)}, u32[]{:S(2)}, u32[]{:S(2)}) collective-permute-start(s32[1,64]{1,0:T(1,128)} %param.6), channel_id=1, source_target_pairs={{0,16},{1,113},{2,18},{3,115},{4,20},{5,117},{6,22},{7,119},{8,24}... | collective-permute-start | bytes 776 | tf_op jit(solution)/shard_map/ppermute | solution.py:26
  11.1 1.6 %collective-permute-done.3 = s32[1,64]{1,0:T(1,128)S(1)} collective-permute-done((s32[1,64]{1,0:T(1,128)}, s32[1,64]{1,0:T(1,128)S(1)}, u32[]{:S(2)}, u32[]{:S(2)}) %collective-permute-start.3) | collective-permute-done | bytes 288 | tf_op jit(solution)/shard_map/ppermute | solution.py:26
  12.7 0.7 %compare_select_fusion.1.place_ref = s32[2,64]{1,0:T(2,128)S(1)} fusion(s32[1,64]{1,0:T(1,128)S(1)} %collective-permute-done.3, s32[1,64]{1,0:T(1,128)} %param.6, s32[]{:T(128)S(6)} %axis_index.77, s32[]{:T(128)S(6)} %add.23, s32[]{:T(128)S(6)} %axis_index.68, s32[]{:T(128)S(6)} %axis_index.65, s32[]{:T(128)S(6)} %axis_index.63), kind=kLoop, calls=%fused_computation.6 | loop fusion | flops 4736 | bytes 1044 | tf_op jit(solution)/shard_map/jit(_where)/select_n | solution.py:65
  13.4 0.0 collective-permute-done.1
  13.4 1.9 %collective-permute-done = bf16[128,256]{1,0:T(8,128)(2,1)S(1)} collective-permute-done((bf16[128,256]{1,0:T(8,128)(2,1)}, bf16[128,256]{1,0:T(8,128)(2,1)S(1)}, u32[]{:S(2)}, u32[]{:S(2)}) %collective-permute-start) | collective-permute-done | bytes 65568 | tf_op jit(solution)/shard_map/ppermute | solution.py:26
  15.3 0.9 %pad_maximum_fusion.1 = bf16[512,256]{1,0:T(8,128)(2,1)S(1)} fusion(bf16[128,256]{1,0:T(8,128)(2,1)S(1)} %collective-permute-done.2, bf16[128,256]{1,0:T(8,128)(2,1)S(1)} %collective-permute-done.1, bf16[128,256]{1,0:T(8,128)(2,1)S(1)} %collective-permute-done, bf16[128,256]{1,0:T(8,128)(2,1)} %param.4), kind=kLoop, calls=%fused_computation.3 | loop fusion | flops 1048576 | bytes 524288 | tf_op jit(solution)/shard_map/concatenate | solution.py:145
  16.2 1.3 %collective-permute-start.6 = (bf16[512,256]{1,0:T(8,128)(2,1)S(1)}, bf16[512,256]{1,0:T(8,128)(2,1)S(1)}, u32[]{:S(2)}, u32[]{:S(2)}) collective-permute-start(bf16[512,256]{1,0:T(8,128)(2,1)S(1)} %pad_maximum_fusion.1), channel_id=1, source_target_pairs={{0,2},{1,5},{2,128},{3,7},{4,6},{5,9},{6,132},{7,11},{8,10},{9,13}... | collective-permute-start | bytes 786440 | tf_op jit(solution)/shard_map/ppermute | solution.py:26
  17.5 2.5 %collective-permute-start.5 = (bf16[512,256]{1,0:T(8,128)(2,1)S(1)}, bf16[512,256]{1,0:T(8,128)(2,1)S(1)}, u32[]{:S(2)}, u32[]{:S(2)}) collective-permute-start(bf16[512,256]{1,0:T(8,128)(2,1)S(1)} %pad_maximum_fusion.1), channel_id=1, source_target_pairs={{0,128},{1,9},{2,130},{3,11},{4,132},{5,13},{6,134},{7,15},{8,136}... | collective-permute-start | bytes 786440 | tf_op jit(solution)/shard_map/ppermute | solution.py:26
  19.9 1.2 %collective-permute-start.4 = (bf16[512,256]{1,0:T(8,128)(2,1)S(1)}, bf16[512,256]{1,0:T(8,128)(2,1)S(1)}, u32[]{:S(2)}, u32[]{:S(2)}) collective-permute-start(bf16[512,256]{1,0:T(8,128)(2,1)S(1)} %pad_maximum_fusion.1), channel_id=1, source_target_pairs={{0,130},{1,13},{2,0},{3,15},{4,134},{5,1},{6,4},{7,3},{8,138},{9,5... | collective-permute-start | bytes 786440 | tf_op jit(solution)/shard_map/ppermute | solution.py:26
  21.1 2.2 %collective-permute-start.11 = (bf16[8192,128]{1,0:T(8,128)(2,1)}, bf16[8192,128]{1,0:T(8,128)(2,1)S(1)}, u32[]{:S(2)}, u32[]{:S(2)}) collective-permute-start(bf16[8192,128]{1,0:T(8,128)(2,1)} %bitcast.2), channel_id=1, source_target_pairs={{0,16},{1,113},{2,18},{3,115},{4,20},{5,117},{6,22},{7,119},{8,24}... | collective-permute-start | bytes 6291464 | tf_op jit(solution)/shard_map/ppermute | solution.py:26
  23.3 0.0 collective-permute-done.6
  23.3 3.5 %collective-permute-done.5 = bf16[512,256]{1,0:T(8,128)(2,1)S(1)} collective-permute-done((bf16[512,256]{1,0:T(8,128)(2,1)S(1)}, bf16[512,256]{1,0:T(8,128)(2,1)S(1)}, u32[]{:S(2)}, u32[]{:S(2)}) %collective-permute-start.5) | collective-permute-done | bytes 262176 | tf_op jit(solution)/shard_map/ppermute | solution.py:26
  26.8 0.1 pad_maximum_fusion.rest_0_
  26.9 0.1 fusion.4
  26.9 1.1 %collective-permute-start.8 = (bf16[1024,256]{1,0:T(8,128)(2,1)S(1)}, bf16[1024,256]{1,0:T(8,128)(2,1)S(1)}, u32[]{:S(2)}, u32[]{:S(2)}) collective-permute-start(bf16[1024,256]{1,0:T(8,128)(2,1)S(1)} %get-tuple-element.27), channel_id=1, source_target_pairs={{0,4},{1,3},{2,6},{3,129},{4,8},{5,7},{6,10},{7,133},{8,12},{9,11}... | collective-permute-start | bytes 1572872 | tf_op jit(solution)/shard_map/ppermute | solution.py:26
  28.0 1.7 %collective-permute-start.7 = (bf16[1024,256]{1,0:T(8,128)(2,1)S(1)}, bf16[1024,256]{1,0:T(8,128)(2,1)S(1)}, u32[]{:S(2)}, u32[]{:S(2)}) collective-permute-start(bf16[1024,256]{1,0:T(8,128)(2,1)S(1)} %get-tuple-element.28), channel_id=1, source_target_pairs={{0,12},{1,131},{2,14},{3,1},{4,0},{5,135},{6,2},{7,5},{8,4},{9,139... | collective-permute-start | bytes 1572872 | tf_op jit(solution)/shard_map/ppermute | solution.py:26
  29.7 1.2 %collective-permute-start.9 = (bf16[1024,256]{1,0:T(8,128)(2,1)S(1)}, bf16[1024,256]{1,0:T(8,128)(2,1)S(1)}, u32[]{:S(2)}, u32[]{:S(2)}) collective-permute-start(bf16[1024,256]{1,0:T(8,128)(2,1)S(1)} %get-tuple-element.27), channel_id=1, source_target_pairs={{0,12},{1,131},{2,14},{3,1},{4,0},{5,135},{6,2},{7,5},{8,4},{9,139... | collective-permute-start | bytes 1572872 | tf_op jit(solution)/shard_map/ppermute | solution.py:26
  30.9 0.2 collective-permute-start.10
  31.2 2.7 %shard_map.46.list_ref = s32[4,65]{1,0:T(4,128)S(1)} custom-call(s32[2,64]{1,0:T(2,128)S(1)} %compare_select_fusion.1.place_ref), custom_call_target="tpu_custom_call" | custom-call | tf_op jit(solution)/shard_map/pallas_call | solution.py:85
  33.9 0.0 copy-start.1
  33.9 2.7 %collective-permute-done.8.rest_6_ = bf16[1024,256]{1,0:T(8,128)(2,1)S(1)} collective-permute-done((bf16[1024,256]{1,0:T(8,128)(2,1)S(1)}, bf16[1024,256]{1,0:T(8,128)(2,1)S(1)}, u32[]{:S(2)}, u32[]{:S(2)}) %collective-permute-start.8) | collective-permute-done | bytes 524320 | tf_op jit(solution)/shard_map/ppermute | solution.py:26
  36.6 0.0 collective-permute-done.7.rest_1_
  36.6 2.7 %collective-permute-start.12 = (bf16[1024,256]{1,0:T(8,128)(2,1)S(1)}, bf16[1024,256]{1,0:T(8,128)(2,1)S(1)}, u32[]{:S(2)}, u32[]{:S(2)}) collective-permute-start(bf16[1024,256]{1,0:T(8,128)(2,1)S(1)} %collective-permute-done.7.rest_1_), channel_id=1, source_target_pairs={{0,12},{1,131},{2,14},{3,1},{4,0},{5,135},{6,2},{7,5},{8,4},{9,139... | collective-permute-start | bytes 1572872 | tf_op jit(solution)/shard_map/ppermute | solution.py:26
  39.2 2.7 %collective-permute-done.9.rest_2_ = bf16[1024,256]{1,0:T(8,128)(2,1)S(1)} collective-permute-done((bf16[1024,256]{1,0:T(8,128)(2,1)S(1)}, bf16[1024,256]{1,0:T(8,128)(2,1)S(1)}, u32[]{:S(2)}, u32[]{:S(2)}) %collective-permute-start.9) | collective-permute-done | bytes 524320 | tf_op jit(solution)/shard_map/ppermute | solution.py:26
  42.0 4.3 %collective-permute-start.15 = (bf16[1024,256]{1,0:T(8,128)(2,1)S(1)}, bf16[1024,256]{1,0:T(8,128)(2,1)S(1)}, u32[]{:S(2)}, u32[]{:S(2)}) collective-permute-start(bf16[1024,256]{1,0:T(8,128)(2,1)S(1)} %collective-permute-done.7.rest_1_), channel_id=1, source_target_pairs={{0,1},{1,0},{2,3},{3,2},{4,5},{5,4},{6,7},{7,6},{8,9},{9,8},{10,11... | collective-permute-start | bytes 1572872 | tf_op jit(solution)/shard_map/ppermute | solution.py:26
  46.3 0.0 collective-permute-done.10.rest_5_
  46.3 0.0 collective-permute-start.14
  46.3 1.3 %collective-permute-done.12.rest_3_ = bf16[1024,256]{1,0:T(8,128)(2,1)S(1)} collective-permute-done((bf16[1024,256]{1,0:T(8,128)(2,1)S(1)}, bf16[1024,256]{1,0:T(8,128)(2,1)S(1)}, u32[]{:S(2)}, u32[]{:S(2)}) %collective-permute-start.12) | collective-permute-done | bytes 524320 | tf_op jit(solution)/shard_map/ppermute | solution.py:26
  47.6 4.3 %collective-permute-start.20 = (bf16[1024,256]{1,0:T(8,128)(2,1)S(1)}, bf16[1024,256]{1,0:T(8,128)(2,1)S(1)}, u32[]{:S(2)}, u32[]{:S(2)}) collective-permute-start(bf16[1024,256]{1,0:T(8,128)(2,1)S(1)} %collective-permute-done.8.rest_6_), channel_id=1, source_target_pairs={{0,1},{1,0},{2,3},{3,2},{4,5},{5,4},{6,7},{7,6},{8,9},{9,8},{10,11... | collective-permute-start | bytes 1572872 | tf_op jit(solution)/shard_map/ppermute | solution.py:26
  51.9 2.1 %collective-permute-start.17 = (bf16[1024,256]{1,0:T(8,128)(2,1)S(1)}, bf16[1024,256]{1,0:T(8,128)(2,1)S(1)}, u32[]{:S(2)}, u32[]{:S(2)}) collective-permute-start(bf16[1024,256]{1,0:T(8,128)(2,1)S(1)} %collective-permute-done.12.rest_3_), channel_id=1, source_target_pairs={{0,1},{1,0},{2,3},{3,2},{4,5},{5,4},{6,7},{7,6},{8,9},{9,8},{10,11... | collective-permute-start | bytes 1572872 | tf_op jit(solution)/shard_map/ppermute | solution.py:26
  54.0 0.0 collective-permute-done.11.tiles_ref
  54.0 0.0 collective-permute-start.18
  54.1 0.5 collective-permute-start.16
  54.6 0.0 collective-permute-done.20.rest_13_
  54.6 0.1 collective-permute-start.19
  54.7 0.0 collective-permute-done.14.rest_7_
  54.7 0.9 %collective-permute-done.17.rest_10_ = bf16[1024,256]{1,0:T(8,128)(2,1)S(1)} collective-permute-done((bf16[1024,256]{1,0:T(8,128)(2,1)S(1)}, bf16[1024,256]{1,0:T(8,128)(2,1)S(1)}, u32[]{:S(2)}, u32[]{:S(2)}) %collective-permute-start.17) | collective-permute-done | bytes 524320 | tf_op jit(solution)/shard_map/ppermute | solution.py:26
  55.6 0.7 %collective-permute-done.18.rest_11_ = bf16[1024,256]{1,0:T(8,128)(2,1)S(1)} collective-permute-done((bf16[1024,256]{1,0:T(8,128)(2,1)S(1)}, bf16[1024,256]{1,0:T(8,128)(2,1)S(1)}, u32[]{:S(2)}, u32[]{:S(2)}) %collective-permute-start.18) | collective-permute-done | bytes 524320 | tf_op jit(solution)/shard_map/ppermute | solution.py:26
  56.3 0.7 %collective-permute-done.16.rest_9_ = bf16[1024,256]{1,0:T(8,128)(2,1)S(1)} collective-permute-done((bf16[1024,256]{1,0:T(8,128)(2,1)S(1)}, bf16[1024,256]{1,0:T(8,128)(2,1)S(1)}, u32[]{:S(2)}, u32[]{:S(2)}) %collective-permute-start.16) | collective-permute-done | bytes 524320 | tf_op jit(solution)/shard_map/ppermute | solution.py:26
  57.1 0.7 %collective-permute-done.19.rest_12_ = bf16[1024,256]{1,0:T(8,128)(2,1)S(1)} collective-permute-done((bf16[1024,256]{1,0:T(8,128)(2,1)S(1)}, bf16[1024,256]{1,0:T(8,128)(2,1)S(1)}, u32[]{:S(2)}, u32[]{:S(2)}) %collective-permute-start.19) | collective-permute-done | bytes 524320 | tf_op jit(solution)/shard_map/ppermute | solution.py:26
  57.8 2.3 %shard_map.48 = f32[128,256]{1,0:T(8,128)S(1)} custom-call(s32[4,65]{1,0:T(4,128)S(1)} %shard_map.46.list_ref, bf16[8192,128]{1,0:T(8,128)(2,1)S(1)} %collective-permute-done.11.tiles_ref, bf16[2048,256]{1,0:T(8,128)(2,1)S(1)} %pad_maximum_fusion.rest_0_, bf16[1024,256]{1,0:T(8,128)(2,1)S(1)} %collective-permute-done.7.rest_1_, ...), custom_call_target="tpu_custom_call" | custom-call | flops 268435456 | bytes 3145728 | tf_op jit(solution)/shard_map/pallas_call | solution.py:127
  60.2 0.1 collective-permute-start.21
  60.3 2.0 %shard_map.47 = f32[128,256]{1,0:T(8,128)S(1)} custom-call(s32[4,65]{1,0:T(4,128)S(1)} %shard_map.46.list_ref, bf16[8192,128]{1,0:T(8,128)(2,1)S(1)} %bitcast.3, bf16[2048,256]{1,0:T(8,128)(2,1)S(1)} %pad_maximum_fusion.rest_0_, bf16[1024,256]{1,0:T(8,128)(2,1)S(1)} %collective-permute-done.7.rest_1_, bf16[1024,256]{1,0:T(8,128)(2,1)S(1)} %collective-permute-done.9.rest_2_, ...), custom_call_target="tpu_custom_call" | custom-call | flops 268435456 | bytes 3145728 | tf_op jit(solution)/shard_map/pallas_call | solution.py:127
  62.2 3.0 %collective-permute-done.21 = f32[128,256]{1,0:T(8,128)S(1)} collective-permute-done((f32[128,256]{1,0:T(8,128)S(1)}, f32[128,256]{1,0:T(8,128)S(1)}, u32[]{:S(2)}, u32[]{:S(2)}) %collective-permute-start.21) | collective-permute-done | bytes 131104 | tf_op jit(solution)/shard_map/ppermute | solution.py:26
  65.3 0.8 %fusion = bf16[128,256]{1,0:T(8,128)(2,1)} fusion(bf16[256,256]{1,0:T(8,128)(2,1)S(1)} %copy-done, f32[128,256]{1,0:T(8,128)S(1)} %shard_map.47, f32[128,256]{1,0:T(8,128)S(1)} %collective-permute-done.21), kind=kOutput, calls=%fused_computation.1 | convolution fusion | flops 16908288 | bytes 458752 | tf_op jit(solution)/shard_map/dot_general | solution.py:162
  (8 shorter events, 0.0 us)
Async XLA Ops:
  0.0 65.3 %copy-start = (bf16[256,256]{1,0:T(8,128)(2,1)S(1)}, bf16[256,256]{1,0:T(8,128)(2,1)}, u32[]{:S(2)}) copy-start(bf16[256,256]{1,0:T(8,128)(2,1)} %param.7) | copy-start | bytes 393220
  0.0 13.4 %collective-permute-start.1 = (bf16[128,256]{1,0:T(8,128)(2,1)}, bf16[128,256]{1,0:T(8,128)(2,1)S(1)}, u32[]{:S(2)}, u32[]{:S(2)}) collective-permute-start(bf16[128,256]{1,0:T(8,128)(2,1)} %param.4), channel_id=1, source_target_pairs={{0,64},{1,65},{2,66},{3,67},{4,68},{5,69},{6,70},{7,71},{8,72},{9,... | collective-permute-start | bytes 196616 | tf_op jit(solution)/shard_map/ppermute | solution.py:26
  7.7 7.6 %collective-permute-start = (bf16[128,256]{1,0:T(8,128)(2,1)}, bf16[128,256]{1,0:T(8,128)(2,1)S(1)}, u32[]{:S(2)}, u32[]{:S(2)}) collective-permute-start(bf16[128,256]{1,0:T(8,128)(2,1)} %param.4), channel_id=1, source_target_pairs={{0,96},{1,97},{2,98},{3,99},{4,100},{5,101},{6,102},{7,103},{8,104... | collective-permute-start | bytes 196616 | tf_op jit(solution)/shard_map/ppermute | solution.py:26
  7.7 7.6 %collective-permute-start.2 = (bf16[128,256]{1,0:T(8,128)(2,1)}, bf16[128,256]{1,0:T(8,128)(2,1)S(1)}, u32[]{:S(2)}, u32[]{:S(2)}) collective-permute-start(bf16[128,256]{1,0:T(8,128)(2,1)} %param.4), channel_id=1, source_target_pairs={{0,32},{1,33},{2,34},{3,35},{4,36},{5,37},{6,38},{7,39},{8,40},{9,... | collective-permute-start | bytes 196616 | tf_op jit(solution)/shard_map/ppermute | solution.py:26
  10.1 2.6 %collective-permute-start.3 = (s32[1,64]{1,0:T(1,128)}, s32[1,64]{1,0:T(1,128)S(1)}, u32[]{:S(2)}, u32[]{:S(2)}) collective-permute-start(s32[1,64]{1,0:T(1,128)} %param.6), channel_id=1, source_target_pairs={{0,16},{1,113},{2,18},{3,115},{4,20},{5,117},{6,22},{7,119},{8,24}... | collective-permute-start | bytes 776 | tf_op jit(solution)/shard_map/ppermute | solution.py:26
  16.2 7.1 %collective-permute-start.6 = (bf16[512,256]{1,0:T(8,128)(2,1)S(1)}, bf16[512,256]{1,0:T(8,128)(2,1)S(1)}, u32[]{:S(2)}, u32[]{:S(2)}) collective-permute-start(bf16[512,256]{1,0:T(8,128)(2,1)S(1)} %pad_maximum_fusion.1), channel_id=1, source_target_pairs={{0,2},{1,5},{2,128},{3,7},{4,6},{5,9},{6,132},{7,11},{8,10},{9,13}... | collective-permute-start | bytes 786440 | tf_op jit(solution)/shard_map/ppermute | solution.py:26
  17.5 9.3 %collective-permute-start.5 = (bf16[512,256]{1,0:T(8,128)(2,1)S(1)}, bf16[512,256]{1,0:T(8,128)(2,1)S(1)}, u32[]{:S(2)}, u32[]{:S(2)}) collective-permute-start(bf16[512,256]{1,0:T(8,128)(2,1)S(1)} %pad_maximum_fusion.1), channel_id=1, source_target_pairs={{0,128},{1,9},{2,130},{3,11},{4,132},{5,13},{6,134},{7,15},{8,136}... | collective-permute-start | bytes 786440 | tf_op jit(solution)/shard_map/ppermute | solution.py:26
  19.9 6.9 %collective-permute-start.4 = (bf16[512,256]{1,0:T(8,128)(2,1)S(1)}, bf16[512,256]{1,0:T(8,128)(2,1)S(1)}, u32[]{:S(2)}, u32[]{:S(2)}) collective-permute-start(bf16[512,256]{1,0:T(8,128)(2,1)S(1)} %pad_maximum_fusion.1), channel_id=1, source_target_pairs={{0,130},{1,13},{2,0},{3,15},{4,134},{5,1},{6,4},{7,3},{8,138},{9,5... | collective-permute-start | bytes 786440 | tf_op jit(solution)/shard_map/ppermute | solution.py:26
  21.1 33.0 %collective-permute-start.11 = (bf16[8192,128]{1,0:T(8,128)(2,1)}, bf16[8192,128]{1,0:T(8,128)(2,1)S(1)}, u32[]{:S(2)}, u32[]{:S(2)}) collective-permute-start(bf16[8192,128]{1,0:T(8,128)(2,1)} %bitcast.2), channel_id=1, source_target_pairs={{0,16},{1,113},{2,18},{3,115},{4,20},{5,117},{6,22},{7,119},{8,24}... | collective-permute-start | bytes 6291464 | tf_op jit(solution)/shard_map/ppermute | solution.py:26
  26.9 9.6 %collective-permute-start.8 = (bf16[1024,256]{1,0:T(8,128)(2,1)S(1)}, bf16[1024,256]{1,0:T(8,128)(2,1)S(1)}, u32[]{:S(2)}, u32[]{:S(2)}) collective-permute-start(bf16[1024,256]{1,0:T(8,128)(2,1)S(1)} %get-tuple-element.27), channel_id=1, source_target_pairs={{0,4},{1,3},{2,6},{3,129},{4,8},{5,7},{6,10},{7,133},{8,12},{9,11}... | collective-permute-start | bytes 1572872 | tf_op jit(solution)/shard_map/ppermute | solution.py:26
  28.0 8.5 %collective-permute-start.7 = (bf16[1024,256]{1,0:T(8,128)(2,1)S(1)}, bf16[1024,256]{1,0:T(8,128)(2,1)S(1)}, u32[]{:S(2)}, u32[]{:S(2)}) collective-permute-start(bf16[1024,256]{1,0:T(8,128)(2,1)S(1)} %get-tuple-element.28), channel_id=1, source_target_pairs={{0,12},{1,131},{2,14},{3,1},{4,0},{5,135},{6,2},{7,5},{8,4},{9,139... | collective-permute-start | bytes 1572872 | tf_op jit(solution)/shard_map/ppermute | solution.py:26
  29.7 12.3 %collective-permute-start.9 = (bf16[1024,256]{1,0:T(8,128)(2,1)S(1)}, bf16[1024,256]{1,0:T(8,128)(2,1)S(1)}, u32[]{:S(2)}, u32[]{:S(2)}) collective-permute-start(bf16[1024,256]{1,0:T(8,128)(2,1)S(1)} %get-tuple-element.27), channel_id=1, source_target_pairs={{0,12},{1,131},{2,14},{3,1},{4,0},{5,135},{6,2},{7,5},{8,4},{9,139... | collective-permute-start | bytes 1572872 | tf_op jit(solution)/shard_map/ppermute | solution.py:26
  30.9 15.4 %collective-permute-start.10 = (bf16[1024,256]{1,0:T(8,128)(2,1)S(1)}, bf16[1024,256]{1,0:T(8,128)(2,1)S(1)}, u32[]{:S(2)}, u32[]{:S(2)}) collective-permute-start(bf16[1024,256]{1,0:T(8,128)(2,1)S(1)} %get-tuple-element.28), channel_id=1, source_target_pairs={{0,4},{1,3},{2,6},{3,129},{4,8},{5,7},{6,10},{7,133},{8,12},{9,11}... | collective-permute-start | bytes 1572872 | tf_op jit(solution)/shard_map/ppermute | solution.py:26
  33.9 26.4 %copy-start.1 = (bf16[1,64,128,128]{3,2,1,0:T(8,128)(2,1)S(1)}, bf16[1,64,128,128]{3,2,1,0:T(8,128)(2,1)}, u32[]{:S(2)}) copy-start(bf16[1,64,128,128]{3,2,1,0:T(8,128)(2,1)} %param.5) | copy-start | bytes 6291460
  36.6 11.0 %collective-permute-start.12 = (bf16[1024,256]{1,0:T(8,128)(2,1)S(1)}, bf16[1024,256]{1,0:T(8,128)(2,1)S(1)}, u32[]{:S(2)}, u32[]{:S(2)}) collective-permute-start(bf16[1024,256]{1,0:T(8,128)(2,1)S(1)} %collective-permute-done.7.rest_1_), channel_id=1, source_target_pairs={{0,12},{1,131},{2,14},{3,1},{4,0},{5,135},{6,2},{7,5},{8,4},{9,139... | collective-permute-start | bytes 1572872 | tf_op jit(solution)/shard_map/ppermute | solution.py:26
  39.2 12.7 %collective-permute-start.13 = (bf16[1024,256]{1,0:T(8,128)(2,1)S(1)}, bf16[1024,256]{1,0:T(8,128)(2,1)S(1)}, u32[]{:S(2)}, u32[]{:S(2)}) collective-permute-start(bf16[1024,256]{1,0:T(8,128)(2,1)S(1)} %collective-permute-done.8.rest_6_), channel_id=1, source_target_pairs={{0,4},{1,3},{2,6},{3,129},{4,8},{5,7},{6,10},{7,133},{8,12},{9,11}... | collective-permute-start | bytes 1572872 | tf_op jit(solution)/shard_map/ppermute | solution.py:26
  42.0 12.1 %collective-permute-start.15 = (bf16[1024,256]{1,0:T(8,128)(2,1)S(1)}, bf16[1024,256]{1,0:T(8,128)(2,1)S(1)}, u32[]{:S(2)}, u32[]{:S(2)}) collective-permute-start(bf16[1024,256]{1,0:T(8,128)(2,1)S(1)} %collective-permute-done.7.rest_1_), channel_id=1, source_target_pairs={{0,1},{1,0},{2,3},{3,2},{4,5},{5,4},{6,7},{7,6},{8,9},{9,8},{10,11... | collective-permute-start | bytes 1572872 | tf_op jit(solution)/shard_map/ppermute | solution.py:26
  46.3 8.3 %collective-permute-start.14 = (bf16[2048,256]{1,0:T(8,128)(2,1)S(1)}, bf16[2048,256]{1,0:T(8,128)(2,1)S(1)}, u32[]{:S(2)}, u32[]{:S(2)}) collective-permute-start(bf16[2048,256]{1,0:T(8,128)(2,1)S(1)} %pad_maximum_fusion.rest_0_), channel_id=1, source_target_pairs={{0,1},{1,0},{2,3},{3,2},{4,5},{5,4},{6,7},{7,6},{8,9},{9,8},{10,11... | collective-permute-start | bytes 3145736 | tf_op jit(solution)/shard_map/ppermute | solution.py:26
  47.6 7.0 %collective-permute-start.20 = (bf16[1024,256]{1,0:T(8,128)(2,1)S(1)}, bf16[1024,256]{1,0:T(8,128)(2,1)S(1)}, u32[]{:S(2)}, u32[]{:S(2)}) collective-permute-start(bf16[1024,256]{1,0:T(8,128)(2,1)S(1)} %collective-permute-done.8.rest_6_), channel_id=1, source_target_pairs={{0,1},{1,0},{2,3},{3,2},{4,5},{5,4},{6,7},{7,6},{8,9},{9,8},{10,11... | collective-permute-start | bytes 1572872 | tf_op jit(solution)/shard_map/ppermute | solution.py:26
  51.9 3.6 %collective-permute-start.17 = (bf16[1024,256]{1,0:T(8,128)(2,1)S(1)}, bf16[1024,256]{1,0:T(8,128)(2,1)S(1)}, u32[]{:S(2)}, u32[]{:S(2)}) collective-permute-start(bf16[1024,256]{1,0:T(8,128)(2,1)S(1)} %collective-permute-done.12.rest_3_), channel_id=1, source_target_pairs={{0,1},{1,0},{2,3},{3,2},{4,5},{5,4},{6,7},{7,6},{8,9},{9,8},{10,11... | collective-permute-start | bytes 1572872 | tf_op jit(solution)/shard_map/ppermute | solution.py:26
  54.0 2.3 %collective-permute-start.18 = (bf16[1024,256]{1,0:T(8,128)(2,1)S(1)}, bf16[1024,256]{1,0:T(8,128)(2,1)S(1)}, u32[]{:S(2)}, u32[]{:S(2)}) collective-permute-start(bf16[1024,256]{1,0:T(8,128)(2,1)S(1)} %collective-permute-done.13.rest_4_), channel_id=1, source_target_pairs={{0,1},{1,0},{2,3},{3,2},{4,5},{5,4},{6,7},{7,6},{8,9},{9,8},{10,11... | collective-permute-start | bytes 1572872 | tf_op jit(solution)/shard_map/ppermute | solution.py:26
  54.1 3.0 %collective-permute-start.16 = (bf16[1024,256]{1,0:T(8,128)(2,1)S(1)}, bf16[1024,256]{1,0:T(8,128)(2,1)S(1)}, u32[]{:S(2)}, u32[]{:S(2)}) collective-permute-start(bf16[1024,256]{1,0:T(8,128)(2,1)S(1)} %collective-permute-done.9.rest_2_), channel_id=1, source_target_pairs={{0,1},{1,0},{2,3},{3,2},{4,5},{5,4},{6,7},{7,6},{8,9},{9,8},{10,11... | collective-permute-start | bytes 1572872 | tf_op jit(solution)/shard_map/ppermute | solution.py:26
  54.6 3.3 %collective-permute-start.19 = (bf16[1024,256]{1,0:T(8,128)(2,1)S(1)}, bf16[1024,256]{1,0:T(8,128)(2,1)S(1)}, u32[]{:S(2)}, u32[]{:S(2)}) collective-permute-start(bf16[1024,256]{1,0:T(8,128)(2,1)S(1)} %collective-permute-done.10.rest_5_), channel_id=1, source_target_pairs={{0,1},{1,0},{2,3},{3,2},{4,5},{5,4},{6,7},{7,6},{8,9},{9,8},{10,11... | collective-permute-start | bytes 1572872 | tf_op jit(solution)/shard_map/ppermute | solution.py:26
  60.2 5.1 %collective-permute-start.21 = (f32[128,256]{1,0:T(8,128)S(1)}, f32[128,256]{1,0:T(8,128)S(1)}, u32[]{:S(2)}, u32[]{:S(2)}) collective-permute-start(f32[128,256]{1,0:T(8,128)S(1)} %shard_map.48), channel_id=1, source_target_pairs={{0,112},{1,17},{2,114},{3,19},{4,116},{5,21},{6,118},{7,23},{8,120... | collective-permute-start | bytes 393224 | tf_op jit(solution)/shard_map/ppermute | solution.py:26

commit v7 on v6

--- a/solution.py
+++ b/solution.py
@@ -14,7 +14,7 @@
 TILES = 64
 PLANE = 16
 BUFFERS = 7
-BATCH = 8
+BATCH = 12
 
 
 def move(a, target):
@@ -146,12 +146,11 @@
     line, place, sent = together(line, place, mine)
     lent = from_lender(sent)
     plane = jnp.concatenate([line] + [from_middle(line, d) for d in (1, 2, 3)], axis=0)
-    plane, place = together(plane, place)
-    lists = listed(place)
+    plane, lists = together(plane, listed(place))
     half = PLANE // 2 * SIDE
     low, high = plane[:half], plane[half:]
     after_low, before_high = from_last(low, 1), from_last(high, -1)
-    after_low, before_high, lists = together(after_low, before_high, lists)
+    after_low, before_high = together(after_low, before_high)
     after_high, before_low = from_last(high, 1), from_last(low, -1)
     after_high, before_low, lent = together(after_high, before_low, lent)
     buffers = [plane, after_low, after_high, from_last(after_low, 1), from_last(before_high, -1), before_low, before_high]

time: 66 us -> 65.8 us (level)
  waiting for transfers between devices: 19.8 us -> 18.6 us
  starting transfers between devices: 36.6 us -> 37.5 us
    ppermute x22, waiting for transfers between devices: 19.8 us -> 18.6 us  [move(): return lax.ppermute(a, AXES, found)]
    ppermute x22, starting transfers between devices: 36.6 us -> 37.5 us  [move(): return lax.ppermute(a, AXES, found)]
  transfers between devices with their start and end apart: 22 -> 22, of which waited for: 11 -> 11; matrix products, arithmetic and copies ran while one was open for 1% -> 1% of each run, Pallas kernels for 7% -> 8%
where the time goes in v7:
time: 65.8 us; the launch traced here: 65.7 us
  starting transfers between devices  37.5 us (57%)
  waiting for transfers between devices  18.6 us (28%)
  Pallas kernels  7.01 us (11%)
  other arithmetic  1.6 us (2%)
  matrix products  0.8 us (1%)
    ppermute x22, starting transfers between devices, move(): return lax.ppermute(a, AXES, found)  37.5 us
    ppermute x22, waiting for transfers between devices, move(): return lax.ppermute(a, AXES, found)  18.6 us
    pallas_call x2, Pallas kernels, multiply(): pl.pallas_call(kernel, out_shape=jax.ShapeDtypeStruct((SIDE, WIDTH), jnp....  4.3 us
    pallas_call x1, Pallas kernels, listed(): pl.pallas_call(list_kernel, out_shape=jax.ShapeDtypeStruct((4, TILES + 1)...  2.71 us
  transfers between devices with their start and end apart: 22, of which 11 were waited for; matrix products, arithmetic and copies ran while one was open for 1% of the time, Pallas kernels for 8%

profile of v7, /device:TPU:1, one launch (start us, length us, event | category | flops | bytes accessed | tf_op | source)
XLA Modules:
  0.0 65.7 jit_solution(13108634839082021376)
XLA Ops:
  0.0 7.7 %collective-permute-start.1 = (bf16[128,256]{1,0:T(8,128)(2,1)}, bf16[128,256]{1,0:T(8,128)(2,1)S(1)}, u32[]{:S(2)}, u32[]{:S(2)}) collective-permute-start(bf16[128,256]{1,0:T(8,128)(2,1)} %param.4), channel_id=1, source_target_pairs={{0,64},{1,65},{2,66},{3,67},{4,68},{5,69},{6,70},{7,71},{8,72},{9,... | collective-permute-start | bytes 196616 | tf_op jit(solution)/shard_map/ppermute | solution.py:26
  7.7 0.0 collective-permute-start
  7.7 2.4 %collective-permute-start.2 = (bf16[128,256]{1,0:T(8,128)(2,1)}, bf16[128,256]{1,0:T(8,128)(2,1)S(1)}, u32[]{:S(2)}, u32[]{:S(2)}) collective-permute-start(bf16[128,256]{1,0:T(8,128)(2,1)} %param.4), channel_id=1, source_target_pairs={{0,32},{1,33},{2,34},{3,35},{4,36},{5,37},{6,38},{7,39},{8,40},{9,... | collective-permute-start | bytes 196616 | tf_op jit(solution)/shard_map/ppermute | solution.py:26
  10.1 1.0 %collective-permute-start.3 = (s32[1,64]{1,0:T(1,128)}, s32[1,64]{1,0:T(1,128)S(1)}, u32[]{:S(2)}, u32[]{:S(2)}) collective-permute-start(s32[1,64]{1,0:T(1,128)} %param.6), channel_id=1, source_target_pairs={{0,16},{1,113},{2,18},{3,115},{4,20},{5,117},{6,22},{7,119},{8,24}... | collective-permute-start | bytes 776 | tf_op jit(solution)/shard_map/ppermute | solution.py:26
  11.1 1.6 %collective-permute-done.3 = s32[1,64]{1,0:T(1,128)S(1)} collective-permute-done((s32[1,64]{1,0:T(1,128)}, s32[1,64]{1,0:T(1,128)S(1)}, u32[]{:S(2)}, u32[]{:S(2)}) %collective-permute-start.3) | collective-permute-done | bytes 288 | tf_op jit(solution)/shard_map/ppermute | solution.py:26
  12.7 0.7 %compare_select_fusion.1.place_ref = s32[2,64]{1,0:T(2,128)S(1)} fusion(s32[1,64]{1,0:T(1,128)S(1)} %collective-permute-done.3, s32[1,64]{1,0:T(1,128)} %param.6, s32[]{:T(128)S(6)} %axis_index.77, s32[]{:T(128)S(6)} %add.23, s32[]{:T(128)S(6)} %axis_index.68, s32[]{:T(128)S(6)} %axis_index.65, s32[]{:T(128)S(6)} %axis_index.63), kind=kLoop, calls=%fused_computation.6 | loop fusion | flops 4736 | bytes 1044 | tf_op jit(solution)/shard_map/jit(_where)/select_n | solution.py:65
  13.4 0.0 collective-permute-done.1
  13.4 1.9 %collective-permute-done = bf16[128,256]{1,0:T(8,128)(2,1)S(1)} collective-permute-done((bf16[128,256]{1,0:T(8,128)(2,1)}, bf16[128,256]{1,0:T(8,128)(2,1)S(1)}, u32[]{:S(2)}, u32[]{:S(2)}) %collective-permute-start) | collective-permute-done | bytes 65568 | tf_op jit(solution)/shard_map/ppermute | solution.py:26
  15.3 0.0 collective-permute-done.2
  15.3 0.9 %pad_maximum_fusion.1 = bf16[512,256]{1,0:T(8,128)(2,1)S(1)} fusion(bf16[128,256]{1,0:T(8,128)(2,1)S(1)} %collective-permute-done.2, bf16[128,256]{1,0:T(8,128)(2,1)S(1)} %collective-permute-done.1, bf16[128,256]{1,0:T(8,128)(2,1)S(1)} %collective-permute-done, bf16[128,256]{1,0:T(8,128)(2,1)} %param.4), kind=kLoop, calls=%fused_computation.3 | loop fusion | flops 1048576 | bytes 524288 | tf_op jit(solution)/shard_map/concatenate | solution.py:145
  16.2 1.3 %collective-permute-start.6 = (bf16[512,256]{1,0:T(8,128)(2,1)S(1)}, bf16[512,256]{1,0:T(8,128)(2,1)S(1)}, u32[]{:S(2)}, u32[]{:S(2)}) collective-permute-start(bf16[512,256]{1,0:T(8,128)(2,1)S(1)} %pad_maximum_fusion.1), channel_id=1, source_target_pairs={{0,2},{1,5},{2,128},{3,7},{4,6},{5,9},{6,132},{7,11},{8,10},{9,13}... | collective-permute-start | bytes 786440 | tf_op jit(solution)/shard_map/ppermute | solution.py:26
  17.5 2.5 %collective-permute-start.5 = (bf16[512,256]{1,0:T(8,128)(2,1)S(1)}, bf16[512,256]{1,0:T(8,128)(2,1)S(1)}, u32[]{:S(2)}, u32[]{:S(2)}) collective-permute-start(bf16[512,256]{1,0:T(8,128)(2,1)S(1)} %pad_maximum_fusion.1), channel_id=1, source_target_pairs={{0,128},{1,9},{2,130},{3,11},{4,132},{5,13},{6,134},{7,15},{8,136}... | collective-permute-start | bytes 786440 | tf_op jit(solution)/shard_map/ppermute | solution.py:26
  19.9 1.2 %collective-permute-start.4 = (bf16[512,256]{1,0:T(8,128)(2,1)S(1)}, bf16[512,256]{1,0:T(8,128)(2,1)S(1)}, u32[]{:S(2)}, u32[]{:S(2)}) collective-permute-start(bf16[512,256]{1,0:T(8,128)(2,1)S(1)} %pad_maximum_fusion.1), channel_id=1, source_target_pairs={{0,130},{1,13},{2,0},{3,15},{4,134},{5,1},{6,4},{7,3},{8,138},{9,5... | collective-permute-start | bytes 786440 | tf_op jit(solution)/shard_map/ppermute | solution.py:26
  21.1 2.2 %collective-permute-start.11 = (bf16[8192,128]{1,0:T(8,128)(2,1)}, bf16[8192,128]{1,0:T(8,128)(2,1)S(1)}, u32[]{:S(2)}, u32[]{:S(2)}) collective-permute-start(bf16[8192,128]{1,0:T(8,128)(2,1)} %bitcast.2), channel_id=1, source_target_pairs={{0,16},{1,113},{2,18},{3,115},{4,20},{5,117},{6,22},{7,119},{8,24}... | collective-permute-start | bytes 6291464 | tf_op jit(solution)/shard_map/ppermute | solution.py:26
  23.3 2.7 %shard_map.46.list_ref = s32[4,65]{1,0:T(4,128)S(1)} custom-call(s32[2,64]{1,0:T(2,128)S(1)} %compare_select_fusion.1.place_ref), custom_call_target="tpu_custom_call" | custom-call | tf_op jit(solution)/shard_map/pallas_call | solution.py:85
  26.0 0.0 collective-permute-done.6
  26.0 0.8 %collective-permute-done.5 = bf16[512,256]{1,0:T(8,128)(2,1)S(1)} collective-permute-done((bf16[512,256]{1,0:T(8,128)(2,1)S(1)}, bf16[512,256]{1,0:T(8,128)(2,1)S(1)}, u32[]{:S(2)}, u32[]{:S(2)}) %collective-permute-start.5) | collective-permute-done | bytes 262176 | tf_op jit(solution)/shard_map/ppermute | solution.py:26
  26.8 0.1 pad_maximum_fusion.rest_0_
  26.9 0.1 fusion.4
  26.9 1.1 %collective-permute-start.8 = (bf16[1024,256]{1,0:T(8,128)(2,1)S(1)}, bf16[1024,256]{1,0:T(8,128)(2,1)S(1)}, u32[]{:S(2)}, u32[]{:S(2)}) collective-permute-start(bf16[1024,256]{1,0:T(8,128)(2,1)S(1)} %get-tuple-element.25), channel_id=1, source_target_pairs={{0,4},{1,3},{2,6},{3,129},{4,8},{5,7},{6,10},{7,133},{8,12},{9,11}... | collective-permute-start | bytes 1572872 | tf_op jit(solution)/shard_map/ppermute | solution.py:26
  28.0 1.7 %collective-permute-start.7 = (bf16[1024,256]{1,0:T(8,128)(2,1)S(1)}, bf16[1024,256]{1,0:T(8,128)(2,1)S(1)}, u32[]{:S(2)}, u32[]{:S(2)}) collective-permute-start(bf16[1024,256]{1,0:T(8,128)(2,1)S(1)} %get-tuple-element.26), channel_id=1, source_target_pairs={{0,12},{1,131},{2,14},{3,1},{4,0},{5,135},{6,2},{7,5},{8,4},{9,139... | collective-permute-start | bytes 1572872 | tf_op jit(solution)/shard_map/ppermute | solution.py:26
  29.7 1.2 %collective-permute-start.9 = (bf16[1024,256]{1,0:T(8,128)(2,1)S(1)}, bf16[1024,256]{1,0:T(8,128)(2,1)S(1)}, u32[]{:S(2)}, u32[]{:S(2)}) collective-permute-start(bf16[1024,256]{1,0:T(8,128)(2,1)S(1)} %get-tuple-element.25), channel_id=1, source_target_pairs={{0,12},{1,131},{2,14},{3,1},{4,0},{5,135},{6,2},{7,5},{8,4},{9,139... | collective-permute-start | bytes 1572872 | tf_op jit(solution)/shard_map/ppermute | solution.py:26
  30.9 0.2 collective-permute-start.10
  31.2 5.4 %collective-permute-done.8.rest_6_ = bf16[1024,256]{1,0:T(8,128)(2,1)S(1)} collective-permute-done((bf16[1024,256]{1,0:T(8,128)(2,1)S(1)}, bf16[1024,256]{1,0:T(8,128)(2,1)S(1)}, u32[]{:S(2)}, u32[]{:S(2)}) %collective-permute-start.8) | collective-permute-done | bytes 524320 | tf_op jit(solution)/shard_map/ppermute | solution.py:26
  36.6 0.0 collective-permute-done.7.rest_1_
  36.6 2.7 %collective-permute-start.12 = (bf16[1024,256]{1,0:T(8,128)(2,1)S(1)}, bf16[1024,256]{1,0:T(8,128)(2,1)S(1)}, u32[]{:S(2)}, u32[]{:S(2)}) collective-permute-start(bf16[1024,256]{1,0:T(8,128)(2,1)S(1)} %collective-permute-done.7.rest_1_), channel_id=1, source_target_pairs={{0,12},{1,131},{2,14},{3,1},{4,0},{5,135},{6,2},{7,5},{8,4},{9,139... | collective-permute-start | bytes 1572872 | tf_op jit(solution)/shard_map/ppermute | solution.py:26
  39.2 2.7 %collective-permute-done.9.rest_2_ = bf16[1024,256]{1,0:T(8,128)(2,1)S(1)} collective-permute-done((bf16[1024,256]{1,0:T(8,128)(2,1)S(1)}, bf16[1024,256]{1,0:T(8,128)(2,1)S(1)}, u32[]{:S(2)}, u32[]{:S(2)}) %collective-permute-start.9) | collective-permute-done | bytes 524320 | tf_op jit(solution)/shard_map/ppermute | solution.py:26
  42.0 4.3 %collective-permute-start.15 = (bf16[1024,256]{1,0:T(8,128)(2,1)S(1)}, bf16[1024,256]{1,0:T(8,128)(2,1)S(1)}, u32[]{:S(2)}, u32[]{:S(2)}) collective-permute-start(bf16[1024,256]{1,0:T(8,128)(2,1)S(1)} %collective-permute-done.7.rest_1_), channel_id=1, source_target_pairs={{0,1},{1,0},{2,3},{3,2},{4,5},{5,4},{6,7},{7,6},{8,9},{9,8},{10,11... | collective-permute-start | bytes 1572872 | tf_op jit(solution)/shard_map/ppermute | solution.py:26
  46.3 0.0 collective-permute-start.14
  46.3 1.3 %collective-permute-done.12.rest_3_ = bf16[1024,256]{1,0:T(8,128)(2,1)S(1)} collective-permute-done((bf16[1024,256]{1,0:T(8,128)(2,1)S(1)}, bf16[1024,256]{1,0:T(8,128)(2,1)S(1)}, u32[]{:S(2)}, u32[]{:S(2)}) %collective-permute-start.12) | collective-permute-done | bytes 524320 | tf_op jit(solution)/shard_map/ppermute | solution.py:26
  47.6 4.3 %collective-permute-start.20 = (bf16[1024,256]{1,0:T(8,128)(2,1)S(1)}, bf16[1024,256]{1,0:T(8,128)(2,1)S(1)}, u32[]{:S(2)}, u32[]{:S(2)}) collective-permute-start(bf16[1024,256]{1,0:T(8,128)(2,1)S(1)} %collective-permute-done.8.rest_6_), channel_id=1, source_target_pairs={{0,1},{1,0},{2,3},{3,2},{4,5},{5,4},{6,7},{7,6},{8,9},{9,8},{10,11... | collective-permute-start | bytes 1572872 | tf_op jit(solution)/shard_map/ppermute | solution.py:26
  51.9 0.0 collective-permute-done.13.rest_4_
  51.9 2.1 %collective-permute-start.17 = (bf16[1024,256]{1,0:T(8,128)(2,1)S(1)}, bf16[1024,256]{1,0:T(8,128)(2,1)S(1)}, u32[]{:S(2)}, u32[]{:S(2)}) collective-permute-start(bf16[1024,256]{1,0:T(8,128)(2,1)S(1)} %collective-permute-done.12.rest_3_), channel_id=1, source_target_pairs={{0,1},{1,0},{2,3},{3,2},{4,5},{5,4},{6,7},{7,6},{8,9},{9,8},{10,11... | collective-permute-start | bytes 1572872 | tf_op jit(solution)/shard_map/ppermute | solution.py:26
  54.0 0.0 collective-permute-done.11.tiles_ref
  54.1 0.0 collective-permute-start.18
  54.1 0.5 collective-permute-start.16
  54.6 0.0 collective-permute-done.20.rest_13_
  54.6 0.1 collective-permute-start.19
  54.7 0.0 collective-permute-done.14.rest_7_
  54.7 0.9 %collective-permute-done.17.rest_10_ = bf16[1024,256]{1,0:T(8,128)(2,1)S(1)} collective-permute-done((bf16[1024,256]{1,0:T(8,128)(2,1)S(1)}, bf16[1024,256]{1,0:T(8,128)(2,1)S(1)}, u32[]{:S(2)}, u32[]{:S(2)}) %collective-permute-start.17) | collective-permute-done | bytes 524320 | tf_op jit(solution)/shard_map/ppermute | solution.py:26
  55.6 0.7 %collective-permute-done.18.rest_11_ = bf16[1024,256]{1,0:T(8,128)(2,1)S(1)} collective-permute-done((bf16[1024,256]{1,0:T(8,128)(2,1)S(1)}, bf16[1024,256]{1,0:T(8,128)(2,1)S(1)}, u32[]{:S(2)}, u32[]{:S(2)}) %collective-permute-start.18) | collective-permute-done | bytes 524320 | tf_op jit(solution)/shard_map/ppermute | solution.py:26
  56.3 0.7 %collective-permute-done.16.rest_9_ = bf16[1024,256]{1,0:T(8,128)(2,1)S(1)} collective-permute-done((bf16[1024,256]{1,0:T(8,128)(2,1)S(1)}, bf16[1024,256]{1,0:T(8,128)(2,1)S(1)}, u32[]{:S(2)}, u32[]{:S(2)}) %collective-permute-start.16) | collective-permute-done | bytes 524320 | tf_op jit(solution)/shard_map/ppermute | solution.py:26
  57.1 0.7 %collective-permute-done.19.rest_12_ = bf16[1024,256]{1,0:T(8,128)(2,1)S(1)} collective-permute-done((bf16[1024,256]{1,0:T(8,128)(2,1)S(1)}, bf16[1024,256]{1,0:T(8,128)(2,1)S(1)}, u32[]{:S(2)}, u32[]{:S(2)}) %collective-permute-start.19) | collective-permute-done | bytes 524320 | tf_op jit(solution)/shard_map/ppermute | solution.py:26
  57.8 1.9 %shard_map.48 = f32[128,256]{1,0:T(8,128)S(1)} custom-call(s32[4,65]{1,0:T(4,128)S(1)} %shard_map.46.list_ref, bf16[8192,128]{1,0:T(8,128)(2,1)S(1)} %collective-permute-done.11.tiles_ref, bf16[2048,256]{1,0:T(8,128)(2,1)S(1)} %pad_maximum_fusion.rest_0_, bf16[1024,256]{1,0:T(8,128)(2,1)S(1)} %collective-permute-done.7.rest_1_, ...), custom_call_target="tpu_custom_call" | custom-call | flops 268435456 | bytes 3145728 | tf_op jit(solution)/shard_map/pallas_call | solution.py:127
  59.8 0.9 %collective-permute-start.21 = (f32[128,256]{1,0:T(8,128)S(1)}, f32[128,256]{1,0:T(8,128)S(1)}, u32[]{:S(2)}, u32[]{:S(2)}) collective-permute-start(f32[128,256]{1,0:T(8,128)S(1)} %shard_map.48), channel_id=1, source_target_pairs={{0,112},{1,17},{2,114},{3,19},{4,116},{5,21},{6,118},{7,23},{8,120... | collective-permute-start | bytes 393224 | tf_op jit(solution)/shard_map/ppermute | solution.py:26
  60.7 2.4 %shard_map.47 = f32[128,256]{1,0:T(8,128)S(1)} custom-call(s32[4,65]{1,0:T(4,128)S(1)} %shard_map.46.list_ref, bf16[8192,128]{1,0:T(8,128)(2,1)S(1)} %bitcast.3, bf16[2048,256]{1,0:T(8,128)(2,1)S(1)} %pad_maximum_fusion.rest_0_, bf16[1024,256]{1,0:T(8,128)(2,1)S(1)} %collective-permute-done.7.rest_1_, bf16[1024,256]{1,0:T(8,128)(2,1)S(1)} %collective-permute-done.9.rest_2_, ...), custom_call_target="tpu_custom_call" | custom-call | flops 268435456 | bytes 3145728 | tf_op jit(solution)/shard_map/pallas_call | solution.py:127
  63.1 1.8 %collective-permute-done.21 = f32[128,256]{1,0:T(8,128)S(1)} collective-permute-done((f32[128,256]{1,0:T(8,128)S(1)}, f32[128,256]{1,0:T(8,128)S(1)}, u32[]{:S(2)}, u32[]{:S(2)}) %collective-permute-start.21) | collective-permute-done | bytes 131104 | tf_op jit(solution)/shard_map/ppermute | solution.py:26
  64.9 0.8 %fusion = bf16[128,256]{1,0:T(8,128)(2,1)} fusion(bf16[256,256]{1,0:T(8,128)(2,1)S(1)} %copy-done, f32[128,256]{1,0:T(8,128)S(1)} %shard_map.47, f32[128,256]{1,0:T(8,128)S(1)} %collective-permute-done.21), kind=kOutput, calls=%fused_computation.1 | convolution fusion | flops 16908288 | bytes 458752 | tf_op jit(solution)/shard_map/dot_general | solution.py:161
  (8 shorter events, 0.0 us)
Async XLA Ops:
  0.0 64.9 %copy-start = (bf16[256,256]{1,0:T(8,128)(2,1)S(1)}, bf16[256,256]{1,0:T(8,128)(2,1)}, u32[]{:S(2)}) copy-start(bf16[256,256]{1,0:T(8,128)(2,1)} %param.7) | copy-start | bytes 393220
  0.0 13.4 %collective-permute-start.1 = (bf16[128,256]{1,0:T(8,128)(2,1)}, bf16[128,256]{1,0:T(8,128)(2,1)S(1)}, u32[]{:S(2)}, u32[]{:S(2)}) collective-permute-start(bf16[128,256]{1,0:T(8,128)(2,1)} %param.4), channel_id=1, source_target_pairs={{0,64},{1,65},{2,66},{3,67},{4,68},{5,69},{6,70},{7,71},{8,72},{9,... | collective-permute-start | bytes 196616 | tf_op jit(solution)/shard_map/ppermute | solution.py:26
  7.7 7.6 %collective-permute-start = (bf16[128,256]{1,0:T(8,128)(2,1)}, bf16[128,256]{1,0:T(8,128)(2,1)S(1)}, u32[]{:S(2)}, u32[]{:S(2)}) collective-permute-start(bf16[128,256]{1,0:T(8,128)(2,1)} %param.4), channel_id=1, source_target_pairs={{0,96},{1,97},{2,98},{3,99},{4,100},{5,101},{6,102},{7,103},{8,104... | collective-permute-start | bytes 196616 | tf_op jit(solution)/shard_map/ppermute | solution.py:26
  7.7 7.6 %collective-permute-start.2 = (bf16[128,256]{1,0:T(8,128)(2,1)}, bf16[128,256]{1,0:T(8,128)(2,1)S(1)}, u32[]{:S(2)}, u32[]{:S(2)}) collective-permute-start(bf16[128,256]{1,0:T(8,128)(2,1)} %param.4), channel_id=1, source_target_pairs={{0,32},{1,33},{2,34},{3,35},{4,36},{5,37},{6,38},{7,39},{8,40},{9,... | collective-permute-start | bytes 196616 | tf_op jit(solution)/shard_map/ppermute | solution.py:26
  10.1 2.6 %collective-permute-start.3 = (s32[1,64]{1,0:T(1,128)}, s32[1,64]{1,0:T(1,128)S(1)}, u32[]{:S(2)}, u32[]{:S(2)}) collective-permute-start(s32[1,64]{1,0:T(1,128)} %param.6), channel_id=1, source_target_pairs={{0,16},{1,113},{2,18},{3,115},{4,20},{5,117},{6,22},{7,119},{8,24}... | collective-permute-start | bytes 776 | tf_op jit(solution)/shard_map/ppermute | solution.py:26
  16.2 9.8 %collective-permute-start.6 = (bf16[512,256]{1,0:T(8,128)(2,1)S(1)}, bf16[512,256]{1,0:T(8,128)(2,1)S(1)}, u32[]{:S(2)}, u32[]{:S(2)}) collective-permute-start(bf16[512,256]{1,0:T(8,128)(2,1)S(1)} %pad_maximum_fusion.1), channel_id=1, source_target_pairs={{0,2},{1,5},{2,128},{3,7},{4,6},{5,9},{6,132},{7,11},{8,10},{9,13}... | collective-permute-start | bytes 786440 | tf_op jit(solution)/shard_map/ppermute | solution.py:26
  17.5 9.3 %collective-permute-start.5 = (bf16[512,256]{1,0:T(8,128)(2,1)S(1)}, bf16[512,256]{1,0:T(8,128)(2,1)S(1)}, u32[]{:S(2)}, u32[]{:S(2)}) collective-permute-start(bf16[512,256]{1,0:T(8,128)(2,1)S(1)} %pad_maximum_fusion.1), channel_id=1, source_target_pairs={{0,128},{1,9},{2,130},{3,11},{4,132},{5,13},{6,134},{7,15},{8,136}... | collective-permute-start | bytes 786440 | tf_op jit(solution)/shard_map/ppermute | solution.py:26
  19.9 6.9 %collective-permute-start.4 = (bf16[512,256]{1,0:T(8,128)(2,1)S(1)}, bf16[512,256]{1,0:T(8,128)(2,1)S(1)}, u32[]{:S(2)}, u32[]{:S(2)}) collective-permute-start(bf16[512,256]{1,0:T(8,128)(2,1)S(1)} %pad_maximum_fusion.1), channel_id=1, source_target_pairs={{0,130},{1,13},{2,0},{3,15},{4,134},{5,1},{6,4},{7,3},{8,138},{9,5... | collective-permute-start | bytes 786440 | tf_op jit(solution)/shard_map/ppermute | solution.py:26
  21.1 33.0 %collective-permute-start.11 = (bf16[8192,128]{1,0:T(8,128)(2,1)}, bf16[8192,128]{1,0:T(8,128)(2,1)S(1)}, u32[]{:S(2)}, u32[]{:S(2)}) collective-permute-start(bf16[8192,128]{1,0:T(8,128)(2,1)} %bitcast.2), channel_id=1, source_target_pairs={{0,16},{1,113},{2,18},{3,115},{4,20},{5,117},{6,22},{7,119},{8,24}... | collective-permute-start | bytes 6291464 | tf_op jit(solution)/shard_map/ppermute | solution.py:26
  26.9 9.6 %collective-permute-start.8 = (bf16[1024,256]{1,0:T(8,128)(2,1)S(1)}, bf16[1024,256]{1,0:T(8,128)(2,1)S(1)}, u32[]{:S(2)}, u32[]{:S(2)}) collective-permute-start(bf16[1024,256]{1,0:T(8,128)(2,1)S(1)} %get-tuple-element.25), channel_id=1, source_target_pairs={{0,4},{1,3},{2,6},{3,129},{4,8},{5,7},{6,10},{7,133},{8,12},{9,11}... | collective-permute-start | bytes 1572872 | tf_op jit(solution)/shard_map/ppermute | solution.py:26
  28.0 32.7 %copy-start.1 = (bf16[1,64,128,128]{3,2,1,0:T(8,128)(2,1)S(1)}, bf16[1,64,128,128]{3,2,1,0:T(8,128)(2,1)}, u32[]{:S(2)}) copy-start(bf16[1,64,128,128]{3,2,1,0:T(8,128)(2,1)} %param.5) | copy-start | bytes 6291460
  28.0 8.5 %collective-permute-start.7 = (bf16[1024,256]{1,0:T(8,128)(2,1)S(1)}, bf16[1024,256]{1,0:T(8,128)(2,1)S(1)}, u32[]{:S(2)}, u32[]{:S(2)}) collective-permute-start(bf16[1024,256]{1,0:T(8,128)(2,1)S(1)} %get-tuple-element.26), channel_id=1, source_target_pairs={{0,12},{1,131},{2,14},{3,1},{4,0},{5,135},{6,2},{7,5},{8,4},{9,139... | collective-permute-start | bytes 1572872 | tf_op jit(solution)/shard_map/ppermute | solution.py:26
  29.7 12.3 %collective-permute-start.9 = (bf16[1024,256]{1,0:T(8,128)(2,1)S(1)}, bf16[1024,256]{1,0:T(8,128)(2,1)S(1)}, u32[]{:S(2)}, u32[]{:S(2)}) collective-permute-start(bf16[1024,256]{1,0:T(8,128)(2,1)S(1)} %get-tuple-element.25), channel_id=1, source_target_pairs={{0,12},{1,131},{2,14},{3,1},{4,0},{5,135},{6,2},{7,5},{8,4},{9,139... | collective-permute-start | bytes 1572872 | tf_op jit(solution)/shard_map/ppermute | solution.py:26
  30.9 15.4 %collective-permute-start.10 = (bf16[1024,256]{1,0:T(8,128)(2,1)S(1)}, bf16[1024,256]{1,0:T(8,128)(2,1)S(1)}, u32[]{:S(2)}, u32[]{:S(2)}) collective-permute-start(bf16[1024,256]{1,0:T(8,128)(2,1)S(1)} %get-tuple-element.26), channel_id=1, source_target_pairs={{0,4},{1,3},{2,6},{3,129},{4,8},{5,7},{6,10},{7,133},{8,12},{9,11}... | collective-permute-start | bytes 1572872 | tf_op jit(solution)/shard_map/ppermute | solution.py:26
  36.6 11.0 %collective-permute-start.12 = (bf16[1024,256]{1,0:T(8,128)(2,1)S(1)}, bf16[1024,256]{1,0:T(8,128)(2,1)S(1)}, u32[]{:S(2)}, u32[]{:S(2)}) collective-permute-start(bf16[1024,256]{1,0:T(8,128)(2,1)S(1)} %collective-permute-done.7.rest_1_), channel_id=1, source_target_pairs={{0,12},{1,131},{2,14},{3,1},{4,0},{5,135},{6,2},{7,5},{8,4},{9,139... | collective-permute-start | bytes 1572872 | tf_op jit(solution)/shard_map/ppermute | solution.py:26
  39.2 12.7 %collective-permute-start.13 = (bf16[1024,256]{1,0:T(8,128)(2,1)S(1)}, bf16[1024,256]{1,0:T(8,128)(2,1)S(1)}, u32[]{:S(2)}, u32[]{:S(2)}) collective-permute-start(bf16[1024,256]{1,0:T(8,128)(2,1)S(1)} %collective-permute-done.8.rest_6_), channel_id=1, source_target_pairs={{0,4},{1,3},{2,6},{3,129},{4,8},{5,7},{6,10},{7,133},{8,12},{9,11}... | collective-permute-start | bytes 1572872 | tf_op jit(solution)/shard_map/ppermute | solution.py:26
  42.0 12.1 %collective-permute-start.15 = (bf16[1024,256]{1,0:T(8,128)(2,1)S(1)}, bf16[1024,256]{1,0:T(8,128)(2,1)S(1)}, u32[]{:S(2)}, u32[]{:S(2)}) collective-permute-start(bf16[1024,256]{1,0:T(8,128)(2,1)S(1)} %collective-permute-done.7.rest_1_), channel_id=1, source_target_pairs={{0,1},{1,0},{2,3},{3,2},{4,5},{5,4},{6,7},{7,6},{8,9},{9,8},{10,11... | collective-permute-start | bytes 1572872 | tf_op jit(solution)/shard_map/ppermute | solution.py:26
  46.3 8.3 %collective-permute-start.14 = (bf16[2048,256]{1,0:T(8,128)(2,1)S(1)}, bf16[2048,256]{1,0:T(8,128)(2,1)S(1)}, u32[]{:S(2)}, u32[]{:S(2)}) collective-permute-start(bf16[2048,256]{1,0:T(8,128)(2,1)S(1)} %pad_maximum_fusion.rest_0_), channel_id=1, source_target_pairs={{0,1},{1,0},{2,3},{3,2},{4,5},{5,4},{6,7},{7,6},{8,9},{9,8},{10,11... | collective-permute-start | bytes 3145736 | tf_op jit(solution)/shard_map/ppermute | solution.py:26
  47.6 7.0 %collective-permute-start.20 = (bf16[1024,256]{1,0:T(8,128)(2,1)S(1)}, bf16[1024,256]{1,0:T(8,128)(2,1)S(1)}, u32[]{:S(2)}, u32[]{:S(2)}) collective-permute-start(bf16[1024,256]{1,0:T(8,128)(2,1)S(1)} %collective-permute-done.8.rest_6_), channel_id=1, source_target_pairs={{0,1},{1,0},{2,3},{3,2},{4,5},{5,4},{6,7},{7,6},{8,9},{9,8},{10,11... | collective-permute-start | bytes 1572872 | tf_op jit(solution)/shard_map/ppermute | solution.py:26
  51.9 3.6 %collective-permute-start.17 = (bf16[1024,256]{1,0:T(8,128)(2,1)S(1)}, bf16[1024,256]{1,0:T(8,128)(2,1)S(1)}, u32[]{:S(2)}, u32[]{:S(2)}) collective-permute-start(bf16[1024,256]{1,0:T(8,128)(2,1)S(1)} %collective-permute-done.12.rest_3_), channel_id=1, source_target_pairs={{0,1},{1,0},{2,3},{3,2},{4,5},{5,4},{6,7},{7,6},{8,9},{9,8},{10,11... | collective-permute-start | bytes 1572872 | tf_op jit(solution)/shard_map/ppermute | solution.py:26
  54.1 2.3 %collective-permute-start.18 = (bf16[1024,256]{1,0:T(8,128)(2,1)S(1)}, bf16[1024,256]{1,0:T(8,128)(2,1)S(1)}, u32[]{:S(2)}, u32[]{:S(2)}) collective-permute-start(bf16[1024,256]{1,0:T(8,128)(2,1)S(1)} %collective-permute-done.13.rest_4_), channel_id=1, source_target_pairs={{0,1},{1,0},{2,3},{3,2},{4,5},{5,4},{6,7},{7,6},{8,9},{9,8},{10,11... | collective-permute-start | bytes 1572872 | tf_op jit(solution)/shard_map/ppermute | solution.py:26
  54.1 3.0 %collective-permute-start.16 = (bf16[1024,256]{1,0:T(8,128)(2,1)S(1)}, bf16[1024,256]{1,0:T(8,128)(2,1)S(1)}, u32[]{:S(2)}, u32[]{:S(2)}) collective-permute-start(bf16[1024,256]{1,0:T(8,128)(2,1)S(1)} %collective-permute-done.9.rest_2_), channel_id=1, source_target_pairs={{0,1},{1,0},{2,3},{3,2},{4,5},{5,4},{6,7},{7,6},{8,9},{9,8},{10,11... | collective-permute-start | bytes 1572872 | tf_op jit(solution)/shard_map/ppermute | solution.py:26
  54.6 3.3 %collective-permute-start.19 = (bf16[1024,256]{1,0:T(8,128)(2,1)S(1)}, bf16[1024,256]{1,0:T(8,128)(2,1)S(1)}, u32[]{:S(2)}, u32[]{:S(2)}) collective-permute-start(bf16[1024,256]{1,0:T(8,128)(2,1)S(1)} %collective-permute-done.10.rest_5_), channel_id=1, source_target_pairs={{0,1},{1,0},{2,3},{3,2},{4,5},{5,4},{6,7},{7,6},{8,9},{9,8},{10,11... | collective-permute-start | bytes 1572872 | tf_op jit(solution)/shard_map/ppermute | solution.py:26
  59.8 5.1 %collective-permute-start.21 = (f32[128,256]{1,0:T(8,128)S(1)}, f32[128,256]{1,0:T(8,128)S(1)}, u32[]{:S(2)}, u32[]{:S(2)}) collective-permute-start(f32[128,256]{1,0:T(8,128)S(1)} %shard_map.48), channel_id=1, source_target_pairs={{0,112},{1,17},{2,114},{3,19},{4,116},{5,21},{6,118},{7,23},{8,120... | collective-permute-start | bytes 393224 | tf_op jit(solution)/shard_map/ppermute | solution.py:26
